TPU v7x, 512 devices: a whole 4x8x8 slice. The times are simulated.
512 devices in a mesh: gx: 8 (over z), gy: 8 (over y_lo, x), gz: 8 (over y_hi, core).
Axes of the slice: x: 4, y: 8 (y_hi: 4, y_lo: 2; y = y_hi * 2 + y_lo), z: 8, core: 2. Of those that a mesh axis runs over, the one named last changes fastest.
Arguments:
- populations: float32 [19, 64, 64, 1024], P(None, 'gz', 'gx', 'gy'), may hold values from 0.6 to 1.4
- solid_codes: int32 [64, 64, 1024], P('gz', 'gx', 'gy'), may hold values from 0 to 8
- plane_offsets: int32 [2, 8], replicated, may hold values from 0 to 63
- plane_fractions: int32 [2, 8], replicated, may hold values from 0 to 63
Outputs:
- populations_next: float32 [19, 64, 64, 1024], P(None, 'gz', 'gx', 'gy')
All inputs are finite; a program needn't handle non-finite values.
Results may differ from a plain program's by a relative error of at most 0.0001.
Values sent between devices are 32-bit elements; how exact they have to be, the bound alone decides.
No kernel may reach another device: no remote copies, remote signals or barrier semaphores. Data moves between devices by JAX's collectives and lax.ppermute only.
A program may use at most 64 MiB of HBM per device.

v0:
```python
import jax
import jax.numpy as jnp
from jax import lax
from jax.sharding import PartitionSpec as P

LEVELS = 8
FRAC_DEN = 64


velocities = (
    (0, 0, 0),
    (1, 0, 0),
    (-1, 0, 0),
    (0, 1, 0),
    (0, -1, 0),
    (0, 0, 1),
    (0, 0, -1),
    (1, 1, 0),
    (-1, -1, 0),
    (1, -1, 0),
    (-1, 1, 0),
    (1, 0, 1),
    (-1, 0, -1),
    (1, 0, -1),
    (-1, 0, 1),
    (0, 1, 1),
    (0, -1, -1),
    (0, 1, -1),
    (0, -1, 1),
)
lattice_weights = (1.0 / 3.0,) + (1.0 / 18.0,) * 6 + (1.0 / 36.0,) * 12
opposite_index = (0, 2, 1, 4, 3, 6, 5, 8, 7, 10, 9, 12, 11, 14, 13, 16, 15, 18, 17)
relax_time = 0.9
rising = (5, 11, 14, 15, 18)
sinking = (6, 12, 13, 16, 17)


def from_behind(array, axis, by):
    peers = lax.axis_size(axis)
    return lax.ppermute(array, axis, [(i, (i + by) % peers) for i in range(peers)])


def extended_2(array, sides, width):
    for axis, dim in sides:
        peers, length = (lax.axis_size(axis), array.shape[dim])
        up = [(i, (i + 1) % peers) for i in range(peers)]
        down = [(j, i) for i, j in up]
        last = lax.slice_in_dim(array, length - width, length, axis=dim)
        initial = lax.slice_in_dim(array, 0, width, axis=dim)
        before = lax.ppermute(last, axis, up)
        after = lax.ppermute(initial, axis, down)
        array = jnp.concatenate([before, array, after], axis=dim)
    return array


def velocity_sum(distribution, component):
    total = jnp.zeros_like(distribution[0])
    for popul_index in range(19):
        moving = velocities[popul_index][component]
        if moving == 1:
            total = total + distribution[popul_index]
        elif moving == -1:
            total = total - distribution[popul_index]
    return total


def collide(distribution, solid_codes):
    solid = solid_codes.astype(jnp.float32) / LEVELS
    density = jnp.sum(distribution, axis=0)
    speed_x = velocity_sum(distribution, 0) / density
    speed_y = velocity_sum(distribution, 1) / density
    speed_z = velocity_sum(distribution, 2) / density
    square = speed_x * speed_x + speed_y * speed_y + speed_z * speed_z
    outgoing = []
    for popul_index in range(19):
        move_x, move_y, move_z = velocities[popul_index]
        along = move_x * speed_x + move_y * speed_y + move_z * speed_z
        balance = (
            lattice_weights[popul_index]
            * density
            * (1.0 + 3.0 * along + 4.5 * along * along - 1.5 * square)
        )
        relaxed = distribution[popul_index] - (distribution[popul_index] - balance) / relax_time
        outgoing.append((1.0 - solid) * relaxed + solid * distribution[opposite_index[popul_index]])
    return jnp.stack(outgoing)


def select_member(stacked, members, popul_index, zero_fill):
    if popul_index in members:
        return stacked[members.index(popul_index)]
    return zero_fill


def realign(strips, shifts, coef_near, coef_far):
    rows_dev = strips.shape[2]
    cycle_size = lax.axis_size("gx")
    whole_blocks = shifts // rows_dev
    within = shifts % rows_dev
    current = strips
    for bit_level in range(max(1, (cycle_size - 1).bit_length())):
        moved = from_behind(current, "gx", 2**bit_level)
        taken = whole_blocks >> bit_level & 1 == 1
        current = jnp.where(taken[:, None, None, None], moved, current)
    previous = from_behind(current, "gx", 1)
    window = jnp.concatenate([previous, current], axis=2)
    results = []
    for strip_index in range(2):
        nearer = lax.dynamic_slice_in_dim(
            window[strip_index], rows_dev - within[strip_index], rows_dev, 1
        )
        farther = lax.dynamic_slice_in_dim(
            window[strip_index], rows_dev - within[strip_index] - 1, rows_dev, 1
        )
        results.append(coef_near[strip_index] * nearer + coef_far[strip_index] * farther)
    return jnp.stack(results)


def surround(collided, moved):
    layers_dev, rows_dev, cols_dev = (collided.shape[1], collided.shape[2], collided.shape[3])
    zero_fill = jnp.zeros((rows_dev, cols_dev), jnp.float32)
    bottom_layer = jnp.stack(
        [select_member(moved[0], sinking, popul_index, zero_fill) for popul_index in range(19)]
    )
    top_layer = jnp.stack(
        [select_member(moved[1], rising, popul_index, zero_fill) for popul_index in range(19)]
    )
    padded = jnp.concatenate([bottom_layer[:, None], collided, top_layer[:, None]], axis=1)
    haloed = extended_2(padded, (("gx", 2), ("gy", 3), ("gz", 1)), 1)
    return jnp.concatenate(
        [haloed[:, 0:1], haloed[:, 2 : layers_dev + 2], haloed[:, layers_dev + 3 : layers_dev + 4]],
        axis=1,
    )


def advance(distribution, solid_codes, offsets, fractions):
    collided = collide(distribution, solid_codes)
    layers_dev, rows_dev, cols_dev = (collided.shape[1], collided.shape[2], collided.shape[3])
    cycle_rows = rows_dev * lax.axis_size("gx")
    plane_here = lax.axis_index("gz")
    plane_next = jnp.mod(plane_here + 1, lax.axis_size("gz"))
    fraction = fractions.astype(jnp.float32) / FRAC_DEN
    strips = jnp.stack(
        [
            jnp.stack([collided[popul_index, 0] for popul_index in sinking]),
            jnp.stack([collided[popul_index, layers_dev - 1] for popul_index in rising]),
        ]
    )
    shifts = jnp.stack([cycle_rows - 1 - offsets[plane_here], offsets[plane_next]])
    coef_near = jnp.stack([fraction[plane_here], 1.0 - fraction[plane_next]])
    coef_far = jnp.stack([1.0 - fraction[plane_here], fraction[plane_next]])
    moved = realign(strips, shifts, coef_near, coef_far)
    extended = surround(collided, moved)
    arrived = []
    for popul_index in range(19):
        move_x, move_y, move_z = velocities[popul_index]
        arrived.append(
            extended[
                popul_index,
                1 - move_z : 1 - move_z + layers_dev,
                1 - move_x : 1 - move_x + rows_dev,
                1 - move_y : 1 - move_y + cols_dev,
            ]
        )
    return jnp.stack(arrived)


def body(populations, solid_codes, plane_offsets, plane_fractions):
    weights = jnp.asarray(lattice_weights, jnp.float32)[:, None, None, None]
    distribution = populations * weights
    for step_index in range(plane_offsets.shape[0]):
        distribution = advance(
            distribution, solid_codes, plane_offsets[step_index], plane_fractions[step_index]
        )
    return distribution / weights


def solution(mesh):
    in_specs = (P(None, "gz", "gx", "gy"), P("gz", "gx", "gy"), P(), P())
    out_specs = P(None, "gz", "gx", "gy")
    return jax.shard_map(body, mesh=mesh, in_specs=in_specs, out_specs=out_specs, check_vma=False)
```

profile of v0, /device:TPU:31, one launch (start us, length us, event | category | flops | bytes accessed | tf_op | source)
XLA Modules:
  0.0 182.9 jit_solution(17851937693631599600)
XLA Ops:
  0.0 1.2 broadcast_multiply_fusion.1
  3.0 4.0 %collective-permute-start = (f32[2,5,8,128]{3,2,1,0:T(8,128)S(1)}, f32[2,5,8,128]{3,2,1,0:T(8,128)S(1)}, u32[]{:S(2)}, u32[]{:S(2)}) collective-permute-start(f32[2,5,8,128]{3,2,1,0:T(8,128)S(1)} %pad_maximum_fusion.14), channel_id=1, source_target_pairs={{0,64},{64,128},{128,192},{192,256},{256,320},{320,384},{384,448},... | collective-permute-start | bytes 122888 | tf_op jit(solution)/shard_map/ppermute | solution.py:40
  10.5 4.6 %collective-permute-done = f32[2,5,8,128]{3,2,1,0:T(8,128)S(1)} collective-permute-done((f32[2,5,8,128]{3,2,1,0:T(8,128)S(1)}, f32[2,5,8,128]{3,2,1,0:T(8,128)S(1)}, u32[]{:S(2)}, u32[]{:S(2)}) %collective-permute-start) | collective-permute-done | bytes 40992 | tf_op jit(solution)/shard_map/ppermute | solution.py:40
  15.1 1.9 %collective-permute-start.1 = (f32[2,5,8,128]{3,2,1,0:T(8,128)S(1)}, f32[2,5,8,128]{3,2,1,0:T(8,128)S(1)}, u32[]{:S(2)}, u32[]{:S(2)}) collective-permute-start(f32[2,5,8,128]{3,2,1,0:T(8,128)S(1)} %broadcast_select_fusion.3), channel_id=1, source_target_pairs={{0,128},{64,192},{128,256},{192,320},{256,384},{320,448},{384,0},{... | collective-permute-start | bytes 122888 | tf_op jit(solution)/shard_map/ppermute | solution.py:40
  17.0 5.0 %collective-permute-done.1 = f32[2,5,8,128]{3,2,1,0:T(8,128)S(1)} collective-permute-done((f32[2,5,8,128]{3,2,1,0:T(8,128)S(1)}, f32[2,5,8,128]{3,2,1,0:T(8,128)S(1)}, u32[]{:S(2)}, u32[]{:S(2)}) %collective-permute-start.1) | collective-permute-done | bytes 40992 | tf_op jit(solution)/shard_map/ppermute | solution.py:40
  22.1 5.5 %collective-permute-start.2 = (f32[2,5,8,128]{3,2,1,0:T(8,128)S(1)}, f32[2,5,8,128]{3,2,1,0:T(8,128)S(1)}, u32[]{:S(2)}, u32[]{:S(2)}) collective-permute-start(f32[2,5,8,128]{3,2,1,0:T(8,128)S(1)} %broadcast_select_fusion.4), channel_id=1, source_target_pairs={{0,256},{64,320},{128,384},{192,448},{256,0},{320,64},{384,128},{4... | collective-permute-start | bytes 122888 | tf_op jit(solution)/shard_map/ppermute | solution.py:40
  27.7 3.1 %collective-permute-done.2 = f32[2,5,8,128]{3,2,1,0:T(8,128)S(1)} collective-permute-done((f32[2,5,8,128]{3,2,1,0:T(8,128)S(1)}, f32[2,5,8,128]{3,2,1,0:T(8,128)S(1)}, u32[]{:S(2)}, u32[]{:S(2)}) %collective-permute-start.2) | collective-permute-done | bytes 40992 | tf_op jit(solution)/shard_map/ppermute | solution.py:40
  30.9 1.9 %collective-permute-start.3 = (f32[2,5,8,128]{3,2,1,0:T(8,128)S(1)}, f32[2,5,8,128]{3,2,1,0:T(8,128)S(1)}, u32[]{:S(2)}, u32[]{:S(2)}) collective-permute-start(f32[2,5,8,128]{3,2,1,0:T(8,128)S(1)} %broadcast_select_fusion.5), channel_id=1, source_target_pairs={{0,64},{64,128},{128,192},{192,256},{256,320},{320,384},{384,448},... | collective-permute-start | bytes 122888 | tf_op jit(solution)/shard_map/ppermute | solution.py:40
  42.0 2.0 %collective-permute-start.4 = (f32[19,10,1,128]{3,2,1,0:T(1,128)S(1)}, f32[19,10,1,128]{3,2,1,0:T(1,128)S(1)}, u32[]{:S(2)}, u32[]{:S(2)}) collective-permute-start(f32[19,10,1,128]{3,2,1,0:T(1,128)S(1)} %get-tuple-element.91), channel_id=1, source_target_pairs={{0,64},{64,128},{128,192},{192,256},{256,320},{320,384},{384,448},... | collective-permute-start | bytes 291848 | tf_op jit(solution)/shard_map/ppermute | solution.py:50
  43.9 4.5 %collective-permute-start.5 = (f32[19,10,1,128]{3,2,1,0:T(1,128)S(1)}, f32[19,10,1,128]{3,2,1,0:T(1,128)S(1)}, u32[]{:S(2)}, u32[]{:S(2)}) collective-permute-start(f32[19,10,1,128]{3,2,1,0:T(1,128)S(1)} %get-tuple-element.90), channel_id=1, source_target_pairs={{64,0},{128,64},{192,128},{256,192},{320,256},{384,320},{448,384},... | collective-permute-start | bytes 291848 | tf_op jit(solution)/shard_map/ppermute | solution.py:51
  48.5 1.6 collective-permute-done.5
  51.0 1.7 fusion.388
  52.8 2.1 %copy.37 = f32[19,10,10,1]{0,3,2,1:T(1,128)S(1)} copy(f32[19,10,10,1]{3,2,1,0:T(8,128)} %get-tuple-element.87) | data formatting | bytes 15200 | tf_op jit(solution)/shard_map/slice | solution.py:48
  54.9 2.0 %collective-permute-start.6 = (f32[19,10,10,1]{0,3,2,1:T(1,128)S(1)}, f32[19,10,10,1]{0,3,2,1:T(1,128)S(1)}, u32[]{:S(2)}, u32[]{:S(2)}) collective-permute-start(f32[19,10,10,1]{0,3,2,1:T(1,128)S(1)} %copy.37), channel_id=1, source_target_pairs={{0,8},{8,16},{16,24},{24,32},{32,40},{40,48},{48,56},{56,0},{1,9},... | collective-permute-start | bytes 22808 | tf_op jit(solution)/shard_map/ppermute | solution.py:50
  57.7 3.3 %collective-permute-start.7 = (f32[19,10,10,1]{0,3,2,1:T(1,128)S(1)}, f32[19,10,10,1]{0,3,2,1:T(1,128)}, u32[]{:S(2)}, u32[]{:S(2)}) collective-permute-start(f32[19,10,10,1]{0,3,2,1:T(1,128)S(1)} %copy.39), channel_id=1, source_target_pairs={{8,0},{16,8},{24,16},{32,24},{40,32},{48,40},{56,48},{0,56},{9,1},... | collective-permute-start | bytes 22808 | tf_op jit(solution)/shard_map/ppermute | solution.py:51
  61.0 1.6 copy.38
  62.6 2.2 %collective-permute-done.7 = f32[19,10,10,1]{0,3,2,1:T(1,128)} collective-permute-done((f32[19,10,10,1]{0,3,2,1:T(1,128)S(1)}, f32[19,10,10,1]{0,3,2,1:T(1,128)}, u32[]{:S(2)}, u32[]{:S(2)}) %collective-permute-start.7) | collective-permute-done | bytes 7632 | tf_op jit(solution)/shard_map/ppermute | solution.py:51
  64.7 2.4 %copy.40 = f32[19,10,10,1]{3,2,1,0:T(8,128)S(1)} copy(f32[19,10,10,1]{0,3,2,1:T(1,128)} %collective-permute-done.7) | data formatting | bytes 15200 | tf_op jit(solution)/shard_map/ppermute | solution.py:51
  67.1 1.3 pad_maximum_fusion.6
  68.4 12.0 %collective-permute-start.8 = (f32[19,1,10,130]{3,2,1,0:T(8,128)S(1)}, f32[19,1,10,130]{3,2,1,0:T(8,128)S(1)}, u32[]{:S(2)}, u32[]{:S(2)}) collective-permute-start(f32[19,1,10,130]{3,2,1,0:T(8,128)S(1)} %get-tuple-element.83), channel_id=1, source_target_pairs={{0,1},{1,2},{2,3},{3,4},{4,5},{5,6},{6,7},{7,0},{8,9},{9,10},{10,1... | collective-permute-start | bytes 296408 | tf_op jit(solution)/shard_map/ppermute | solution.py:50
  80.4 1.9 %collective-permute-start.9 = (f32[19,1,10,130]{3,2,1,0:T(8,128)S(1)}, f32[19,1,10,130]{3,2,1,0:T(8,128)S(1)}, u32[]{:S(2)}, u32[]{:S(2)}) collective-permute-start(f32[19,1,10,130]{3,2,1,0:T(8,128)S(1)} %get-tuple-element.82), channel_id=1, source_target_pairs={{1,0},{2,1},{3,2},{4,3},{5,4},{6,5},{7,6},{0,7},{9,8},{10,9},{11,1... | collective-permute-start | bytes 296408 | tf_op jit(solution)/shard_map/ppermute | solution.py:51
  82.4 2.1 %pad_maximum_fusion = f32[19,10,10,130]{3,2,1,0:T(8,128)S(1)} fusion(f32[19,10,10,1]{3,2,1,0:T(8,128)S(1)} %copy.40, f32[19,10,1,128]{3,2,1,0:T(1,128)S(1)} %copy-done.5, f32[19,1,8,128]{3,2,1,0:T(8,128)S(1)} %bitcast.611, f32[19,8,8,128]{3,2,1,0:T(8,128)S(1)} %copy-done.3, f32[19,1,8,128]{3,2,1,0:T(8,128)S(1)} %bitcast.606, ...), kind=kLoop, calls=%fused_computation | loop fusion | flops 1482000 | bytes 1976000 | tf_op jit(solution)/shard_map/concatenate | solution.py:52
  84.7 2.8 %collective-permute-done.8 = f32[19,1,10,130]{3,2,1,0:T(8,128)S(1)} collective-permute-done((f32[19,1,10,130]{3,2,1,0:T(8,128)S(1)}, f32[19,1,10,130]{3,2,1,0:T(8,128)S(1)}, u32[]{:S(2)}, u32[]{:S(2)}) %collective-permute-start.8) | collective-permute-done | bytes 98832 | tf_op jit(solution)/shard_map/ppermute | solution.py:50
  87.6 5.7 %collective-permute-done.9 = f32[19,1,10,130]{3,2,1,0:T(8,128)S(1)} collective-permute-done((f32[19,1,10,130]{3,2,1,0:T(8,128)S(1)}, f32[19,1,10,130]{3,2,1,0:T(8,128)S(1)}, u32[]{:S(2)}, u32[]{:S(2)}) %collective-permute-start.9) | collective-permute-done | bytes 98832 | tf_op jit(solution)/shard_map/ppermute | solution.py:51
  94.7 3.4 %collective-permute-start.10 = (f32[2,5,8,128]{3,2,1,0:T(8,128)S(1)}, f32[2,5,8,128]{3,2,1,0:T(8,128)S(1)}, u32[]{:S(2)}, u32[]{:S(2)}) collective-permute-start(f32[2,5,8,128]{3,2,1,0:T(8,128)S(1)} %pad_maximum_fusion.15), channel_id=1, source_target_pairs={{0,64},{64,128},{128,192},{192,256},{256,320},{320,384},{384,448},... | collective-permute-start | bytes 122888 | tf_op jit(solution)/shard_map/ppermute | solution.py:40
  98.1 3.2 %collective-permute-done.10 = f32[2,5,8,128]{3,2,1,0:T(8,128)S(1)} collective-permute-done((f32[2,5,8,128]{3,2,1,0:T(8,128)S(1)}, f32[2,5,8,128]{3,2,1,0:T(8,128)S(1)}, u32[]{:S(2)}, u32[]{:S(2)}) %collective-permute-start.10) | collective-permute-done | bytes 40992 | tf_op jit(solution)/shard_map/ppermute | solution.py:40
  101.4 3.6 %collective-permute-start.11 = (f32[2,5,8,128]{3,2,1,0:T(8,128)S(1)}, f32[2,5,8,128]{3,2,1,0:T(8,128)S(1)}, u32[]{:S(2)}, u32[]{:S(2)}) collective-permute-start(f32[2,5,8,128]{3,2,1,0:T(8,128)S(1)} %broadcast_select_fusion), channel_id=1, source_target_pairs={{0,128},{64,192},{128,256},{192,320},{256,384},{320,448},{384,0},{... | collective-permute-start | bytes 122888 | tf_op jit(solution)/shard_map/ppermute | solution.py:40
  105.0 3.6 %collective-permute-done.11 = f32[2,5,8,128]{3,2,1,0:T(8,128)S(1)} collective-permute-done((f32[2,5,8,128]{3,2,1,0:T(8,128)S(1)}, f32[2,5,8,128]{3,2,1,0:T(8,128)S(1)}, u32[]{:S(2)}, u32[]{:S(2)}) %collective-permute-start.11) | collective-permute-done | bytes 40992 | tf_op jit(solution)/shard_map/ppermute | solution.py:40
  108.7 6.1 %collective-permute-start.12 = (f32[2,5,8,128]{3,2,1,0:T(8,128)S(1)}, f32[2,5,8,128]{3,2,1,0:T(8,128)S(1)}, u32[]{:S(2)}, u32[]{:S(2)}) collective-permute-start(f32[2,5,8,128]{3,2,1,0:T(8,128)S(1)} %broadcast_select_fusion.1), channel_id=1, source_target_pairs={{0,256},{64,320},{128,384},{192,448},{256,0},{320,64},{384,128},{4... | collective-permute-start | bytes 122888 | tf_op jit(solution)/shard_map/ppermute | solution.py:40
  114.8 3.0 %collective-permute-done.12 = f32[2,5,8,128]{3,2,1,0:T(8,128)S(1)} collective-permute-done((f32[2,5,8,128]{3,2,1,0:T(8,128)S(1)}, f32[2,5,8,128]{3,2,1,0:T(8,128)S(1)}, u32[]{:S(2)}, u32[]{:S(2)}) %collective-permute-start.12) | collective-permute-done | bytes 40992 | tf_op jit(solution)/shard_map/ppermute | solution.py:40
  117.8 1.9 %collective-permute-start.13 = (f32[2,5,8,128]{3,2,1,0:T(8,128)S(1)}, f32[2,5,8,128]{3,2,1,0:T(8,128)S(1)}, u32[]{:S(2)}, u32[]{:S(2)}) collective-permute-start(f32[2,5,8,128]{3,2,1,0:T(8,128)S(1)} %broadcast_select_fusion.2), channel_id=1, source_target_pairs={{0,64},{64,128},{128,192},{192,256},{256,320},{320,384},{384,448},... | collective-permute-start | bytes 122888 | tf_op jit(solution)/shard_map/ppermute | solution.py:40
  128.6 2.4 %collective-permute-start.14 = (f32[19,10,1,128]{3,0,2,1:T(8,128)S(1)}, f32[19,10,1,128]{3,0,2,1:T(8,128)S(1)}, u32[]{:S(2)}, u32[]{:S(2)}) collective-permute-start(f32[19,10,1,128]{3,0,2,1:T(8,128)S(1)} %copy.45), channel_id=1, source_target_pairs={{0,64},{64,128},{128,192},{192,256},{256,320},{320,384},{384,448},... | collective-permute-start | bytes 291848 | tf_op jit(solution)/shard_map/ppermute | solution.py:50
  131.0 4.3 %collective-permute-start.15 = (f32[19,10,1,128]{3,0,2,1:T(8,128)S(1)}, f32[19,10,1,128]{3,0,2,1:T(8,128)S(1)}, u32[]{:S(2)}, u32[]{:S(2)}) collective-permute-start(f32[19,10,1,128]{3,0,2,1:T(8,128)S(1)} %copy.47), channel_id=1, source_target_pairs={{64,0},{128,64},{192,128},{256,192},{320,256},{384,320},{448,384},... | collective-permute-start | bytes 291848 | tf_op jit(solution)/shard_map/ppermute | solution.py:51
  135.6 1.4 collective-permute-done.15
  137.4 1.7 fusion.387
  139.1 2.5 %copy.51 = f32[19,10,10,1]{0,2,3,1:T(8,128)S(1)} copy(f32[19,10,10,1]{3,2,1,0:T(8,128)} %get-tuple-element.85) | data formatting | bytes 15200 | tf_op jit(solution)/shard_map/slice | solution.py:48
  141.6 2.4 %collective-permute-start.16 = (f32[19,10,10,1]{0,2,3,1:T(8,128)S(1)}, f32[19,10,10,1]{0,2,3,1:T(8,128)S(1)}, u32[]{:S(2)}, u32[]{:S(2)}) collective-permute-start(f32[19,10,10,1]{0,2,3,1:T(8,128)S(1)} %copy.51), channel_id=1, source_target_pairs={{0,8},{8,16},{16,24},{24,32},{32,40},{40,48},{48,56},{56,0},{1,9},... | collective-permute-start | bytes 22808 | tf_op jit(solution)/shard_map/ppermute | solution.py:50
  144.0 1.2 copy.53
  145.2 2.9 %collective-permute-start.17 = (f32[19,10,10,1]{0,2,3,1:T(8,128)S(1)}, f32[19,10,10,1]{0,2,3,1:T(8,128)S(1)}, u32[]{:S(2)}, u32[]{:S(2)}) collective-permute-start(f32[19,10,10,1]{0,2,3,1:T(8,128)S(1)} %copy.53), channel_id=1, source_target_pairs={{8,0},{16,8},{24,16},{32,24},{40,32},{48,40},{56,48},{0,56},{9,1},... | collective-permute-start | bytes 22808 | tf_op jit(solution)/shard_map/ppermute | solution.py:51
  148.1 1.5 copy.52
  149.6 3.4 %collective-permute-done.17 = f32[19,10,10,1]{0,2,3,1:T(8,128)S(1)} collective-permute-done((f32[19,10,10,1]{0,2,3,1:T(8,128)S(1)}, f32[19,10,10,1]{0,2,3,1:T(8,128)S(1)}, u32[]{:S(2)}, u32[]{:S(2)}) %collective-permute-start.17) | collective-permute-done | bytes 7632 | tf_op jit(solution)/shard_map/ppermute | solution.py:51
  153.0 2.7 %copy.54 = f32[19,10,10,1]{3,2,1,0:T(8,128)} copy(f32[19,10,10,1]{0,2,3,1:T(8,128)S(1)} %collective-permute-done.17) | data formatting | bytes 15200 | tf_op jit(solution)/shard_map/ppermute | solution.py:51
  155.7 3.6 %pad_maximum_fusion.1 = f32[19,10,10,130]{3,2,1,0:T(8,128)S(1)} fusion(f32[19,10,10,1]{3,2,1,0:T(8,128)} %copy.54, f32[19,10,1,128]{3,2,1,0:T(1,128)S(1)} %copy.48, f32[19,1,8,128]{3,2,1,0:T(8,128)S(1)} %bitcast.595, f32[19,8,8,128]{3,2,1,0:T(8,128)S(1)} %get-tuple-element.5, f32[19,1,8,128]{3,2,1,0:T(8,128)S(1)} %bitcast.583, ...), kind=kLoop, calls=%fused_computation.1 | loop fusion | flops 1482000 | bytes 1976000 | tf_op jit(solution)/shard_map/concatenate | solution.py:52
  160.2 6.7 %collective-permute-start.18 = (f32[19,1,10,130]{3,2,1,0:T(8,128)S(1)}, f32[19,1,10,130]{3,2,1,0:T(8,128)S(1)}, u32[]{:S(2)}, u32[]{:S(2)}) collective-permute-start(f32[19,1,10,130]{3,2,1,0:T(8,128)S(1)} %get-tuple-element.81), channel_id=1, source_target_pairs={{0,1},{1,2},{2,3},{3,4},{4,5},{5,6},{6,7},{7,0},{8,9},{9,10},{10,1... | collective-permute-start | bytes 296408 | tf_op jit(solution)/shard_map/ppermute | solution.py:50
  166.9 1.9 %collective-permute-start.19 = (f32[19,1,10,130]{3,2,1,0:T(8,128)S(1)}, f32[19,1,10,130]{3,2,1,0:T(8,128)S(1)}, u32[]{:S(2)}, u32[]{:S(2)}) collective-permute-start(f32[19,1,10,130]{3,2,1,0:T(8,128)S(1)} %get-tuple-element.80), channel_id=1, source_target_pairs={{1,0},{2,1},{3,2},{4,3},{5,4},{6,5},{7,6},{0,7},{9,8},{10,9},{11,1... | collective-permute-start | bytes 296408 | tf_op jit(solution)/shard_map/ppermute | solution.py:51
  168.9 5.0 %collective-permute-done.18 = f32[19,1,10,130]{3,2,1,0:T(8,128)S(1)} collective-permute-done((f32[19,1,10,130]{3,2,1,0:T(8,128)S(1)}, f32[19,1,10,130]{3,2,1,0:T(8,128)S(1)}, u32[]{:S(2)}, u32[]{:S(2)}) %collective-permute-start.18) | collective-permute-done | bytes 98832 | tf_op jit(solution)/shard_map/ppermute | solution.py:50
  174.0 6.4 %collective-permute-done.19 = f32[19,1,10,130]{3,2,1,0:T(8,128)S(1)} collective-permute-done((f32[19,1,10,130]{3,2,1,0:T(8,128)S(1)}, f32[19,1,10,130]{3,2,1,0:T(8,128)S(1)}, u32[]{:S(2)}, u32[]{:S(2)}) %collective-permute-start.19) | collective-permute-done | bytes 98832 | tf_op jit(solution)/shard_map/ppermute | solution.py:51
  181.9 0.9 broadcast_multiply_fusion
  (178 shorter events, 15.4 us)
Async XLA Ops:
  0.0 2.1 %copy-start.1 = (s32[8,8,128]{2,1,0:T(8,128)S(1)}, s32[8,8,128]{2,1,0:T(8,128)}, u32[]{:S(2)}) copy-start(s32[8,8,128]{2,1,0:T(8,128)} %param.6) | copy-start | bytes 98308
  2.4 4.5 %copy-start.6 = (s32[2,8]{1,0:T(2,128)S(1)}, s32[2,8]{1,0:T(2,128)}, u32[]{:S(2)}) copy-start(s32[2,8]{1,0:T(2,128)} %param.7) | copy-start | bytes 196
  2.5 6.6 %copy-start.7 = (s32[2,8]{1,0:T(2,128)S(1)}, s32[2,8]{1,0:T(2,128)}, u32[]{:S(2)}) copy-start(s32[2,8]{1,0:T(2,128)} %param.8) | copy-start | bytes 196
  2.8 48.2 %copy-start.2 = (f32[19,8,8,128]{3,2,1,0:T(8,128)}, f32[19,8,8,128]{3,2,1,0:T(8,128)S(1)}, u32[]{:S(2)}) copy-start(f32[19,8,8,128]{3,2,1,0:T(8,128)S(1)} %get-tuple-element.51) | copy-start | bytes 1867780
  3.0 12.1 %collective-permute-start = (f32[2,5,8,128]{3,2,1,0:T(8,128)S(1)}, f32[2,5,8,128]{3,2,1,0:T(8,128)S(1)}, u32[]{:S(2)}, u32[]{:S(2)}) collective-permute-start(f32[2,5,8,128]{3,2,1,0:T(8,128)S(1)} %pad_maximum_fusion.14), channel_id=1, source_target_pairs={{0,64},{64,128},{128,192},{192,256},{256,320},{320,384},{384,448},... | collective-permute-start | bytes 122888 | tf_op jit(solution)/shard_map/ppermute | solution.py:40
  15.1 6.9 %collective-permute-start.1 = (f32[2,5,8,128]{3,2,1,0:T(8,128)S(1)}, f32[2,5,8,128]{3,2,1,0:T(8,128)S(1)}, u32[]{:S(2)}, u32[]{:S(2)}) collective-permute-start(f32[2,5,8,128]{3,2,1,0:T(8,128)S(1)} %broadcast_select_fusion.3), channel_id=1, source_target_pairs={{0,128},{64,192},{128,256},{192,320},{256,384},{320,448},{384,0},{... | collective-permute-start | bytes 122888 | tf_op jit(solution)/shard_map/ppermute | solution.py:40
  22.1 8.7 %collective-permute-start.2 = (f32[2,5,8,128]{3,2,1,0:T(8,128)S(1)}, f32[2,5,8,128]{3,2,1,0:T(8,128)S(1)}, u32[]{:S(2)}, u32[]{:S(2)}) collective-permute-start(f32[2,5,8,128]{3,2,1,0:T(8,128)S(1)} %broadcast_select_fusion.4), channel_id=1, source_target_pairs={{0,256},{64,320},{128,384},{192,448},{256,0},{320,64},{384,128},{4... | collective-permute-start | bytes 122888 | tf_op jit(solution)/shard_map/ppermute | solution.py:40
  30.9 9.5 %collective-permute-start.3 = (f32[2,5,8,128]{3,2,1,0:T(8,128)S(1)}, f32[2,5,8,128]{3,2,1,0:T(8,128)S(1)}, u32[]{:S(2)}, u32[]{:S(2)}) collective-permute-start(f32[2,5,8,128]{3,2,1,0:T(8,128)S(1)} %broadcast_select_fusion.5), channel_id=1, source_target_pairs={{0,64},{64,128},{128,192},{192,256},{256,320},{320,384},{384,448},... | collective-permute-start | bytes 122888 | tf_op jit(solution)/shard_map/ppermute | solution.py:40
  42.0 6.6 %collective-permute-start.4 = (f32[19,10,1,128]{3,2,1,0:T(1,128)S(1)}, f32[19,10,1,128]{3,2,1,0:T(1,128)S(1)}, u32[]{:S(2)}, u32[]{:S(2)}) collective-permute-start(f32[19,10,1,128]{3,2,1,0:T(1,128)S(1)} %get-tuple-element.91), channel_id=1, source_target_pairs={{0,64},{64,128},{128,192},{192,256},{256,320},{320,384},{384,448},... | collective-permute-start | bytes 291848 | tf_op jit(solution)/shard_map/ppermute | solution.py:50
  43.9 6.2 %collective-permute-start.5 = (f32[19,10,1,128]{3,2,1,0:T(1,128)S(1)}, f32[19,10,1,128]{3,2,1,0:T(1,128)S(1)}, u32[]{:S(2)}, u32[]{:S(2)}) collective-permute-start(f32[19,10,1,128]{3,2,1,0:T(1,128)S(1)} %get-tuple-element.90), channel_id=1, source_target_pairs={{64,0},{128,64},{192,128},{256,192},{320,256},{384,320},{448,384},... | collective-permute-start | bytes 291848 | tf_op jit(solution)/shard_map/ppermute | solution.py:51
  50.1 0.6 copy-start.4
  54.9 6.1 %collective-permute-start.6 = (f32[19,10,10,1]{0,3,2,1:T(1,128)S(1)}, f32[19,10,10,1]{0,3,2,1:T(1,128)S(1)}, u32[]{:S(2)}, u32[]{:S(2)}) collective-permute-start(f32[19,10,10,1]{0,3,2,1:T(1,128)S(1)} %copy.37), channel_id=1, source_target_pairs={{0,8},{8,16},{16,24},{24,32},{32,40},{40,48},{48,56},{56,0},{1,9},... | collective-permute-start | bytes 22808 | tf_op jit(solution)/shard_map/ppermute | solution.py:50
  57.7 7.1 %collective-permute-start.7 = (f32[19,10,10,1]{0,3,2,1:T(1,128)S(1)}, f32[19,10,10,1]{0,3,2,1:T(1,128)}, u32[]{:S(2)}, u32[]{:S(2)}) collective-permute-start(f32[19,10,10,1]{0,3,2,1:T(1,128)S(1)} %copy.39), channel_id=1, source_target_pairs={{8,0},{16,8},{24,16},{32,24},{40,32},{48,40},{56,48},{0,56},{9,1},... | collective-permute-start | bytes 22808 | tf_op jit(solution)/shard_map/ppermute | solution.py:51
  67.1 15.3 %copy-start.3 = (f32[19,8,8,128]{3,2,1,0:T(8,128)S(1)}, f32[19,8,8,128]{3,2,1,0:T(8,128)}, u32[]{:S(2)}) copy-start(f32[19,8,8,128]{3,2,1,0:T(8,128)} %copy-done.2) | copy-start | bytes 1867780
  67.1 15.3 %copy-start.5 = (f32[19,10,1,128]{3,2,1,0:T(1,128)S(1)}, f32[19,10,1,128]{3,2,1,0:T(1,128)}, u32[]{:S(2)}) copy-start(f32[19,10,1,128]{3,2,1,0:T(1,128)} %copy-done.4) | copy-start | bytes 291844
  68.4 19.2 %collective-permute-start.8 = (f32[19,1,10,130]{3,2,1,0:T(8,128)S(1)}, f32[19,1,10,130]{3,2,1,0:T(8,128)S(1)}, u32[]{:S(2)}, u32[]{:S(2)}) collective-permute-start(f32[19,1,10,130]{3,2,1,0:T(8,128)S(1)} %get-tuple-element.83), channel_id=1, source_target_pairs={{0,1},{1,2},{2,3},{3,4},{4,5},{5,6},{6,7},{7,0},{8,9},{9,10},{10,1... | collective-permute-start | bytes 296408 | tf_op jit(solution)/shard_map/ppermute | solution.py:50
  80.4 12.9 %collective-permute-start.9 = (f32[19,1,10,130]{3,2,1,0:T(8,128)S(1)}, f32[19,1,10,130]{3,2,1,0:T(8,128)S(1)}, u32[]{:S(2)}, u32[]{:S(2)}) collective-permute-start(f32[19,1,10,130]{3,2,1,0:T(8,128)S(1)} %get-tuple-element.82), channel_id=1, source_target_pairs={{1,0},{2,1},{3,2},{4,3},{5,4},{6,5},{7,6},{0,7},{9,8},{10,9},{11,1... | collective-permute-start | bytes 296408 | tf_op jit(solution)/shard_map/ppermute | solution.py:51
  94.7 6.6 %collective-permute-start.10 = (f32[2,5,8,128]{3,2,1,0:T(8,128)S(1)}, f32[2,5,8,128]{3,2,1,0:T(8,128)S(1)}, u32[]{:S(2)}, u32[]{:S(2)}) collective-permute-start(f32[2,5,8,128]{3,2,1,0:T(8,128)S(1)} %pad_maximum_fusion.15), channel_id=1, source_target_pairs={{0,64},{64,128},{128,192},{192,256},{256,320},{320,384},{384,448},... | collective-permute-start | bytes 122888 | tf_op jit(solution)/shard_map/ppermute | solution.py:40
  101.4 7.2 %collective-permute-start.11 = (f32[2,5,8,128]{3,2,1,0:T(8,128)S(1)}, f32[2,5,8,128]{3,2,1,0:T(8,128)S(1)}, u32[]{:S(2)}, u32[]{:S(2)}) collective-permute-start(f32[2,5,8,128]{3,2,1,0:T(8,128)S(1)} %broadcast_select_fusion), channel_id=1, source_target_pairs={{0,128},{64,192},{128,256},{192,320},{256,384},{320,448},{384,0},{... | collective-permute-start | bytes 122888 | tf_op jit(solution)/shard_map/ppermute | solution.py:40
  108.7 9.1 %collective-permute-start.12 = (f32[2,5,8,128]{3,2,1,0:T(8,128)S(1)}, f32[2,5,8,128]{3,2,1,0:T(8,128)S(1)}, u32[]{:S(2)}, u32[]{:S(2)}) collective-permute-start(f32[2,5,8,128]{3,2,1,0:T(8,128)S(1)} %broadcast_select_fusion.1), channel_id=1, source_target_pairs={{0,256},{64,320},{128,384},{192,448},{256,0},{320,64},{384,128},{4... | collective-permute-start | bytes 122888 | tf_op jit(solution)/shard_map/ppermute | solution.py:40
  117.8 9.0 %collective-permute-start.13 = (f32[2,5,8,128]{3,2,1,0:T(8,128)S(1)}, f32[2,5,8,128]{3,2,1,0:T(8,128)S(1)}, u32[]{:S(2)}, u32[]{:S(2)}) collective-permute-start(f32[2,5,8,128]{3,2,1,0:T(8,128)S(1)} %broadcast_select_fusion.2), channel_id=1, source_target_pairs={{0,64},{64,128},{128,192},{192,256},{256,320},{320,384},{384,448},... | collective-permute-start | bytes 122888 | tf_op jit(solution)/shard_map/ppermute | solution.py:40
  128.6 6.8 %collective-permute-start.14 = (f32[19,10,1,128]{3,0,2,1:T(8,128)S(1)}, f32[19,10,1,128]{3,0,2,1:T(8,128)S(1)}, u32[]{:S(2)}, u32[]{:S(2)}) collective-permute-start(f32[19,10,1,128]{3,0,2,1:T(8,128)S(1)} %copy.45), channel_id=1, source_target_pairs={{0,64},{64,128},{128,192},{192,256},{256,320},{320,384},{384,448},... | collective-permute-start | bytes 291848 | tf_op jit(solution)/shard_map/ppermute | solution.py:50
  131.0 6.0 %collective-permute-start.15 = (f32[19,10,1,128]{3,0,2,1:T(8,128)S(1)}, f32[19,10,1,128]{3,0,2,1:T(8,128)S(1)}, u32[]{:S(2)}, u32[]{:S(2)}) collective-permute-start(f32[19,10,1,128]{3,0,2,1:T(8,128)S(1)} %copy.47), channel_id=1, source_target_pairs={{64,0},{128,64},{192,128},{256,192},{320,256},{384,320},{448,384},... | collective-permute-start | bytes 291848 | tf_op jit(solution)/shard_map/ppermute | solution.py:51
  141.6 6.5 %collective-permute-start.16 = (f32[19,10,10,1]{0,2,3,1:T(8,128)S(1)}, f32[19,10,10,1]{0,2,3,1:T(8,128)S(1)}, u32[]{:S(2)}, u32[]{:S(2)}) collective-permute-start(f32[19,10,10,1]{0,2,3,1:T(8,128)S(1)} %copy.51), channel_id=1, source_target_pairs={{0,8},{8,16},{16,24},{24,32},{32,40},{40,48},{48,56},{56,0},{1,9},... | collective-permute-start | bytes 22808 | tf_op jit(solution)/shard_map/ppermute | solution.py:50
  145.2 7.8 %collective-permute-start.17 = (f32[19,10,10,1]{0,2,3,1:T(8,128)S(1)}, f32[19,10,10,1]{0,2,3,1:T(8,128)S(1)}, u32[]{:S(2)}, u32[]{:S(2)}) collective-permute-start(f32[19,10,10,1]{0,2,3,1:T(8,128)S(1)} %copy.53), channel_id=1, source_target_pairs={{8,0},{16,8},{24,16},{32,24},{40,32},{48,40},{56,48},{0,56},{9,1},... | collective-permute-start | bytes 22808 | tf_op jit(solution)/shard_map/ppermute | solution.py:51
  155.7 3.6 %copy-start = (f32[19,10,10,1]{3,2,1,0:T(8,128)S(1)}, f32[19,10,10,1]{3,2,1,0:T(8,128)}, u32[]{:S(2)}) copy-start(f32[19,10,10,1]{3,2,1,0:T(8,128)} %copy.54) | copy-start | bytes 22804
  160.2 13.7 %collective-permute-start.18 = (f32[19,1,10,130]{3,2,1,0:T(8,128)S(1)}, f32[19,1,10,130]{3,2,1,0:T(8,128)S(1)}, u32[]{:S(2)}, u32[]{:S(2)}) collective-permute-start(f32[19,1,10,130]{3,2,1,0:T(8,128)S(1)} %get-tuple-element.81), channel_id=1, source_target_pairs={{0,1},{1,2},{2,3},{3,4},{4,5},{5,6},{6,7},{7,0},{8,9},{9,10},{10,1... | collective-permute-start | bytes 296408 | tf_op jit(solution)/shard_map/ppermute | solution.py:50
  166.9 13.5 %collective-permute-start.19 = (f32[19,1,10,130]{3,2,1,0:T(8,128)S(1)}, f32[19,1,10,130]{3,2,1,0:T(8,128)S(1)}, u32[]{:S(2)}, u32[]{:S(2)}) collective-permute-start(f32[19,1,10,130]{3,2,1,0:T(8,128)S(1)} %get-tuple-element.80), channel_id=1, source_target_pairs={{1,0},{2,1},{3,2},{4,3},{5,4},{6,5},{7,6},{0,7},{9,8},{10,9},{11,1... | collective-permute-start | bytes 296408 | tf_op jit(solution)/shard_map/ppermute | solution.py:51
  181.3 0.7 copy-start.8
where the time goes:
time: 184 us; the launch traced here: 183 us
  starting transfers between devices  74.7 us (41%)
  waiting for transfers between devices  51.1 us (28%)
  local copies, waits for them, and re-layouts  22.9 us (12%)
  other arithmetic  18.9 us (10%)
  between operations  15.3 us (8%)
    ppermute x8, starting transfers between devices, from_behind(): lax.ppermute(array, axis, [(i, (i + by) % peers) for i in range(peers)])  28.4 us
    ppermute x6, starting transfers between devices, extended_2(): before = lax.ppermute(last, axis, up)  27.4 us
    ppermute x8, waiting for transfers between devices, from_behind(): lax.ppermute(array, axis, [(i, (i + by) % peers) for i in range(peers)])  22.4 us
    ppermute x6, waiting for transfers between devices, extended_2(): after = lax.ppermute(initial, axis, down)  20.6 us
    ppermute x6, starting transfers between devices, extended_2(): after = lax.ppermute(initial, axis, down)  18.9 us
    ppermute x6, waiting for transfers between devices, extended_2(): before = lax.ppermute(last, axis, up)  8.03 us
    concatenate x4, other arithmetic, extended_2(): array = jnp.concatenate([before, array, after], axis=dim)  6.36 us
    slice x5, local copies, waits for them, and re-layouts, extended_2(): initial = lax.slice_in_dim(array, 0, width, axis=dim)  5.43 us
  transfers between devices with their start and end apart: 20, of which 15 were waited for; matrix products, arithmetic and copies ran while one was open for 6% of the time, Pallas kernels for 0%

commit v1 on v0

v1 whole, which is shorter than its diff:
```python
import jax
import jax.numpy as jnp
from jax import lax
from jax.experimental import pallas as pl
from jax.experimental.pallas import tpu as pltpu
from jax.sharding import PartitionSpec as P

LEVELS = 8
FRAC_DEN = 64
velocities = (
    (0, 0, 0), (1, 0, 0), (-1, 0, 0), (0, 1, 0), (0, -1, 0), (0, 0, 1), (0, 0, -1),
    (1, 1, 0), (-1, -1, 0), (1, -1, 0), (-1, 1, 0), (1, 0, 1), (-1, 0, -1), (1, 0, -1),
    (-1, 0, 1), (0, 1, 1), (0, -1, -1), (0, 1, -1), (0, -1, 1),
)
weight_inverse = (3.0,) + (18.0,) * 6 + (36.0,) * 12
lattice_weights = tuple(1.0 / v for v in weight_inverse)
relax_time = 0.9
pairs = ((1, 2), (3, 4), (5, 6), (7, 8), (9, 10), (11, 12), (13, 14), (15, 16), (17, 18))
rising = (5, 11, 14, 15, 18)
sinking = (6, 13, 12, 17, 16)
level = (0, 1, 2, 3, 4, 7, 8, 9, 10)
forward = (1, 7, 9, 11, 13)
backward = (2, 8, 10, 12, 14)
F32 = jnp.float32


def roll(value, by, axis):
    if isinstance(by, int):
        by %= value.shape[axis]
        if by == 0:
            return value
    return pltpu.roll(value, by, axis)


def lanes(shape=(8, 128)):
    return lax.broadcasted_iota(jnp.int32, shape, 1)


def rows(shape=(8, 128)):
    return lax.broadcasted_iota(jnp.int32, shape, 0)


def collide(f, solid):
    density = f[0]
    for i, j in pairs:
        density = density + (f[i] + f[j])
    inverse = 1.0 / density
    speed = []
    for axis in range(3):
        total = None
        for i, j in pairs:
            moving = velocities[i][axis]
            if moving == 0:
                continue
            part = f[i] - f[j] if moving == 1 else f[j] - f[i]
            total = part if total is None else total + part
        speed.append(total * inverse)
    square = speed[0] * speed[0] + speed[1] * speed[1] + speed[2] * speed[2]
    fluid = 1.0 - solid
    keep = fluid * (1.0 - 1.0 / relax_time)
    pull = fluid * density * (1.0 / relax_time)
    calm = pull - 1.5 * square * pull
    post = [None] * 19
    post[0] = keep * f[0] + lattice_weights[0] * calm + solid * f[0]
    for i, j in pairs:
        along = None
        for axis in range(3):
            moving = velocities[i][axis]
            if moving == 0:
                continue
            if along is None:
                along = speed[axis] if moving == 1 else -speed[axis]
            else:
                along = along + speed[axis] if moving == 1 else along - speed[axis]
        weight = lattice_weights[i]
        flow = (3.0 * weight) * (pull * along)
        even = weight * calm + (1.5 * flow) * along
        post[i] = keep * f[i] + solid * f[j] + (even + flow)
        post[j] = keep * f[j] + solid * f[i] + (even - flow)
    return post


def edge_kernel(pops, codes, out):
    lane = lanes()
    for tile in range(5):
        packed = jnp.zeros((8, 128), F32)
        for slot in range(4):
            item = tile * 4 + slot
            for z in range(8):
                start = slot * 32 + z * 4
                source = pops[item, z] if item < 19 else codes[z].astype(F32)
                moved = roll(source, start + 2, 1)
                packed = jnp.where(lane < start, packed, moved)
        out[tile] = packed


def first_kernel(pops, codes, left, right, p1, side, chunks, ahead, behind):
    lane = lanes()
    outer = []
    for tile in range(5):
        both = jnp.where(lane % 4 < 2, left[tile], right[tile])
        for slot in range(4):
            outer.append(roll(both, -32 * slot, 1))
    beside = collide([outer[i] * lattice_weights[i] for i in range(19)], outer[19] * (1.0 / LEVELS))
    shifted = []
    for i in range(19):
        shifted.append(roll(beside[i], velocities[i][1], 1))
    for z in range(8):
        f = [pops[i, z] * lattice_weights[i] for i in range(19)]
        post = collide(f, codes[z].astype(F32) * (1.0 / LEVELS))
        for i in range(19):
            step = velocities[i][1]
            value = post[i]
            if step == 1:
                shifted[i] = jnp.where(lane == 4 * z + 2, roll(value, 4 * z + 3, 1), shifted[i])
                value = jnp.where(lane == 0, roll(beside[i], -(4 * z + 1), 1), roll(value, 1, 1))
            elif step == -1:
                shifted[i] = jnp.where(lane == 4 * z + 1, roll(value, 4 * z + 1, 1), shifted[i])
                value = jnp.where(lane == 127, roll(beside[i], 127 - (4 * z + 2), 1), roll(value, -1, 1))
            p1[i, z] = value
            if i in forward:
                ahead[forward.index(i), z : z + 1, :] = value[7:8, :]
            if i in backward:
                behind[backward.index(i), z : z + 1, :] = value[0:1, :]
    for i in range(19):
        side[i] = shifted[i]
    side[19] = outer[19]
    for slot in range(5):
        ahead[5, slot : slot + 1, :] = shifted[forward[slot]][7:8, :]
        behind[5, slot : slot + 1, :] = shifted[backward[slot]][0:1, :]
    for slot in range(5, 8):
        ahead[5, slot : slot + 1, :] = jnp.zeros((1, 128), F32)
        behind[5, slot : slot + 1, :] = jnp.zeros((1, 128), F32)
    upper = [(i, 7) for i in rising] + [(i, 7) for i in level] + [(i, 6) for i in rising] + [(19, 7)]
    lower = [(i, 0) for i in sinking] + [(i, 0) for i in level] + [(i, 1) for i in sinking] + [(19, 0)]
    for group, items in enumerate((upper, lower)):
        for tile in range(3):
            held = [jnp.zeros((8, 128), F32)] * 8
            for slot, (i, z) in enumerate(items[tile * 7 : tile * 7 + 7]):
                main = p1[i, z] if i < 19 else codes[z].astype(F32)
                extra = shifted[i] if i < 19 else outer[19]
                first = jnp.where(lane == 127, roll(extra, 127 - (4 * z + 1), 1), main)
                last = jnp.where(lane == 0, roll(extra, -(4 * z + 2), 1), main)
                for d in range(8):
                    source = first if d == 0 else last if d == 7 else main
                    moved = roll(source, 18 * slot - 16 * d + 1, 1)
                    held[d] = jnp.where(lane < 18 * slot, held[d], moved)
            for d in range(8):
                chunks[d, group * 3 + tile] = held[d]


def cross(outgoing, lane, shift_a, shift_b, frac_a, frac_b):
    length = outgoing.shape[0]
    low = (lane // 32) % 2 == 1
    up_a, down_a = roll(outgoing, shift_a, 0), roll(outgoing, (length - shift_a) % length, 0)
    up_b, down_b = roll(outgoing, shift_b, 0), roll(outgoing, (length - shift_b) % length, 0)
    near = jnp.where(lane < 64, jnp.where(low, down_a, up_a), jnp.where(low, down_b, up_b))
    far = jnp.where(low, roll(near, -1, 0), roll(near, 1, 0))
    share = jnp.where(lane < 64, frac_a, frac_b)
    mixed = (1.0 - share) * near + share * far
    return jnp.where(low, roll(mixed, 32, 1), roll(mixed, -32, 1))


def plane_kernel(offsets, fractions, own, below, above, out, work, state):
    length = work.shape[1]
    lane8 = lanes()
    lane = lanes((length, 128))
    here = lax.axis_index("gz")
    after = (here + 1) % lax.axis_size("gz")

    def params(step):
        return (
            offsets[step, here],
            offsets[step, after],
            fractions[step, here].astype(F32) * (1.0 / FRAC_DEN),
            fractions[step, after].astype(F32) * (1.0 / FRAC_DEN),
        )

    for item in range(20):
        tile, slot = divmod(item, 7)
        for b in range(8):
            sets = (below[b, tile], own[b, 3 + tile], own[b, tile], above[b, tile])
            moved = [roll(s, 32 * q - 18 * slot, 1) for q, s in enumerate(sets)]
            value = jnp.where(
                lane8 < 64,
                jnp.where(lane8 < 32, moved[0], moved[1]),
                jnp.where(lane8 < 96, moved[2], moved[3]),
            )
            work[item, 8 * b : 8 * b + 8, :] = value
    for j in range(5):
        step_x = velocities[rising[j]][0]
        state[sinking[j]] = roll(cross(work[j], lane, *params(0)), step_x, 0)
        state[rising[j]] = roll(work[14 + j], step_x, 0)
    for k, i in enumerate(level):
        state[i] = roll(work[5 + k], velocities[i][0], 0)
    for b in range(8):
        at = slice(8 * b, 8 * b + 8)
        post = collide([state[i, at, :] for i in range(19)], work[19, at, :] * (1.0 / LEVELS))
        for i in range(19):
            state[i, at, :] = roll(post[i], velocities[i][1], 1)
    final = []
    for i in level:
        final.append((i, None))
    for j in range(5):
        final.append((sinking[j], None))
    for j in range(5):
        final.append((rising[j], j))
    for n, (i, crossing) in enumerate(final):
        value = state[i]
        if crossing is not None:
            value = cross(value, lane, *params(1))
        work[n] = roll(value, velocities[i][0], 0)
    for b in range(8):
        for tile in range(5):
            packed = jnp.zeros((8, 128), F32)
            for slot in range(8):
                n = tile * 8 + slot
                if n >= 38:
                    break
                group, q = (n, 2) if n < 19 else (n - 19, 1)
                moved = roll(work[group, 8 * b : 8 * b + 8, :], 16 * slot - 32 * q - 1, 1)
                packed = jnp.where(lane8 < 16 * slot, packed, moved)
            out[b, tile] = packed


def streamed_x(source, z, i, from_behind, from_ahead, row):
    value = source[i, z]
    if i in forward:
        j = forward.index(i)
        return jnp.where(row == 0, jnp.broadcast_to(from_behind[j, z + 0 : z + 1, :], (8, 128)), roll(value, 1, 0))
    if i in backward:
        j = backward.index(i)
        return jnp.where(row == 7, jnp.broadcast_to(from_ahead[j, z + 0 : z + 1, :], (8, 128)), roll(value, -1, 0))
    return value


def inner_kernel(p1, side, codes, from_behind, from_ahead, p2, ahead, behind):
    lane, row = lanes(), rows()
    f = []
    for i in range(19):
        value = side[i]
        if i in forward:
            j = forward.index(i)
            value = jnp.where(row == 0, jnp.broadcast_to(from_behind[5, j : j + 1, :], (8, 128)), roll(value, 1, 0))
        elif i in backward:
            j = backward.index(i)
            value = jnp.where(row == 7, jnp.broadcast_to(from_ahead[5, j : j + 1, :], (8, 128)), roll(value, -1, 0))
        f.append(roll(value, 4 * velocities[i][2], 1))
    beside = collide(f, side[19] * (1.0 / LEVELS))
    for j in range(5):
        for z in (0, 7):
            ahead[j, z : z + 1, :] = jnp.zeros((1, 128), F32)
            behind[j, z : z + 1, :] = jnp.zeros((1, 128), F32)
    for z in range(1, 7):
        f = [streamed_x(p1, z - velocities[i][2], i, from_behind, from_ahead, row) for i in range(19)]
        post = collide(f, codes[z].astype(F32) * (1.0 / LEVELS))
        for i in range(19):
            step = velocities[i][1]
            value = post[i]
            if step == 1:
                value = jnp.where(lane == 0, roll(beside[i], -(4 * z + 1), 1), roll(value, 1, 1))
            elif step == -1:
                value = jnp.where(lane == 127, roll(beside[i], 127 - (4 * z + 2), 1), roll(value, -1, 1))
            p2[i, z] = value
            if i in forward:
                ahead[forward.index(i), z : z + 1, :] = value[7:8, :]
            if i in backward:
                behind[backward.index(i), z : z + 1, :] = value[0:1, :]
    for i in range(19):
        for z in (0, 7):
            p2[i, z] = jnp.zeros((8, 128), F32)


def last_kernel(p2, from_behind, from_ahead, planes, out):
    lane, row = lanes(), rows()
    for i in range(19):
        for z in range(8):
            source = z - velocities[i][2]
            if 1 <= source <= 6:
                out[i, z] = streamed_x(p2, source, i, from_behind, from_ahead, row) * weight_inverse[i]
    target = []
    for group in range(2):
        z, inner = (7, 6) if group == 0 else (0, 1)
        inward, outward = (sinking, rising) if group == 0 else (rising, sinking)
        target += [(i, z) for i in level] + [(i, inner) for i in inward] + [(i, z) for i in inward]
    part = lane // 16
    for tile in range(5):
        held = [planes[h, tile] for h in range(8)]
        for k in (1, 2, 4):
            fixed = part & k == 0
            for h in range(8):
                if h & k == 0:
                    lo, hi = held[h], held[h | k]
                    held[h] = jnp.where(fixed, lo, roll(hi, 16 * k, 1))
                    held[h | k] = jnp.where(fixed, roll(lo, -16 * k, 1), hi)
        for slot in range(8):
            n = tile * 8 + slot
            if n < 38:
                i, z = target[n]
                out[i, z] = held[slot] * weight_inverse[i]


def run(kernel, outs, args, scalars=0, scratch=()):
    specs = [pl.BlockSpec(memory_space=pltpu.SMEM)] * scalars
    specs += [pl.BlockSpec(memory_space=pltpu.VMEM)] * (len(args) - scalars)
    shapes = [jax.ShapeDtypeStruct(s, F32) for s in outs]
    return pl.pallas_call(
        kernel,
        out_shape=shapes,
        in_specs=specs,
        out_specs=[pl.BlockSpec(memory_space=pltpu.VMEM)] * len(outs),
        scratch_shapes=[pltpu.VMEM(s, F32) for s in scratch],
        compiler_params=pltpu.CompilerParams(vmem_limit_bytes=32 * 1024 * 1024),
    )(*args)


def neighbours(value_up, value_down, axis):
    peers = lax.axis_size(axis)
    up = [(i, (i + 1) % peers) for i in range(peers)]
    down = [(j, i) for i, j in up]
    return lax.ppermute(value_up, axis, up), lax.ppermute(value_down, axis, down)


def body(pops, codes, offsets, fractions):
    tile = (8, 128)
    (edges,) = run(edge_kernel, [(5,) + tile], (pops, codes))
    left, right = neighbours(edges, edges, "gy")
    p1, side, chunks, ahead, behind = run(
        first_kernel,
        [(19, 8) + tile, (20,) + tile, (8, 6) + tile, (6,) + tile, (6,) + tile],
        (pops, codes, left, right),
    )
    own = lax.all_to_all(chunks, "gx", 0, 0)
    from_behind, from_ahead = neighbours(ahead, behind, "gx")
    below, above = neighbours(own[:, 0:3], own[:, 3:6], "gz")
    p2, ahead, behind = run(
        inner_kernel,
        [(19, 8) + tile, (5,) + tile, (5,) + tile],
        (p1, side, codes, from_behind, from_ahead),
    )
    (planes,) = run(
        plane_kernel,
        [(8, 5) + tile],
        (offsets, fractions, own, below, above),
        scalars=2,
        scratch=[(20, 64, 128), (19, 64, 128)],
    )
    planes = lax.all_to_all(planes, "gx", 0, 0)
    from_behind, from_ahead = neighbours(ahead, behind, "gx")
    (out,) = run(last_kernel, [(19, 8) + tile], (p2, from_behind, from_ahead, planes))
    return out


def solution(mesh):
    in_specs = (P(None, "gz", "gx", "gy"), P("gz", "gx", "gy"), P(), P())
    out_specs = P(None, "gz", "gx", "gy")
    return jax.shard_map(body, mesh=mesh, in_specs=in_specs, out_specs=out_specs, check_vma=False)
```

time: 184 us -> 77.6 us (0.42)
  the two profiles are of different devices: /device:TPU:31 before, /device:TPU:72 now
where the time goes in v1:
time: 77.6 us; the launch traced here: 77 us
  starting transfers between devices  28 us (36%)
  waiting for transfers between devices  21.2 us (27%)
  blocking collectives  18 us (23%)
  Pallas kernels  7.8 us (10%)
  local copies, waits for them, and re-layouts  1.86 us (2%)
    all_to_all x1, blocking collectives, body(): own = lax.all_to_all(chunks, 'gx', 0, 0)  18 us
    ppermute x4, waiting for transfers between devices, neighbours(): lax.ppermute(value_up, axis, up)  12.8 us
    ppermute x4, starting transfers between devices, neighbours(): lax.ppermute(value_down, axis, down)  11.7 us
    ppermute x4, starting transfers between devices, neighbours(): lax.ppermute(value_up, axis, up)  11.3 us
    ppermute x4, waiting for transfers between devices, neighbours(): lax.ppermute(value_down, axis, down)  8.45 us
    pallas_call x5, Pallas kernels, run(): pl.pallas_call(kernel, out_shape=shapes, in_specs=specs, out_specs=[pl.Bl...  7.8 us
    all_to_all x1, starting transfers between devices, body(): planes = lax.all_to_all(planes, 'gx', 0, 0)  5.04 us
    unnamed x10, local copies, waits for them, and re-layouts  1.85 us
  transfers between devices with their start and end apart: 9, of which 5 were waited for; matrix products, arithmetic and copies ran while one was open for 0% of the time, Pallas kernels for 0%

profile of v1, /device:TPU:72, one launch (start us, length us, event | category | flops | bytes accessed | tf_op | source)
XLA Modules:
  0.0 77.0 jit_solution(3812423942392999000)
XLA Ops:
  0.0 0.0 copy-start
  0.0 1.1 %copy-done = f32[19,8,8,128]{3,2,1,0:T(8,128)S(1)} copy-done((f32[19,8,8,128]{3,2,1,0:T(8,128)S(1)}, f32[19,8,8,128]{3,2,1,0:T(8,128)}, u32[]{:S(2)}) %copy-start) | copy-done | bytes 622616
  1.1 0.0 copy-start.1
  1.1 0.8 copy-done.1
  1.8 0.2 shard_map.46
  2.1 4.6 %collective-permute-start.1 = (f32[5,8,128]{2,1,0:T(8,128)S(1)}, f32[5,8,128]{2,1,0:T(8,128)S(1)}, u32[]{:S(2)}, u32[]{:S(2)}) collective-permute-start(f32[5,8,128]{2,1,0:T(8,128)S(1)} %shard_map.46), channel_id=1, source_target_pairs={{8,0},{16,8},{24,16},{32,24},{40,32},{48,40},{56,48},{0,56},{9,1},... | collective-permute-start | bytes 61448 | tf_op jit(solution)/shard_map/ppermute | solution.py:321
  6.6 1.9 %collective-permute-start = (f32[5,8,128]{2,1,0:T(8,128)S(1)}, f32[5,8,128]{2,1,0:T(8,128)S(1)}, u32[]{:S(2)}, u32[]{:S(2)}) collective-permute-start(f32[5,8,128]{2,1,0:T(8,128)S(1)} %shard_map.46), channel_id=1, source_target_pairs={{0,8},{8,16},{16,24},{24,32},{32,40},{40,48},{48,56},{56,0},{1,9},... | collective-permute-start | bytes 61448 | tf_op jit(solution)/shard_map/ppermute | solution.py:321
  8.6 0.0 collective-permute-done.1.right
  8.6 5.8 %collective-permute-done.left = f32[5,8,128]{2,1,0:T(8,128)S(1)} collective-permute-done((f32[5,8,128]{2,1,0:T(8,128)S(1)}, f32[5,8,128]{2,1,0:T(8,128)S(1)}, u32[]{:S(2)}, u32[]{:S(2)}) %collective-permute-start) | collective-permute-done | bytes 20512 | tf_op jit(solution)/shard_map/ppermute | solution.py:321
  14.4 3.1 %shard_map.47 = (f32[19,8,8,128]{3,2,1,0:T(8,128)S(1)}, f32[20,8,128]{2,1,0:T(8,128)S(1)}, f32[8,6,8,128]{3,2,1,0:T(8,128)S(1)}, f32[6,8,128]{2,1,0:T(8,128)S(1)}, f32[6,8,128]{2,1,0:T(8,128)S(1)}) custom-call(f32[19,8,8,128]{3,2,1,0:T(8,128)S(1)} %copy-done, s32[8,8,128]{2,1,0:T(8,128)S(1)} %copy-done.1, f32[5,8,128]{2,1,0:T(8,128)S(1)} %collective-permute-done.left, ...), custom_call_target="tpu_custom_call" | custom-call | tf_op jit(solution)/shard_map/pallas_call | solution.py:307
  17.5 18.0 %all_to_all.10.own = f32[8,6,8,128]{3,2,1,0:T(8,128)S(1)} all-to-all(f32[8,6,8,128]{3,2,1,0:T(8,128)S(1)} %get-tuple-element.20), channel_id=1, replica_groups=mesh['gx'=8,'gy'=8,'gz'=8] {'gx'}, dimensions={0} | all-to-all | bytes 393216 | tf_op jit(solution)/shard_map/all_to_all | solution.py:333
  35.6 0.0 copy-start.4
  35.6 0.0 copy-start.3
  35.6 2.7 %collective-permute-start.7 = (f32[8,3,8,128]{3,2,1,0:T(8,128)S(1)}, f32[8,3,8,128]{3,2,1,0:T(8,128)S(1)}, u32[]{:S(2)}, u32[]{:S(2)}) collective-permute-start(f32[8,3,8,128]{3,2,1,0:T(8,128)S(1)} %get-tuple-element.21), channel_id=1, source_target_pairs={{1,0},{2,1},{3,2},{4,3},{5,4},{6,5},{7,6},{0,7},{9,8},{10,9},{11,1... | collective-permute-start | bytes 294920 | tf_op jit(solution)/shard_map/ppermute | solution.py:321
  38.4 1.9 %collective-permute-start.6 = (f32[8,3,8,128]{3,2,1,0:T(8,128)S(1)}, f32[8,3,8,128]{3,2,1,0:T(8,128)S(1)}, u32[]{:S(2)}, u32[]{:S(2)}) collective-permute-start(f32[8,3,8,128]{3,2,1,0:T(8,128)S(1)} %get-tuple-element.22), channel_id=1, source_target_pairs={{0,1},{1,2},{2,3},{3,4},{4,5},{5,6},{6,7},{7,0},{8,9},{9,10},{10,1... | collective-permute-start | bytes 294920 | tf_op jit(solution)/shard_map/ppermute | solution.py:321
  40.3 0.3 collective-permute-done.7.above
  40.5 6.9 %collective-permute-done.6.below = f32[8,3,8,128]{3,2,1,0:T(8,128)S(1)} collective-permute-done((f32[8,3,8,128]{3,2,1,0:T(8,128)S(1)}, f32[8,3,8,128]{3,2,1,0:T(8,128)S(1)}, u32[]{:S(2)}, u32[]{:S(2)}) %collective-permute-start.6) | collective-permute-done | bytes 98336 | tf_op jit(solution)/shard_map/ppermute | solution.py:321
  47.5 0.0 copy-done.4
  47.5 0.0 copy-done.3
  47.5 3.1 %shard_map.49 = f32[8,5,8,128]{3,2,1,0:T(8,128)} custom-call(s32[2,8]{1,0:T(2,128)S(1)} %copy-done.3, s32[2,8]{1,0:T(2,128)S(1)} %copy-done.4, f32[8,6,8,128]{3,2,1,0:T(8,128)S(1)} %all_to_all.10.own, f32[8,3,8,128]{3,2,1,0:T(8,128)S(1)} %collective-permute-done.6.below, f32[8,3,8,128]{3,2,1,0:T(8,128)S(1)} %collective-permute-done.7.above), custom_call_target="tpu_custom_call" | custom-call | tf_op jit(solution)/shard_map/pallas_call | solution.py:307
  50.5 0.0 copy-start.2
  50.5 5.0 %all-to-all-start.1 = ((f32[8,5,8,128]{3,2,1,0:T(8,128)}), f32[8,5,8,128]{3,2,1,0:T(8,128)S(1)}, u32[]{:S(2)}, u32[]{:S(2)}) async-start(f32[8,5,8,128]{3,2,1,0:T(8,128)} %shard_map.49), calls=%async_computation.1 | async-start | bytes 327680 | tf_op jit(solution)/shard_map/all_to_all | solution.py:348
  55.6 3.4 %collective-permute-start.2 = (f32[6,8,128]{2,1,0:T(8,128)S(1)}, f32[6,8,128]{2,1,0:T(8,128)S(1)}, u32[]{:S(2)}, u32[]{:S(2)}) collective-permute-start(f32[6,8,128]{2,1,0:T(8,128)S(1)} %get-tuple-element.15), channel_id=1, source_target_pairs={{0,64},{64,128},{128,192},{192,256},{256,320},{320,384},{384,448},... | collective-permute-start | bytes 73736 | tf_op jit(solution)/shard_map/ppermute | solution.py:321
  58.9 2.5 %collective-permute-start.3 = (f32[6,8,128]{2,1,0:T(8,128)S(1)}, f32[6,8,128]{2,1,0:T(8,128)S(1)}, u32[]{:S(2)}, u32[]{:S(2)}) collective-permute-start(f32[6,8,128]{2,1,0:T(8,128)S(1)} %get-tuple-element.16), channel_id=1, source_target_pairs={{64,0},{128,64},{192,128},{256,192},{320,256},{384,320},{448,384},... | collective-permute-start | bytes 73736 | tf_op jit(solution)/shard_map/ppermute | solution.py:321
  61.4 0.0 collective-permute-done.2.from_behind
  61.4 3.2 %collective-permute-done.3.from_ahead = f32[6,8,128]{2,1,0:T(8,128)S(1)} collective-permute-done((f32[6,8,128]{2,1,0:T(8,128)S(1)}, f32[6,8,128]{2,1,0:T(8,128)S(1)}, u32[]{:S(2)}, u32[]{:S(2)}) %collective-permute-start.3) | collective-permute-done | bytes 24608 | tf_op jit(solution)/shard_map/ppermute | solution.py:321
  64.7 0.0 copy-done.2
  64.7 0.3 shard_map.48
  65.0 4.0 %collective-permute-start.4 = (f32[5,8,128]{2,1,0:T(8,128)S(1)}, f32[5,8,128]{2,1,0:T(8,128)S(1)}, u32[]{:S(2)}, u32[]{:S(2)}) collective-permute-start(f32[5,8,128]{2,1,0:T(8,128)S(1)} %get-tuple-element.18), channel_id=1, source_target_pairs={{0,64},{64,128},{128,192},{192,256},{256,320},{320,384},{384,448},... | collective-permute-start | bytes 61448 | tf_op jit(solution)/shard_map/ppermute | solution.py:321
  69.0 1.9 %collective-permute-start.5 = (f32[5,8,128]{2,1,0:T(8,128)S(1)}, f32[5,8,128]{2,1,0:T(8,128)S(1)}, u32[]{:S(2)}, u32[]{:S(2)}) collective-permute-start(f32[5,8,128]{2,1,0:T(8,128)S(1)} %get-tuple-element.19), channel_id=1, source_target_pairs={{64,0},{128,64},{192,128},{256,192},{320,256},{384,320},{448,384},... | collective-permute-start | bytes 61448 | tf_op jit(solution)/shard_map/ppermute | solution.py:321
  71.0 0.0 collective-permute-done.4.from_behind
  71.0 4.9 %collective-permute-done.5.from_ahead = f32[5,8,128]{2,1,0:T(8,128)S(1)} collective-permute-done((f32[5,8,128]{2,1,0:T(8,128)S(1)}, f32[5,8,128]{2,1,0:T(8,128)S(1)}, u32[]{:S(2)}, u32[]{:S(2)}) %collective-permute-start.5) | collective-permute-done | bytes 20512 | tf_op jit(solution)/shard_map/ppermute | solution.py:321
  75.9 0.0 all-to-all-done.1.planes
  75.9 1.1 %shard_map.50 = f32[19,8,8,128]{3,2,1,0:T(8,128)} custom-call(f32[19,8,8,128]{3,2,1,0:T(8,128)S(1)} %get-tuple-element.17.p2, f32[5,8,128]{2,1,0:T(8,128)S(1)} %collective-permute-done.4.from_behind, f32[5,8,128]{2,1,0:T(8,128)S(1)} %collective-permute-done.5.from_ahead, f32[8,5,8,128]{3,2,1,0:T(8,128)S(1)} %all-to-all-done.1.planes), custom_call_target="tpu_custom_call" | custom-call | tf_op jit(solution)/shard_map/pallas_call | solution.py:307
  (1 shorter events, 0.0 us)
Async XLA Ops:
  0.0 1.1 %copy-start = (f32[19,8,8,128]{3,2,1,0:T(8,128)S(1)}, f32[19,8,8,128]{3,2,1,0:T(8,128)}, u32[]{:S(2)}) copy-start(f32[19,8,8,128]{3,2,1,0:T(8,128)} %pops.3) | copy-start | bytes 1867780
  1.1 0.8 copy-start.1
  2.1 6.5 %collective-permute-start.1 = (f32[5,8,128]{2,1,0:T(8,128)S(1)}, f32[5,8,128]{2,1,0:T(8,128)S(1)}, u32[]{:S(2)}, u32[]{:S(2)}) collective-permute-start(f32[5,8,128]{2,1,0:T(8,128)S(1)} %shard_map.46), channel_id=1, source_target_pairs={{8,0},{16,8},{24,16},{32,24},{40,32},{48,40},{56,48},{0,56},{9,1},... | collective-permute-start | bytes 61448 | tf_op jit(solution)/shard_map/ppermute | solution.py:321
  6.6 7.8 %collective-permute-start = (f32[5,8,128]{2,1,0:T(8,128)S(1)}, f32[5,8,128]{2,1,0:T(8,128)S(1)}, u32[]{:S(2)}, u32[]{:S(2)}) collective-permute-start(f32[5,8,128]{2,1,0:T(8,128)S(1)} %shard_map.46), channel_id=1, source_target_pairs={{0,8},{8,16},{16,24},{24,32},{32,40},{40,48},{48,56},{56,0},{1,9},... | collective-permute-start | bytes 61448 | tf_op jit(solution)/shard_map/ppermute | solution.py:321
  35.6 11.9 %copy-start.4 = (s32[2,8]{1,0:T(2,128)S(1)}, s32[2,8]{1,0:T(2,128)}, u32[]{:S(2)}) copy-start(s32[2,8]{1,0:T(2,128)} %fractions.1) | copy-start | bytes 196
  35.6 11.9 %copy-start.3 = (s32[2,8]{1,0:T(2,128)S(1)}, s32[2,8]{1,0:T(2,128)}, u32[]{:S(2)}) copy-start(s32[2,8]{1,0:T(2,128)} %offsets.1) | copy-start | bytes 196
  35.6 4.9 %collective-permute-start.7 = (f32[8,3,8,128]{3,2,1,0:T(8,128)S(1)}, f32[8,3,8,128]{3,2,1,0:T(8,128)S(1)}, u32[]{:S(2)}, u32[]{:S(2)}) collective-permute-start(f32[8,3,8,128]{3,2,1,0:T(8,128)S(1)} %get-tuple-element.21), channel_id=1, source_target_pairs={{1,0},{2,1},{3,2},{4,3},{5,4},{6,5},{7,6},{0,7},{9,8},{10,9},{11,1... | collective-permute-start | bytes 294920 | tf_op jit(solution)/shard_map/ppermute | solution.py:321
  38.4 9.1 %collective-permute-start.6 = (f32[8,3,8,128]{3,2,1,0:T(8,128)S(1)}, f32[8,3,8,128]{3,2,1,0:T(8,128)S(1)}, u32[]{:S(2)}, u32[]{:S(2)}) collective-permute-start(f32[8,3,8,128]{3,2,1,0:T(8,128)S(1)} %get-tuple-element.22), channel_id=1, source_target_pairs={{0,1},{1,2},{2,3},{3,4},{4,5},{5,6},{6,7},{7,0},{8,9},{9,10},{10,1... | collective-permute-start | bytes 294920 | tf_op jit(solution)/shard_map/ppermute | solution.py:321
  50.5 14.1 %copy-start.2 = (s32[8,8,128]{2,1,0:T(8,128)S(1)}, s32[8,8,128]{2,1,0:T(8,128)}, u32[]{:S(2)}) copy-start(s32[8,8,128]{2,1,0:T(8,128)} %codes.5) | copy-start | bytes 98308
  50.5 25.4 %all-to-all-start.1 = ((f32[8,5,8,128]{3,2,1,0:T(8,128)}), f32[8,5,8,128]{3,2,1,0:T(8,128)S(1)}, u32[]{:S(2)}, u32[]{:S(2)}) async-start(f32[8,5,8,128]{3,2,1,0:T(8,128)} %shard_map.49), calls=%async_computation.1 | async-start | bytes 327680 | tf_op jit(solution)/shard_map/all_to_all | solution.py:348
  55.6 5.8 %collective-permute-start.2 = (f32[6,8,128]{2,1,0:T(8,128)S(1)}, f32[6,8,128]{2,1,0:T(8,128)S(1)}, u32[]{:S(2)}, u32[]{:S(2)}) collective-permute-start(f32[6,8,128]{2,1,0:T(8,128)S(1)} %get-tuple-element.15), channel_id=1, source_target_pairs={{0,64},{64,128},{128,192},{192,256},{256,320},{320,384},{384,448},... | collective-permute-start | bytes 73736 | tf_op jit(solution)/shard_map/ppermute | solution.py:321
  58.9 5.7 %collective-permute-start.3 = (f32[6,8,128]{2,1,0:T(8,128)S(1)}, f32[6,8,128]{2,1,0:T(8,128)S(1)}, u32[]{:S(2)}, u32[]{:S(2)}) collective-permute-start(f32[6,8,128]{2,1,0:T(8,128)S(1)} %get-tuple-element.16), channel_id=1, source_target_pairs={{64,0},{128,64},{192,128},{256,192},{320,256},{384,320},{448,384},... | collective-permute-start | bytes 73736 | tf_op jit(solution)/shard_map/ppermute | solution.py:321
  65.0 6.0 %collective-permute-start.4 = (f32[5,8,128]{2,1,0:T(8,128)S(1)}, f32[5,8,128]{2,1,0:T(8,128)S(1)}, u32[]{:S(2)}, u32[]{:S(2)}) collective-permute-start(f32[5,8,128]{2,1,0:T(8,128)S(1)} %get-tuple-element.18), channel_id=1, source_target_pairs={{0,64},{64,128},{128,192},{192,256},{256,320},{320,384},{384,448},... | collective-permute-start | bytes 61448 | tf_op jit(solution)/shard_map/ppermute | solution.py:321
  69.0 6.9 %collective-permute-start.5 = (f32[5,8,128]{2,1,0:T(8,128)S(1)}, f32[5,8,128]{2,1,0:T(8,128)S(1)}, u32[]{:S(2)}, u32[]{:S(2)}) collective-permute-start(f32[5,8,128]{2,1,0:T(8,128)S(1)} %get-tuple-element.19), channel_id=1, source_target_pairs={{64,0},{128,64},{192,128},{256,192},{320,256},{384,320},{448,384},... | collective-permute-start | bytes 61448 | tf_op jit(solution)/shard_map/ppermute | solution.py:321

commit v2 on v1

--- a/solution.py
+++ b/solution.py
@@ -21,6 +21,7 @@
 level = (0, 1, 2, 3, 4, 7, 8, 9, 10)
 forward = (1, 7, 9, 11, 13)
 backward = (2, 8, 10, 12, 14)
+sideways = (3, 4, 7, 8, 9, 10, 15, 16, 17, 18)
 F32 = jnp.float32
 
 
@@ -94,59 +95,110 @@
         out[tile] = packed
 
 
-def first_kernel(pops, codes, left, right, p1, side, chunks, ahead, behind):
+UPPER = [(i, 7) for i in rising] + [(i, 7) for i in level] + [(i, 6) for i in rising] + [(19, 7)]
+LOWER = [(i, 0) for i in sinking] + [(i, 0) for i in level] + [(i, 1) for i in sinking] + [(19, 0)]
+NEAR = [(group, tile, slot, i, z) for group, items in enumerate((UPPER, LOWER)) for tile in range(3) for slot, (i, z) in enumerate(items[7 * tile : 7 * tile + 7])]
+AHEAD_ROW, BEHIND_ROW = slice(7, 8), slice(0, 1)
+
+
+def row_place(j, z):
+    r = 6 * j + z - 1
+    return r // 8, slice(r % 8, r % 8 + 1)
+
+
+def main_kernel(pops, codes, p1, wrapped, chunks, ahead, behind):
     lane = lanes()
+    side = [jnp.zeros((8, 128), F32) for _ in range(19)]
+    for z in range(8):
+        f = [pops[i, z] * lattice_weights[i] for i in range(19)]
+        post = collide(f, codes[z].astype(F32) * (1.0 / LEVELS))
+        for i in range(19):
+            step = velocities[i][1]
+            value = roll(post[i], step, 1)
+            if step == 1:
+                side[i] = jnp.where(lane == 4 * z + 2, roll(value, 4 * z + 2, 1), side[i])
+            elif step == -1:
+                side[i] = jnp.where(lane == 4 * z + 1, roll(value, 4 * z + 2, 1), side[i])
+            p1[i, z] = value
+            target = z + velocities[i][2]
+            if 1 <= target <= 6 and i in forward:
+                tile, at = row_place(forward.index(i), target)
+                ahead[tile, at, :] = value[AHEAD_ROW, :]
+            if 1 <= target <= 6 and i in backward:
+                tile, at = row_place(backward.index(i), target)
+                behind[tile, at, :] = value[BEHIND_ROW, :]
+    for k, i in enumerate(sideways):
+        wrapped[k] = side[i]
+    for group in range(2):
+        for tile in range(3):
+            held = [jnp.zeros((8, 128), F32)] * 6
+            for _, _, slot, i, z in [n for n in NEAR if n[:2] == (group, tile)]:
+                source = p1[i, z] if i < 19 else codes[z].astype(F32)
+                for d in range(1, 7):
+                    moved = roll(source, 18 * slot - 16 * d + 1, 1)
+                    held[d - 1] = jnp.where(lane < 18 * slot, held[d - 1], moved)
+            for d in range(6):
+                chunks[d, group * 3 + tile] = held[d]
+
+
+def edge_kernel_2(left, right, p1, codes, wrapped, middle, ahead, behind, chunks, post_side, side):
+    lane = lanes()
+    ends = (lane == 0) | (lane == 127)
+    me, peers = lax.axis_index("gx"), lax.axis_size("gx")
+    after, before = (me + 1) % peers, (me + peers - 1) % peers
+    for tile in range(4):
+        chunks[after, 6 + tile] = ahead[tile]
+        chunks[before, 6 + tile] = behind[tile]
+    for d in range(1, 7):
+        for tile in range(6):
+            chunks[d, tile] = middle[d - 1, tile]
     outer = []
     for tile in range(5):
         both = jnp.where(lane % 4 < 2, left[tile], right[tile])
         for slot in range(4):
             outer.append(roll(both, -32 * slot, 1))
     beside = collide([outer[i] * lattice_weights[i] for i in range(19)], outer[19] * (1.0 / LEVELS))
-    shifted = []
-    for i in range(19):
-        shifted.append(roll(beside[i], velocities[i][1], 1))
-    for z in range(8):
-        f = [pops[i, z] * lattice_weights[i] for i in range(19)]
-        post = collide(f, codes[z].astype(F32) * (1.0 / LEVELS))
-        for i in range(19):
+    beside.append(outer[19])
+    shifted = list(beside)
+    for k, i in enumerate(sideways):
+        step = velocities[i][1]
+        shifted[i] = jnp.where(lane % 4 == (2 if step == 1 else 1), wrapped[k], roll(beside[i], step, 1))
+    for i in range(20):
+        side[i] = shifted[i]
+        post_side[i] = beside[i]
+    row_lane = lanes((1, 128))
+    for members, to, source, at_x in ((forward, after, ahead, AHEAD_ROW), (backward, before, behind, BEHIND_ROW)):
+        extra = [jnp.zeros((1, 128), F32)] * 2
+        for j, i in enumerate(members):
+            extra[j // 4] = jnp.where(row_lane // 32 == j % 4, roll(shifted[i][at_x, :], 32 * (j % 4), 1), extra[j // 4])
             step = velocities[i][1]
-            value = post[i]
-            if step == 1:
-                shifted[i] = jnp.where(lane == 4 * z + 2, roll(value, 4 * z + 3, 1), shifted[i])
-                value = jnp.where(lane == 0, roll(beside[i], -(4 * z + 1), 1), roll(value, 1, 1))
-            elif step == -1:
-                shifted[i] = jnp.where(lane == 4 * z + 1, roll(value, 4 * z + 1, 1), shifted[i])
-                value = jnp.where(lane == 127, roll(beside[i], 127 - (4 * z + 2), 1), roll(value, -1, 1))
-            p1[i, z] = value
-            if i in forward:
-                ahead[forward.index(i), z : z + 1, :] = value[7:8, :]
-            if i in backward:
-                behind[backward.index(i), z : z + 1, :] = value[0:1, :]
-    for i in range(19):
-        side[i] = shifted[i]
-    side[19] = outer[19]
-    for slot in range(5):
-        ahead[5, slot : slot + 1, :] = shifted[forward[slot]][7:8, :]
-        behind[5, slot : slot + 1, :] = shifted[backward[slot]][0:1, :]
-    for slot in range(5, 8):
-        ahead[5, slot : slot + 1, :] = jnp.zeros((1, 128), F32)
-        behind[5, slot : slot + 1, :] = jnp.zeros((1, 128), F32)
-    upper = [(i, 7) for i in rising] + [(i, 7) for i in level] + [(i, 6) for i in rising] + [(19, 7)]
-    lower = [(i, 0) for i in sinking] + [(i, 0) for i in level] + [(i, 1) for i in sinking] + [(19, 0)]
-    for group, items in enumerate((upper, lower)):
+            if step == 0:
+                continue
+            for z in range(1, 7):
+                tile, at = row_place(j, z)
+                lane_at, start = (0, 4 * z + 1) if step == 1 else (127, 4 * z + 2)
+                fixed = roll(beside[i][at_x, :], lane_at - start, 1)
+                chunks[to, 6 + tile, at, :] = jnp.where(row_lane == lane_at, fixed, source[tile, at, :])
+        chunks[to, 9, 6:7, :] = extra[0]
+        chunks[to, 9, 7:8, :] = extra[1]
+    for group in range(2):
         for tile in range(3):
-            held = [jnp.zeros((8, 128), F32)] * 8
-            for slot, (i, z) in enumerate(items[tile * 7 : tile * 7 + 7]):
+            held = [jnp.zeros((8, 128), F32)] * 2
+            for _, _, slot, i, z in [n for n in NEAR if n[:2] == (group, tile)]:
                 main = p1[i, z] if i < 19 else codes[z].astype(F32)
-                extra = shifted[i] if i < 19 else outer[19]
-                first = jnp.where(lane == 127, roll(extra, 127 - (4 * z + 1), 1), main)
-                last = jnp.where(lane == 0, roll(extra, -(4 * z + 2), 1), main)
-                for d in range(8):
-                    source = first if d == 0 else last if d == 7 else main
-                    moved = roll(source, 18 * slot - 16 * d + 1, 1)
-                    held[d] = jnp.where(lane < 18 * slot, held[d], moved)
-            for d in range(8):
-                chunks[d, group * 3 + tile] = held[d]
+                step = velocities[i][1] if i < 19 else 0
+                first = last = main
+                if step == 1:
+                    first = jnp.where(ends, roll(beside[i], 127 - 4 * z, 1), main)
+                elif step == -1:
+                    last = jnp.where(ends, roll(beside[i], 125 - 4 * z, 1), main)
+                else:
+                    first = jnp.where(lane == 127, roll(beside[i], 126 - 4 * z, 1), main)
+                    last = jnp.where(lane == 0, roll(beside[i], -(4 * z + 2), 1), main)
+                held[0] = jnp.where(lane < 18 * slot, held[0], roll(first, 18 * slot + 1, 1))
+                held[1] = jnp.where(lane < 18 * slot, held[1], roll(last, 18 * slot - 111, 1))
+            chunks[0, group * 3 + tile] = held[0]
+            chunks[7, group * 3 + tile] = held[1]
 
 
 def cross(outgoing, lane, shift_a, shift_b, frac_a, frac_b):
@@ -161,12 +213,29 @@
     return jnp.where(low, roll(mixed, 32, 1), roll(mixed, -32, 1))
 
 
-def plane_kernel(offsets, fractions, own, below, above, out, work, state):
+def spread_kernel(own, work):
+    lane8 = lanes()
+    for item in range(20):
+        tile, slot = divmod(item, 7)
+        for b in range(8):
+            value = jnp.where(
+                lane8 < 64,
+                roll(own[b, 3 + tile], 32 - 18 * slot, 1),
+                roll(own[b, tile], 64 - 18 * slot, 1),
+            )
+            work[item, 8 * b : 8 * b + 8, :] = value
+
+
+def plane_kernel(offsets, fractions, spread, below, above, ahead, behind, out, work, state):
     length = work.shape[1]
     lane8 = lanes()
     lane = lanes((length, 128))
     here = lax.axis_index("gz")
     after = (here + 1) % lax.axis_size("gz")
+    me, peers = lax.axis_index("gx"), lax.axis_size("gx")
+    for tile in range(4):
+        out[(me + 1) % peers, 5 + tile] = ahead[tile]
+        out[(me + peers - 1) % peers, 5 + tile] = behind[tile]
 
     def params(step):
         return (
@@ -179,14 +248,13 @@
     for item in range(20):
         tile, slot = divmod(item, 7)
         for b in range(8):
-            sets = (below[b, tile], own[b, 3 + tile], own[b, tile], above[b, tile])
-            moved = [roll(s, 32 * q - 18 * slot, 1) for q, s in enumerate(sets)]
-            value = jnp.where(
+            at = slice(8 * b, 8 * b + 8)
+            moved = jnp.where(
                 lane8 < 64,
-                jnp.where(lane8 < 32, moved[0], moved[1]),
-                jnp.where(lane8 < 96, moved[2], moved[3]),
+                roll(below[b, tile], -18 * slot, 1),
+                roll(above[b, tile], 96 - 18 * slot, 1),
             )
-            work[item, 8 * b : 8 * b + 8, :] = value
+            work[item, at, :] = jnp.where((lane8 >= 32) & (lane8 < 96), spread[item, at, :], moved)
     for j in range(5):
         step_x = velocities[rising[j]][0]
         state[sinking[j]] = roll(cross(work[j], lane, *params(0)), step_x, 0)
@@ -223,61 +291,86 @@
             out[b, tile] = packed
 
 
-def streamed_x(source, z, i, from_behind, from_ahead, row):
-    value = source[i, z]
+def moved_x(value, i, z, rows_behind, rows_ahead, first_tile, row):
     if i in forward:
-        j = forward.index(i)
-        return jnp.where(row == 0, jnp.broadcast_to(from_behind[j, z + 0 : z + 1, :], (8, 128)), roll(value, 1, 0))
-    if i in backward:
-        j = backward.index(i)
-        return jnp.where(row == 7, jnp.broadcast_to(from_ahead[j, z + 0 : z + 1, :], (8, 128)), roll(value, -1, 0))
-    return value
-
-
-def inner_kernel(p1, side, codes, from_behind, from_ahead, p2, ahead, behind):
+        tile, at = row_place(forward.index(i), z)
+        source, to = rows_behind(first_tile + tile, at), 0
+    elif i in backward:
+        tile, at = row_place(backward.index(i), z)
+        source, to = rows_ahead(first_tile + tile, at), 7
+    else:
+        return value
+    return jnp.where(row == to, jnp.broadcast_to(source, (8, 128)), roll(value, velocities[i][0], 0))
+
+
+def inner_kernel(p1, post_side, side, codes, own, p2, ahead, behind):
     lane, row = lanes(), rows()
+    me, peers = lax.axis_index("gx"), lax.axis_size("gx")
+    after, before = (me + 1) % peers, (me + peers - 1) % peers
+
+    def rows_behind(tile, at):
+        return own[before, tile, at, :]
+
+    def rows_ahead(tile, at):
+        return own[after, tile, at, :]
+
     f = []
     for i in range(19):
         value = side[i]
-        if i in forward:
-            j = forward.index(i)
-            value = jnp.where(row == 0, jnp.broadcast_to(from_behind[5, j : j + 1, :], (8, 128)), roll(value, 1, 0))
-        elif i in backward:
-            j = backward.index(i)
-            value = jnp.where(row == 7, jnp.broadcast_to(from_ahead[5, j : j + 1, :], (8, 128)), roll(value, -1, 0))
+        for members, get, to in ((forward, rows_behind, 0), (backward, rows_ahead, 7)):
+            if i in members:
+                j = members.index(i)
+                source = roll(get(9, slice(6 + j // 4, 7 + j // 4)), -32 * (j % 4), 1)
+                value = jnp.where(row == to, jnp.broadcast_to(source, (8, 128)), roll(value, velocities[i][0], 0))
         f.append(roll(value, 4 * velocities[i][2], 1))
     beside = collide(f, side[19] * (1.0 / LEVELS))
-    for j in range(5):
-        for z in (0, 7):
-            ahead[j, z : z + 1, :] = jnp.zeros((1, 128), F32)
-            behind[j, z : z + 1, :] = jnp.zeros((1, 128), F32)
+    for j in range(2):
+        ahead[3, 6 + j : 7 + j, :] = jnp.zeros((1, 128), F32)
+        behind[3, 6 + j : 7 + j, :] = jnp.zeros((1, 128), F32)
+
+    def mended(value, edge, step, z):
+        if step == 1:
+            return jnp.where(lane == 0, roll(edge, -(4 * z + 1), 1), value)
+        if step == -1:
+            return jnp.where(lane == 127, roll(edge, 127 - (4 * z + 2), 1), value)
+        return value
+
     for z in range(1, 7):
-        f = [streamed_x(p1, z - velocities[i][2], i, from_behind, from_ahead, row) for i in range(19)]
+        f = []
+        for i in range(19):
+            source = z - velocities[i][2]
+            value = mended(p1[i, source], post_side[i], velocities[i][1], source)
+            f.append(moved_x(value, i, z, rows_behind, rows_ahead, 6, row))
         post = collide(f, codes[z].astype(F32) * (1.0 / LEVELS))
         for i in range(19):
             step = velocities[i][1]
-            value = post[i]
-            if step == 1:
-                value = jnp.where(lane == 0, roll(beside[i], -(4 * z + 1), 1), roll(value, 1, 1))
-            elif step == -1:
-                value = jnp.where(lane == 127, roll(beside[i], 127 - (4 * z + 2), 1), roll(value, -1, 1))
-            p2[i, z] = value
+            value = mended(roll(post[i], step, 1), beside[i], step, z)
+            p2[i, z - 1] = value
             if i in forward:
-                ahead[forward.index(i), z : z + 1, :] = value[7:8, :]
+                tile, at = row_place(forward.index(i), z)
+                ahead[tile, at, :] = value[AHEAD_ROW, :]
             if i in backward:
-                behind[backward.index(i), z : z + 1, :] = value[0:1, :]
-    for i in range(19):
-        for z in (0, 7):
-            p2[i, z] = jnp.zeros((8, 128), F32)
-
-
-def last_kernel(p2, from_behind, from_ahead, planes, out):
+                tile, at = row_place(backward.index(i), z)
+                behind[tile, at, :] = value[BEHIND_ROW, :]
+
+
+def last_kernel(p2, planes, out):
     lane, row = lanes(), rows()
+    me, peers = lax.axis_index("gx"), lax.axis_size("gx")
+    after, before = (me + 1) % peers, (me + peers - 1) % peers
+
+    def rows_behind(tile, at):
+        return planes[before, tile, at, :]
+
+    def rows_ahead(tile, at):
+        return planes[after, tile, at, :]
+
     for i in range(19):
         for z in range(8):
             source = z - velocities[i][2]
             if 1 <= source <= 6:
-                out[i, z] = streamed_x(p2, source, i, from_behind, from_ahead, row) * weight_inverse[i]
+                value = moved_x(p2[i, source - 1], i, source, rows_behind, rows_ahead, 5, row)
+                out[i, z] = value * weight_inverse[i]
     target = []
     for group in range(2):
         z, inner = (7, 6) if group == 0 else (0, 1)
@@ -325,29 +418,33 @@
     tile = (8, 128)
     (edges,) = run(edge_kernel, [(5,) + tile], (pops, codes))
     left, right = neighbours(edges, edges, "gy")
-    p1, side, chunks, ahead, behind = run(
-        first_kernel,
-        [(19, 8) + tile, (20,) + tile, (8, 6) + tile, (6,) + tile, (6,) + tile],
-        (pops, codes, left, right),
+    p1, wrapped, middle, ahead, behind = run(
+        main_kernel,
+        [(19, 8) + tile, (10,) + tile, (6, 6) + tile, (4,) + tile, (4,) + tile],
+        (pops, codes),
+    )
+    chunks, post_side, side = run(
+        edge_kernel_2,
+        [(8, 10) + tile, (20,) + tile, (20,) + tile],
+        (left, right, p1, codes, wrapped, middle, ahead, behind),
     )
     own = lax.all_to_all(chunks, "gx", 0, 0)
-    from_behind, from_ahead = neighbours(ahead, behind, "gx")
     below, above = neighbours(own[:, 0:3], own[:, 3:6], "gz")
     p2, ahead, behind = run(
         inner_kernel,
-        [(19, 8) + tile, (5,) + tile, (5,) + tile],
-        (p1, side, codes, from_behind, from_ahead),
+        [(19, 6) + tile, (4,) + tile, (4,) + tile],
+        (p1, post_side, side, codes, own),
     )
+    (spread,) = run(spread_kernel, [(20, 64, 128)], (own,))
     (planes,) = run(
         plane_kernel,
-        [(8, 5) + tile],
-        (offsets, fractions, own, below, above),
+        [(8, 9) + tile],
+        (offsets, fractions, spread, below, above, ahead, behind),
         scalars=2,
         scratch=[(20, 64, 128), (19, 64, 128)],
     )
     planes = lax.all_to_all(planes, "gx", 0, 0)
-    from_behind, from_ahead = neighbours(ahead, behind, "gx")
-    (out,) = run(last_kernel, [(19, 8) + tile], (p2, from_behind, from_ahead, planes))
+    (out,) = run(last_kernel, [(19, 8) + tile], (p2, planes))
     return out
 
 

time: 77.6 us -> 66.1 us (0.85)
  the two profiles are of different devices: /device:TPU:72 before, /device:TPU:40 now
where the time goes in v2:
time: 66.1 us; the launch traced here: 65.6 us
  blocking collectives  35.2 us (53%)
  starting transfers between devices  11.7 us (18%)
  waiting for transfers between devices  11 us (17%)
  Pallas kernels  5.13 us (8%)
  local copies, waits for them, and re-layouts  2.53 us (4%)
    all_to_all x1, blocking collectives, body(): own = lax.all_to_all(chunks, 'gx', 0, 0)  22 us
    all_to_all x1, blocking collectives, body(): planes = lax.all_to_all(planes, 'gx', 0, 0)  13.2 us
    ppermute x2, waiting for transfers between devices, neighbours(): lax.ppermute(value_up, axis, up)  10.9 us
    ppermute x2, starting transfers between devices, neighbours(): lax.ppermute(value_down, axis, down)  7.37 us
    pallas_call x7, Pallas kernels, run(): pl.pallas_call(kernel, out_shape=shapes, in_specs=specs, out_specs=[pl.Bl...  5.13 us
    ppermute x2, starting transfers between devices, neighbours(): lax.ppermute(value_up, axis, up)  4.33 us
    unnamed x8, local copies, waits for them, and re-layouts  2.52 us
  transfers between devices with their start and end apart: 4, of which 2 were waited for; matrix products, arithmetic and copies ran while one was open for 0% of the time, Pallas kernels for 2%

profile of v2, /device:TPU:40, one launch (start us, length us, event | category | flops | bytes accessed | tf_op | source)
XLA Modules:
  0.0 65.6 jit_solution(10315783198228151195)
XLA Ops:
  0.0 0.0 copy-start
  0.0 1.1 %copy-done = f32[19,8,8,128]{3,2,1,0:T(8,128)S(1)} copy-done((f32[19,8,8,128]{3,2,1,0:T(8,128)S(1)}, f32[19,8,8,128]{3,2,1,0:T(8,128)}, u32[]{:S(2)}) %copy-start) | copy-done | bytes 622616
  1.1 0.0 copy-start.1
  1.1 0.8 %copy-done.1 = s32[8,8,128]{2,1,0:T(8,128)S(1)} copy-done((s32[8,8,128]{2,1,0:T(8,128)S(1)}, s32[8,8,128]{2,1,0:T(8,128)}, u32[]{:S(2)}) %copy-start.1) | copy-done | bytes 32792
  1.8 0.2 shard_map.47
  2.1 5.5 %collective-permute-start.1 = (f32[5,8,128]{2,1,0:T(8,128)S(1)}, f32[5,8,128]{2,1,0:T(8,128)S(1)}, u32[]{:S(2)}, u32[]{:S(2)}) collective-permute-start(f32[5,8,128]{2,1,0:T(8,128)S(1)} %shard_map.47), channel_id=1, source_target_pairs={{8,0},{16,8},{24,16},{32,24},{40,32},{48,40},{56,48},{0,56},{9,1},... | collective-permute-start | bytes 61448 | tf_op jit(solution)/shard_map/ppermute | solution.py:414
  7.5 1.9 %collective-permute-start = (f32[5,8,128]{2,1,0:T(8,128)S(1)}, f32[5,8,128]{2,1,0:T(8,128)S(1)}, u32[]{:S(2)}, u32[]{:S(2)}) collective-permute-start(f32[5,8,128]{2,1,0:T(8,128)S(1)} %shard_map.47), channel_id=1, source_target_pairs={{0,8},{8,16},{16,24},{24,32},{32,40},{40,48},{48,56},{56,0},{1,9},... | collective-permute-start | bytes 61448 | tf_op jit(solution)/shard_map/ppermute | solution.py:414
  9.5 0.7 %shard_map.46 = (f32[19,8,8,128]{3,2,1,0:T(8,128)S(1)}, f32[10,8,128]{2,1,0:T(8,128)S(1)}, f32[6,6,8,128]{3,2,1,0:T(8,128)S(1)}, f32[4,8,128]{2,1,0:T(8,128)S(1)}, f32[4,8,128]{2,1,0:T(8,128)S(1)}) custom-call(f32[19,8,8,128]{3,2,1,0:T(8,128)S(1)} %copy-done, s32[8,8,128]{2,1,0:T(8,128)S(1)} %copy-done.1), custom_call_target="tpu_custom_call" | custom-call | tf_op jit(solution)/shard_map/pallas_call | solution.py:400
  10.1 0.0 collective-permute-done.1.right
  10.2 5.2 %collective-permute-done.left = f32[5,8,128]{2,1,0:T(8,128)S(1)} collective-permute-done((f32[5,8,128]{2,1,0:T(8,128)S(1)}, f32[5,8,128]{2,1,0:T(8,128)S(1)}, u32[]{:S(2)}, u32[]{:S(2)}) %collective-permute-start) | collective-permute-done | bytes 20512 | tf_op jit(solution)/shard_map/ppermute | solution.py:414
  15.3 0.3 shard_map.48
  15.7 22.0 %all_to_all.10.own = f32[8,10,8,128]{3,2,1,0:T(8,128)S(1)} all-to-all(f32[8,10,8,128]{3,2,1,0:T(8,128)S(1)} %get-tuple-element.23), channel_id=1, replica_groups=mesh['gx'=8,'gy'=8,'gz'=8] {'gx'}, dimensions={0} | all-to-all | bytes 655360 | tf_op jit(solution)/shard_map/all_to_all | solution.py:431
  37.6 1.9 %collective-permute-start.3 = (f32[8,3,8,128]{3,2,1,0:T(8,128)S(1)}, f32[8,3,8,128]{3,2,1,0:T(8,128)S(1)}, u32[]{:S(2)}, u32[]{:S(2)}) collective-permute-start(f32[8,3,8,128]{3,2,1,0:T(8,128)S(1)} %get-tuple-element.27), channel_id=1, source_target_pairs={{1,0},{2,1},{3,2},{4,3},{5,4},{6,5},{7,6},{0,7},{9,8},{10,9},{11,1... | collective-permute-start | bytes 294920 | tf_op jit(solution)/shard_map/ppermute | solution.py:414
  39.6 2.4 %collective-permute-start.2 = (f32[8,3,8,128]{3,2,1,0:T(8,128)S(1)}, f32[8,3,8,128]{3,2,1,0:T(8,128)S(1)}, u32[]{:S(2)}, u32[]{:S(2)}) collective-permute-start(f32[8,3,8,128]{3,2,1,0:T(8,128)S(1)} %get-tuple-element.28), channel_id=1, source_target_pairs={{0,1},{1,2},{2,3},{3,4},{4,5},{5,6},{6,7},{7,0},{8,9},{9,10},{10,1... | collective-permute-start | bytes 294920 | tf_op jit(solution)/shard_map/ppermute | solution.py:414
  42.0 0.4 shard_map.50.spread
  42.4 0.0 copy-start.3
  42.4 0.5 shard_map.49
  42.9 0.0 collective-permute-done.3.above
  42.9 5.8 %collective-permute-done.2.below = f32[8,3,8,128]{3,2,1,0:T(8,128)S(1)} collective-permute-done((f32[8,3,8,128]{3,2,1,0:T(8,128)S(1)}, f32[8,3,8,128]{3,2,1,0:T(8,128)S(1)}, u32[]{:S(2)}, u32[]{:S(2)}) %collective-permute-start.2) | collective-permute-done | bytes 98336 | tf_op jit(solution)/shard_map/ppermute | solution.py:414
  48.7 0.0 copy-start.2
  48.7 0.0 copy-done.3
  48.7 0.7 %copy-done.2 = s32[2,8]{1,0:T(2,128)S(1)} copy-done((s32[2,8]{1,0:T(2,128)S(1)}, s32[2,8]{1,0:T(2,128)}, u32[]{:S(2)}) %copy-start.2) | copy-done | bytes 88
  49.3 1.9 %shard_map.51 = f32[8,9,8,128]{3,2,1,0:T(8,128)S(1)} custom-call(s32[2,8]{1,0:T(2,128)S(1)} %copy-done.2, s32[2,8]{1,0:T(2,128)S(1)} %copy-done.3, f32[20,64,128]{2,1,0:T(8,128)S(1)} %shard_map.50.spread, f32[8,3,8,128]{3,2,1,0:T(8,128)S(1)} %collective-permute-done.2.below, f32[8,3,8,128]{3,2,1,0:T(8,128)S(1)} %collective-permute-done.3.above, ...), custom_call_target="tpu_custom_call" | custom-call | tf_op jit(solution)/shard_map/pallas_call | solution.py:400
  51.3 13.2 %all_to_all.11.planes = f32[8,9,8,128]{3,2,1,0:T(8,128)S(1)} all-to-all(f32[8,9,8,128]{3,2,1,0:T(8,128)S(1)} %shard_map.51), channel_id=1, replica_groups=mesh['gx'=8,'gy'=8,'gz'=8] {'gx'}, dimensions={0} | all-to-all | bytes 589824 | tf_op jit(solution)/shard_map/all_to_all | solution.py:446
  64.5 1.1 %shard_map.52 = f32[19,8,8,128]{3,2,1,0:T(8,128)} custom-call(f32[19,6,8,128]{3,2,1,0:T(8,128)S(1)} %get-tuple-element.24.p2, f32[8,9,8,128]{3,2,1,0:T(8,128)S(1)} %all_to_all.11.planes), custom_call_target="tpu_custom_call" | custom-call | tf_op jit(solution)/shard_map/pallas_call | solution.py:400
  (1 shorter events, 0.0 us)
Async XLA Ops:
  0.0 1.1 %copy-start = (f32[19,8,8,128]{3,2,1,0:T(8,128)S(1)}, f32[19,8,8,128]{3,2,1,0:T(8,128)}, u32[]{:S(2)}) copy-start(f32[19,8,8,128]{3,2,1,0:T(8,128)} %pops.3) | copy-start | bytes 1867780
  1.1 0.8 %copy-start.1 = (s32[8,8,128]{2,1,0:T(8,128)S(1)}, s32[8,8,128]{2,1,0:T(8,128)}, u32[]{:S(2)}) copy-start(s32[8,8,128]{2,1,0:T(8,128)} %codes.7) | copy-start | bytes 98308
  2.1 8.1 %collective-permute-start.1 = (f32[5,8,128]{2,1,0:T(8,128)S(1)}, f32[5,8,128]{2,1,0:T(8,128)S(1)}, u32[]{:S(2)}, u32[]{:S(2)}) collective-permute-start(f32[5,8,128]{2,1,0:T(8,128)S(1)} %shard_map.47), channel_id=1, source_target_pairs={{8,0},{16,8},{24,16},{32,24},{40,32},{48,40},{56,48},{0,56},{9,1},... | collective-permute-start | bytes 61448 | tf_op jit(solution)/shard_map/ppermute | solution.py:414
  7.5 7.8 %collective-permute-start = (f32[5,8,128]{2,1,0:T(8,128)S(1)}, f32[5,8,128]{2,1,0:T(8,128)S(1)}, u32[]{:S(2)}, u32[]{:S(2)}) collective-permute-start(f32[5,8,128]{2,1,0:T(8,128)S(1)} %shard_map.47), channel_id=1, source_target_pairs={{0,8},{8,16},{16,24},{24,32},{32,40},{40,48},{48,56},{56,0},{1,9},... | collective-permute-start | bytes 61448 | tf_op jit(solution)/shard_map/ppermute | solution.py:414
  37.6 5.2 %collective-permute-start.3 = (f32[8,3,8,128]{3,2,1,0:T(8,128)S(1)}, f32[8,3,8,128]{3,2,1,0:T(8,128)S(1)}, u32[]{:S(2)}, u32[]{:S(2)}) collective-permute-start(f32[8,3,8,128]{3,2,1,0:T(8,128)S(1)} %get-tuple-element.27), channel_id=1, source_target_pairs={{1,0},{2,1},{3,2},{4,3},{5,4},{6,5},{7,6},{0,7},{9,8},{10,9},{11,1... | collective-permute-start | bytes 294920 | tf_op jit(solution)/shard_map/ppermute | solution.py:414
  39.6 9.1 %collective-permute-start.2 = (f32[8,3,8,128]{3,2,1,0:T(8,128)S(1)}, f32[8,3,8,128]{3,2,1,0:T(8,128)S(1)}, u32[]{:S(2)}, u32[]{:S(2)}) collective-permute-start(f32[8,3,8,128]{3,2,1,0:T(8,128)S(1)} %get-tuple-element.28), channel_id=1, source_target_pairs={{0,1},{1,2},{2,3},{3,4},{4,5},{5,6},{6,7},{7,0},{8,9},{9,10},{10,1... | collective-permute-start | bytes 294920 | tf_op jit(solution)/shard_map/ppermute | solution.py:414
  42.4 6.3 %copy-start.3 = (s32[2,8]{1,0:T(2,128)S(1)}, s32[2,8]{1,0:T(2,128)}, u32[]{:S(2)}) copy-start(s32[2,8]{1,0:T(2,128)} %fractions.1) | copy-start | bytes 196
  48.7 0.7 %copy-start.2 = (s32[2,8]{1,0:T(2,128)S(1)}, s32[2,8]{1,0:T(2,128)}, u32[]{:S(2)}) copy-start(s32[2,8]{1,0:T(2,128)} %offsets.1) | copy-start | bytes 196

commit v3 on v2

--- a/solution.py
+++ b/solution.py
@@ -81,12 +81,17 @@
     return post
 
 
-def edge_kernel(pops, codes, out):
+def edge_kernel(pops_far, codes_far, out, pops, codes, sems):
     lane = lanes()
+    copies = [pltpu.make_async_copy(pops_far.at[i], pops.at[i], sems.at[i]) for i in range(19)]
+    copies.append(pltpu.make_async_copy(codes_far, codes, sems.at[19]))
+    for copy in copies:
+        copy.start()
     for tile in range(5):
         packed = jnp.zeros((8, 128), F32)
         for slot in range(4):
             item = tile * 4 + slot
+            copies[item].wait()
             for z in range(8):
                 start = slot * 32 + z * 4
                 source = pops[item, z] if item < 19 else codes[z].astype(F32)
@@ -111,7 +116,7 @@
     side = [jnp.zeros((8, 128), F32) for _ in range(19)]
     for z in range(8):
         f = [pops[i, z] * lattice_weights[i] for i in range(19)]
-        post = collide(f, codes[z].astype(F32) * (1.0 / LEVELS))
+        post = collide(f, codes[z] * (1.0 / LEVELS))
         for i in range(19):
             step = velocities[i][1]
             value = roll(post[i], step, 1)
@@ -133,7 +138,7 @@
         for tile in range(3):
             held = [jnp.zeros((8, 128), F32)] * 6
             for _, _, slot, i, z in [n for n in NEAR if n[:2] == (group, tile)]:
-                source = p1[i, z] if i < 19 else codes[z].astype(F32)
+                source = p1[i, z] if i < 19 else codes[z]
                 for d in range(1, 7):
                     moved = roll(source, 18 * slot - 16 * d + 1, 1)
                     held[d - 1] = jnp.where(lane < 18 * slot, held[d - 1], moved)
@@ -185,7 +190,7 @@
         for tile in range(3):
             held = [jnp.zeros((8, 128), F32)] * 2
             for _, _, slot, i, z in [n for n in NEAR if n[:2] == (group, tile)]:
-                main = p1[i, z] if i < 19 else codes[z].astype(F32)
+                main = p1[i, z] if i < 19 else codes[z]
                 step = velocities[i][1] if i < 19 else 0
                 first = last = main
                 if step == 1:
@@ -213,7 +218,7 @@
     return jnp.where(low, roll(mixed, 32, 1), roll(mixed, -32, 1))
 
 
-def spread_kernel(own, work):
+def spread_kernel(offsets, fractions, own, work):
     lane8 = lanes()
     for item in range(20):
         tile, slot = divmod(item, 7)
@@ -226,11 +231,12 @@
             work[item, 8 * b : 8 * b + 8, :] = value
 
 
-def plane_kernel(offsets, fractions, spread, below, above, ahead, behind, out, work, state):
+def plane_kernel(offsets, fractions, spread, near, far, ahead, behind, out, work, state):
     length = work.shape[1]
     lane8 = lanes()
     lane = lanes((length, 128))
     here = lax.axis_index("gz")
+    even = here % 2 == 0
     after = (here + 1) % lax.axis_size("gz")
     me, peers = lax.axis_index("gx"), lax.axis_size("gx")
     for tile in range(4):
@@ -249,10 +255,12 @@
         tile, slot = divmod(item, 7)
         for b in range(8):
             at = slice(8 * b, 8 * b + 8)
+            below = jnp.where(even, far[b, tile], near[b, tile])
+            above = jnp.where(even, near[b, tile], far[b, tile])
             moved = jnp.where(
                 lane8 < 64,
-                roll(below[b, tile], -18 * slot, 1),
-                roll(above[b, tile], 96 - 18 * slot, 1),
+                roll(below, -18 * slot, 1),
+                roll(above, 96 - 18 * slot, 1),
             )
             work[item, at, :] = jnp.where((lane8 >= 32) & (lane8 < 96), spread[item, at, :], moved)
     for j in range(5):
@@ -341,7 +349,7 @@
             source = z - velocities[i][2]
             value = mended(p1[i, source], post_side[i], velocities[i][1], source)
             f.append(moved_x(value, i, z, rows_behind, rows_ahead, 6, row))
-        post = collide(f, codes[z].astype(F32) * (1.0 / LEVELS))
+        post = collide(f, codes[z] * (1.0 / LEVELS))
         for i in range(19):
             step = velocities[i][1]
             value = mended(roll(post[i], step, 1), beside[i], step, z)
@@ -354,7 +362,7 @@
                 behind[tile, at, :] = value[BEHIND_ROW, :]
 
 
-def last_kernel(p2, planes, out):
+def last_kernel(p2, planes, out, held_out, sems):
     lane, row = lanes(), rows()
     me, peers = lax.axis_index("gx"), lax.axis_size("gx")
     after, before = (me + 1) % peers, (me + peers - 1) % peers
@@ -365,12 +373,6 @@
     def rows_ahead(tile, at):
         return planes[after, tile, at, :]
 
-    for i in range(19):
-        for z in range(8):
-            source = z - velocities[i][2]
-            if 1 <= source <= 6:
-                value = moved_x(p2[i, source - 1], i, source, rows_behind, rows_ahead, 5, row)
-                out[i, z] = value * weight_inverse[i]
     target = []
     for group in range(2):
         z, inner = (7, 6) if group == 0 else (0, 1)
@@ -390,19 +392,36 @@
             n = tile * 8 + slot
             if n < 38:
                 i, z = target[n]
-                out[i, z] = held[slot] * weight_inverse[i]
-
-
-def run(kernel, outs, args, scalars=0, scratch=()):
+                held_out[i, z] = held[slot] * weight_inverse[i]
+    copies = []
+    for i in range(19):
+        for z in range(8):
+            source = z - velocities[i][2]
+            if 1 <= source <= 6:
+                value = moved_x(p2[i, source - 1], i, source, rows_behind, rows_ahead, 5, row)
+                held_out[i, z] = value * weight_inverse[i]
+        copies.append(pltpu.make_async_copy(held_out.at[i], out.at[i], sems.at[i]))
+        copies[i].start()
+    for copy in copies:
+        copy.wait()
+
+
+def run(kernel, outs, args, scalars=0, scratch=(), far_in=False, far_out=False, sems=0):
+    near = pl.BlockSpec(memory_space=pltpu.VMEM)
+    away = pl.BlockSpec(memory_space=pltpu.HBM)
     specs = [pl.BlockSpec(memory_space=pltpu.SMEM)] * scalars
-    specs += [pl.BlockSpec(memory_space=pltpu.VMEM)] * (len(args) - scalars)
+    specs += [away if far_in else near] * (len(args) - scalars)
     shapes = [jax.ShapeDtypeStruct(s, F32) for s in outs]
+
+    def held(s):
+        return pltpu.VMEM(s.shape, s.dtype) if isinstance(s, jax.ShapeDtypeStruct) else pltpu.VMEM(s, F32)
+
     return pl.pallas_call(
         kernel,
         out_shape=shapes,
         in_specs=specs,
-        out_specs=[pl.BlockSpec(memory_space=pltpu.VMEM)] * len(outs),
-        scratch_shapes=[pltpu.VMEM(s, F32) for s in scratch],
+        out_specs=[away if far_out else near] * len(outs),
+        scratch_shapes=[held(s) for s in scratch] + [pltpu.SemaphoreType.DMA((sems,))] * (sems > 0),
         compiler_params=pltpu.CompilerParams(vmem_limit_bytes=32 * 1024 * 1024),
     )(*args)
 
@@ -414,9 +433,29 @@
     return lax.ppermute(value_up, axis, up), lax.ppermute(value_down, axis, down)
 
 
+def swaps(own):
+    peers = lax.axis_size("gz")
+    even = lax.axis_index("gz") % 2 == 0
+    upper, lower = own[:, 0:3], own[:, 3:6]
+    pair = [(i, i ^ 1) for i in range(peers)]
+    other = [(i, (i + peers - 1) % peers if i % 2 == 0 else (i + 1) % peers) for i in range(peers)]
+    far = lax.ppermute(jnp.where(even, lower, upper), "gz", other)
+    near = lax.ppermute(jnp.where(even, upper, lower), "gz", pair)
+    return near, far
+
+
 def body(pops, codes, offsets, fractions):
     tile = (8, 128)
-    (edges,) = run(edge_kernel, [(5,) + tile], (pops, codes))
+    far = [pltpu.with_memory_space_constraint(value, pltpu.HBM) for value in (pops, codes)]
+    (edges,) = run(
+        edge_kernel,
+        [(5,) + tile],
+        far,
+        scratch=[(19, 8) + tile, jax.ShapeDtypeStruct((8,) + tile, jnp.int32)],
+        far_in=True,
+        sems=20,
+    )
+    codes = codes.astype(F32)
     left, right = neighbours(edges, edges, "gy")
     p1, wrapped, middle, ahead, behind = run(
         main_kernel,
@@ -429,22 +468,24 @@
         (left, right, p1, codes, wrapped, middle, ahead, behind),
     )
     own = lax.all_to_all(chunks, "gx", 0, 0)
-    below, above = neighbours(own[:, 0:3], own[:, 3:6], "gz")
+    near, far = swaps(own)
     p2, ahead, behind = run(
         inner_kernel,
         [(19, 6) + tile, (4,) + tile, (4,) + tile],
         (p1, post_side, side, codes, own),
     )
-    (spread,) = run(spread_kernel, [(20, 64, 128)], (own,))
+    (spread,) = run(spread_kernel, [(20, 64, 128)], (offsets, fractions, own), scalars=2)
     (planes,) = run(
         plane_kernel,
         [(8, 9) + tile],
-        (offsets, fractions, spread, below, above, ahead, behind),
+        (offsets, fractions, spread, near, far, ahead, behind),
         scalars=2,
         scratch=[(20, 64, 128), (19, 64, 128)],
     )
     planes = lax.all_to_all(planes, "gx", 0, 0)
-    (out,) = run(last_kernel, [(19, 8) + tile], (p2, planes))
+    (out,) = run(
+        last_kernel, [(19, 8) + tile], (p2, planes), scratch=[(19, 8) + tile], far_out=True, sems=19
+    )
     return out
 
 

time: 66.1 us -> 67.2 us (1.017)
  the two profiles are of different devices: /device:TPU:40 before, /device:TPU:1 now
where the time goes in v3:
time: 67.2 us; the launch traced here: 66.8 us
  starting transfers between devices  28.5 us (42%)
  blocking collectives  15.1 us (22%)
  waiting for transfers between devices  13.9 us (21%)
  Pallas kernels  8.95 us (13%)
    all_to_all x1, blocking collectives, body(): planes = lax.all_to_all(planes, 'gx', 0, 0)  15.1 us
    all_to_all x1, starting transfers between devices, body(): own = lax.all_to_all(chunks, 'gx', 0, 0)  10 us
    all_to_all x1, waiting for transfers between devices, body(): own = lax.all_to_all(chunks, 'gx', 0, 0)  9.97 us
    pallas_call x7, Pallas kernels, run(): pl.pallas_call(kernel, out_shape=shapes, in_specs=specs, out_specs=[away...  8.95 us
    ppermute x1, starting transfers between devices, swaps(): far = lax.ppermute(jnp.where(even, lower, upper), 'gz', other)  8.37 us
    ppermute x1, starting transfers between devices, neighbours(): lax.ppermute(value_down, axis, down)  6.23 us
    ppermute x1, waiting for transfers between devices, neighbours(): lax.ppermute(value_up, axis, up)  3.97 us
    ppermute x1, starting transfers between devices, neighbours(): lax.ppermute(value_up, axis, up)  1.92 us
  transfers between devices with their start and end apart: 5, of which 2 were waited for; matrix products, arithmetic and copies ran while one was open for 0% of the time, Pallas kernels for 3%

profile of v3, /device:TPU:1, one launch (start us, length us, event | category | flops | bytes accessed | tf_op | source)
XLA Modules:
  0.0 66.8 jit_solution(14772190681232420617)
XLA Ops:
  0.0 0.0 copy-start.3
  0.0 0.0 copy-start
  0.0 2.5 %shard_map.47 = f32[5,8,128]{2,1,0:T(8,128)S(1)} custom-call(f32[19,8,8,128]{3,2,1,0:T(8,128)} %pops_far.1, s32[8,8,128]{2,1,0:T(8,128)} %codes_far.1), custom_call_target="tpu_custom_call" | custom-call | tf_op jit(solution)/shard_map/pallas_call | solution.py:419
  2.5 6.2 %collective-permute-start.1 = (f32[5,8,128]{2,1,0:T(8,128)S(1)}, f32[5,8,128]{2,1,0:T(8,128)S(1)}, u32[]{:S(2)}, u32[]{:S(2)}) collective-permute-start(f32[5,8,128]{2,1,0:T(8,128)S(1)} %shard_map.47), channel_id=1, source_target_pairs={{8,0},{16,8},{24,16},{32,24},{40,32},{48,40},{56,48},{0,56},{9,1},... | collective-permute-start | bytes 61448 | tf_op jit(solution)/shard_map/ppermute | solution.py:433
  8.8 1.9 %collective-permute-start = (f32[5,8,128]{2,1,0:T(8,128)S(1)}, f32[5,8,128]{2,1,0:T(8,128)S(1)}, u32[]{:S(2)}, u32[]{:S(2)}) collective-permute-start(f32[5,8,128]{2,1,0:T(8,128)S(1)} %shard_map.47), channel_id=1, source_target_pairs={{0,8},{8,16},{16,24},{24,32},{32,40},{40,48},{48,56},{56,0},{1,9},... | collective-permute-start | bytes 61448 | tf_op jit(solution)/shard_map/ppermute | solution.py:433
  10.7 0.0 copy-done.3
  10.7 0.0 copy-done
  10.7 0.7 %shard_map.46 = (f32[19,8,8,128]{3,2,1,0:T(8,128)S(1)}, f32[10,8,128]{2,1,0:T(8,128)S(1)}, f32[6,6,8,128]{3,2,1,0:T(8,128)S(1)}, f32[4,8,128]{2,1,0:T(8,128)S(1)}, f32[4,8,128]{2,1,0:T(8,128)S(1)}) custom-call(f32[19,8,8,128]{3,2,1,0:T(8,128)S(1)} %copy-done, f32[8,8,128]{2,1,0:T(8,128)S(1)} %convert_element_type.3.codes), custom_call_target="tpu_custom_call" | custom-call | tf_op jit(solution)/shard_map/pallas_call | solution.py:419
  11.4 0.0 collective-permute-done.1.right
  11.5 4.0 %collective-permute-done.left = f32[5,8,128]{2,1,0:T(8,128)S(1)} collective-permute-done((f32[5,8,128]{2,1,0:T(8,128)S(1)}, f32[5,8,128]{2,1,0:T(8,128)S(1)}, u32[]{:S(2)}, u32[]{:S(2)}) %collective-permute-start) | collective-permute-done | bytes 20512 | tf_op jit(solution)/shard_map/ppermute | solution.py:433
  15.4 1.1 %shard_map.48 = (f32[8,10,8,128]{3,2,1,0:T(8,128)}, f32[20,8,128]{2,1,0:T(8,128)S(1)}, f32[20,8,128]{2,1,0:T(8,128)S(1)}) custom-call(f32[5,8,128]{2,1,0:T(8,128)S(1)} %collective-permute-done.left, f32[5,8,128]{2,1,0:T(8,128)S(1)} %collective-permute-done.1.right, f32[19,8,8,128]{3,2,1,0:T(8,128)S(1)} %get-tuple-element.16.p1, ...), custom_call_target="tpu_custom_call" | custom-call | tf_op jit(solution)/shard_map/pallas_call | solution.py:419
  16.5 10.0 %all-to-all-start = ((f32[8,10,8,128]{3,2,1,0:T(8,128)}), f32[8,10,8,128]{3,2,1,0:T(8,128)S(1)}, u32[]{:S(2)}, u32[]{:S(2)}) async-start(f32[8,10,8,128]{3,2,1,0:T(8,128)} %get-tuple-element.23), calls=%async_computation | async-start | bytes 655360 | tf_op jit(solution)/shard_map/all_to_all | solution.py:470
  26.5 10.0 %all-to-all-done.own = f32[8,10,8,128]{3,2,1,0:T(8,128)S(1)} async-done(((f32[8,10,8,128]{3,2,1,0:T(8,128)}), f32[8,10,8,128]{3,2,1,0:T(8,128)S(1)}, u32[]{:S(2)}, u32[]{:S(2)}) %all-to-all-start) | async-done | bytes 327712 | tf_op jit(solution)/shard_map/all_to_all | solution.py:470
  36.5 8.4 %collective-permute-start.3 = (f32[8,3,8,128]{3,2,1,0:T(8,128)S(1)}, f32[8,3,8,128]{3,2,1,0:T(8,128)S(1)}, u32[]{:S(2)}, u32[]{:S(2)}) collective-permute-start(f32[8,3,8,128]{3,2,1,0:T(8,128)S(1)} %get-tuple-element.27), channel_id=1, source_target_pairs={{0,7},{1,2},{2,1},{3,4},{4,3},{5,6},{6,5},{7,0},{8,15},{9,10},{10,... | collective-permute-start | bytes 294920 | tf_op jit(solution)/shard_map/ppermute | solution.py:442
  44.9 1.9 %collective-permute-start.2 = (f32[8,3,8,128]{3,2,1,0:T(8,128)S(1)}, f32[8,3,8,128]{3,2,1,0:T(8,128)S(1)}, u32[]{:S(2)}, u32[]{:S(2)}) collective-permute-start(f32[8,3,8,128]{3,2,1,0:T(8,128)S(1)} %get-tuple-element.28), channel_id=1, source_target_pairs={{0,1},{1,0},{2,3},{3,2},{4,5},{5,4},{6,7},{7,6},{8,9},{9,8},{10,11... | collective-permute-start | bytes 294920 | tf_op jit(solution)/shard_map/ppermute | solution.py:443
  46.8 0.0 copy-start.1
  46.8 0.0 copy-start.2
  46.8 0.5 shard_map.49
  47.3 0.2 copy-done.1
  47.5 0.0 copy-done.2
  47.5 1.0 %shard_map.50.spread = f32[20,64,128]{2,1,0:T(8,128)S(1)} custom-call(s32[2,8]{1,0:T(2,128)S(1)} %copy-done.1, s32[2,8]{1,0:T(2,128)S(1)} %copy-done.2, f32[8,10,8,128]{3,2,1,0:T(8,128)S(1)} %all-to-all-done.own), custom_call_target="tpu_custom_call" | custom-call | tf_op jit(solution)/shard_map/pallas_call | solution.py:419
  48.5 0.0 collective-permute-done.3.far
  48.5 0.0 collective-permute-done.2.near
  48.5 2.0 %shard_map.51 = f32[8,9,8,128]{3,2,1,0:T(8,128)S(1)} custom-call(s32[2,8]{1,0:T(2,128)S(1)} %copy-done.1, s32[2,8]{1,0:T(2,128)S(1)} %copy-done.2, f32[20,64,128]{2,1,0:T(8,128)S(1)} %shard_map.50.spread, f32[8,3,8,128]{3,2,1,0:T(8,128)S(1)} %collective-permute-done.2.near, f32[8,3,8,128]{3,2,1,0:T(8,128)S(1)} %collective-permute-done.3.far, ...), custom_call_target="tpu_custom_call" | custom-call | tf_op jit(solution)/shard_map/pallas_call | solution.py:419
  50.5 15.1 %all_to_all.10.planes = f32[8,9,8,128]{3,2,1,0:T(8,128)S(1)} all-to-all(f32[8,9,8,128]{3,2,1,0:T(8,128)S(1)} %shard_map.51), channel_id=1, replica_groups=mesh['gx'=8,'gy'=8,'gz'=8] {'gx'}, dimensions={0} | all-to-all | bytes 589824 | tf_op jit(solution)/shard_map/all_to_all | solution.py:485
  65.6 1.2 %shard_map.52 = f32[19,8,8,128]{3,2,1,0:T(8,128)} custom-call(f32[19,6,8,128]{3,2,1,0:T(8,128)S(1)} %get-tuple-element.24.p2, f32[8,9,8,128]{3,2,1,0:T(8,128)S(1)} %all_to_all.10.planes), custom_call_target="tpu_custom_call" | custom-call | tf_op jit(solution)/shard_map/pallas_call | solution.py:419
  (2 shorter events, 0.0 us)
Async XLA Ops:
  0.0 10.7 %copy-start.3 = (s32[8,8,128]{2,1,0:T(8,128)S(1)}, s32[8,8,128]{2,1,0:T(8,128)}, u32[]{:S(2)}) copy-start(s32[8,8,128]{2,1,0:T(8,128)} %codes_far.1) | copy-start | bytes 98308
  0.0 10.7 %copy-start = (f32[19,8,8,128]{3,2,1,0:T(8,128)S(1)}, f32[19,8,8,128]{3,2,1,0:T(8,128)}, u32[]{:S(2)}) copy-start(f32[19,8,8,128]{3,2,1,0:T(8,128)} %pops_far.1) | copy-start | bytes 1867780
  2.5 8.9 %collective-permute-start.1 = (f32[5,8,128]{2,1,0:T(8,128)S(1)}, f32[5,8,128]{2,1,0:T(8,128)S(1)}, u32[]{:S(2)}, u32[]{:S(2)}) collective-permute-start(f32[5,8,128]{2,1,0:T(8,128)S(1)} %shard_map.47), channel_id=1, source_target_pairs={{8,0},{16,8},{24,16},{32,24},{40,32},{48,40},{56,48},{0,56},{9,1},... | collective-permute-start | bytes 61448 | tf_op jit(solution)/shard_map/ppermute | solution.py:433
  8.8 6.6 %collective-permute-start = (f32[5,8,128]{2,1,0:T(8,128)S(1)}, f32[5,8,128]{2,1,0:T(8,128)S(1)}, u32[]{:S(2)}, u32[]{:S(2)}) collective-permute-start(f32[5,8,128]{2,1,0:T(8,128)S(1)} %shard_map.47), channel_id=1, source_target_pairs={{0,8},{8,16},{16,24},{24,32},{32,40},{40,48},{48,56},{56,0},{1,9},... | collective-permute-start | bytes 61448 | tf_op jit(solution)/shard_map/ppermute | solution.py:433
  16.5 20.0 %all-to-all-start = ((f32[8,10,8,128]{3,2,1,0:T(8,128)}), f32[8,10,8,128]{3,2,1,0:T(8,128)S(1)}, u32[]{:S(2)}, u32[]{:S(2)}) async-start(f32[8,10,8,128]{3,2,1,0:T(8,128)} %get-tuple-element.23), calls=%async_computation | async-start | bytes 655360 | tf_op jit(solution)/shard_map/all_to_all | solution.py:470
  36.5 12.0 %collective-permute-start.3 = (f32[8,3,8,128]{3,2,1,0:T(8,128)S(1)}, f32[8,3,8,128]{3,2,1,0:T(8,128)S(1)}, u32[]{:S(2)}, u32[]{:S(2)}) collective-permute-start(f32[8,3,8,128]{3,2,1,0:T(8,128)S(1)} %get-tuple-element.27), channel_id=1, source_target_pairs={{0,7},{1,2},{2,1},{3,4},{4,3},{5,6},{6,5},{7,0},{8,15},{9,10},{10,... | collective-permute-start | bytes 294920 | tf_op jit(solution)/shard_map/ppermute | solution.py:442
  44.9 3.6 %collective-permute-start.2 = (f32[8,3,8,128]{3,2,1,0:T(8,128)S(1)}, f32[8,3,8,128]{3,2,1,0:T(8,128)S(1)}, u32[]{:S(2)}, u32[]{:S(2)}) collective-permute-start(f32[8,3,8,128]{3,2,1,0:T(8,128)S(1)} %get-tuple-element.28), channel_id=1, source_target_pairs={{0,1},{1,0},{2,3},{3,2},{4,5},{5,4},{6,7},{7,6},{8,9},{9,8},{10,11... | collective-permute-start | bytes 294920 | tf_op jit(solution)/shard_map/ppermute | solution.py:443
  46.8 0.7 %copy-start.1 = (s32[2,8]{1,0:T(2,128)S(1)}, s32[2,8]{1,0:T(2,128)}, u32[]{:S(2)}) copy-start(s32[2,8]{1,0:T(2,128)} %offsets.3) | copy-start | bytes 196
  46.8 0.7 %copy-start.2 = (s32[2,8]{1,0:T(2,128)S(1)}, s32[2,8]{1,0:T(2,128)}, u32[]{:S(2)}) copy-start(s32[2,8]{1,0:T(2,128)} %fractions.3) | copy-start | bytes 196

commit v4 on v3

--- a/solution.py
+++ b/solution.py
@@ -83,15 +83,20 @@
 
 def edge_kernel(pops_far, codes_far, out, pops, codes, sems):
     lane = lanes()
-    copies = [pltpu.make_async_copy(pops_far.at[i], pops.at[i], sems.at[i]) for i in range(19)]
-    copies.append(pltpu.make_async_copy(codes_far, codes, sems.at[19]))
+    copies = []
+    for tile in range(5):
+        part = pl.ds(4 * tile, min(4, 19 - 4 * tile))
+        copies.append(pltpu.make_async_copy(pops_far.at[part], pops.at[part], sems.at[tile]))
+    copies.append(pltpu.make_async_copy(codes_far, codes, sems.at[5]))
     for copy in copies:
         copy.start()
     for tile in range(5):
+        copies[tile].wait()
         packed = jnp.zeros((8, 128), F32)
         for slot in range(4):
             item = tile * 4 + slot
-            copies[item].wait()
+            if item == 19:
+                copies[5].wait()
             for z in range(8):
                 start = slot * 32 + z * 4
                 source = pops[item, z] if item < 19 else codes[z].astype(F32)
@@ -106,6 +111,11 @@
 AHEAD_ROW, BEHIND_ROW = slice(7, 8), slice(0, 1)
 
 
+def set_bases():
+    odd = lax.axis_index("gz") % 2
+    return 3 * odd, 3 - 3 * odd
+
+
 def row_place(j, z):
     r = 6 * j + z - 1
     return r // 8, slice(r % 8, r % 8 + 1)
@@ -116,7 +126,7 @@
     side = [jnp.zeros((8, 128), F32) for _ in range(19)]
     for z in range(8):
         f = [pops[i, z] * lattice_weights[i] for i in range(19)]
-        post = collide(f, codes[z] * (1.0 / LEVELS))
+        post = collide(f, codes[z].astype(F32) * (1.0 / LEVELS))
         for i in range(19):
             step = velocities[i][1]
             value = roll(post[i], step, 1)
@@ -137,11 +147,12 @@
     for group in range(2):
         for tile in range(3):
             held = [jnp.zeros((8, 128), F32)] * 6
+            place = (lane + 32 * group) % 128
             for _, _, slot, i, z in [n for n in NEAR if n[:2] == (group, tile)]:
-                source = p1[i, z] if i < 19 else codes[z]
+                source = p1[i, z] if i < 19 else codes[z].astype(F32)
                 for d in range(1, 7):
-                    moved = roll(source, 18 * slot - 16 * d + 1, 1)
-                    held[d - 1] = jnp.where(lane < 18 * slot, held[d - 1], moved)
+                    moved = roll(source, 18 * slot - 16 * d + 1 + 96 * group, 1)
+                    held[d - 1] = jnp.where(place < 18 * slot, held[d - 1], moved)
             for d in range(6):
                 chunks[d, group * 3 + tile] = held[d]
 
@@ -154,9 +165,11 @@
     for tile in range(4):
         chunks[after, 6 + tile] = ahead[tile]
         chunks[before, 6 + tile] = behind[tile]
+    bases = set_bases()
     for d in range(1, 7):
-        for tile in range(6):
-            chunks[d, tile] = middle[d - 1, tile]
+        for tile in range(3):
+            chunks[d, bases[0] + tile] = middle[d - 1, tile]
+            chunks[d, bases[1] + tile] = middle[d - 1, 3 + tile]
     outer = []
     for tile in range(5):
         both = jnp.where(lane % 4 < 2, left[tile], right[tile])
@@ -189,8 +202,9 @@
     for group in range(2):
         for tile in range(3):
             held = [jnp.zeros((8, 128), F32)] * 2
+            place, shift = (lane + 32 * group) % 128, 96 * group
             for _, _, slot, i, z in [n for n in NEAR if n[:2] == (group, tile)]:
-                main = p1[i, z] if i < 19 else codes[z]
+                main = p1[i, z] if i < 19 else codes[z].astype(F32)
                 step = velocities[i][1] if i < 19 else 0
                 first = last = main
                 if step == 1:
@@ -200,10 +214,10 @@
                 else:
                     first = jnp.where(lane == 127, roll(beside[i], 126 - 4 * z, 1), main)
                     last = jnp.where(lane == 0, roll(beside[i], -(4 * z + 2), 1), main)
-                held[0] = jnp.where(lane < 18 * slot, held[0], roll(first, 18 * slot + 1, 1))
-                held[1] = jnp.where(lane < 18 * slot, held[1], roll(last, 18 * slot - 111, 1))
-            chunks[0, group * 3 + tile] = held[0]
-            chunks[7, group * 3 + tile] = held[1]
+                held[0] = jnp.where(place < 18 * slot, held[0], roll(first, 18 * slot + 1 + shift, 1))
+                held[1] = jnp.where(place < 18 * slot, held[1], roll(last, 18 * slot - 111 + shift, 1))
+            chunks[0, bases[group] + tile] = held[0]
+            chunks[7, bases[group] + tile] = held[1]
 
 
 def cross(outgoing, lane, shift_a, shift_b, frac_a, frac_b):
@@ -218,25 +232,30 @@
     return jnp.where(low, roll(mixed, 32, 1), roll(mixed, -32, 1))
 
 
-def spread_kernel(offsets, fractions, own, work):
+def spread_kernel(own, work):
     lane8 = lanes()
+    upper, lower = set_bases()
     for item in range(20):
         tile, slot = divmod(item, 7)
+        to = (64 - 18 * slot) % 128
+        mine = (lane8 + to) % 128 >= 64
         for b in range(8):
-            value = jnp.where(
-                lane8 < 64,
-                roll(own[b, 3 + tile], 32 - 18 * slot, 1),
-                roll(own[b, tile], 64 - 18 * slot, 1),
-            )
-            work[item, 8 * b : 8 * b + 8, :] = value
-
-
-def plane_kernel(offsets, fractions, spread, near, far, ahead, behind, out, work, state):
+            value = jnp.where(mine, own[b, upper + tile], own[b, lower + tile])
+            work[item, 8 * b : 8 * b + 8, :] = roll(value, to, 1)
+
+
+def plane_kernel(offsets_far, fractions_far, spread, near, far, ahead, behind, out, work, state, offsets, fractions, sems):
+    copies = [
+        pltpu.make_async_copy(offsets_far, offsets, sems.at[0]),
+        pltpu.make_async_copy(fractions_far, fractions, sems.at[1]),
+    ]
+    for copy in copies:
+        copy.start()
     length = work.shape[1]
     lane8 = lanes()
     lane = lanes((length, 128))
     here = lax.axis_index("gz")
-    even = here % 2 == 0
+    odd = here % 2
     after = (here + 1) % lax.axis_size("gz")
     me, peers = lax.axis_index("gx"), lax.axis_size("gx")
     for tile in range(4):
@@ -253,16 +272,14 @@
 
     for item in range(20):
         tile, slot = divmod(item, 7)
+        to = (-18 * slot) % 128
+        paired = (lane8 + to + 64 * (1 - odd)) % 128 < 64
         for b in range(8):
             at = slice(8 * b, 8 * b + 8)
-            below = jnp.where(even, far[b, tile], near[b, tile])
-            above = jnp.where(even, near[b, tile], far[b, tile])
-            moved = jnp.where(
-                lane8 < 64,
-                roll(below, -18 * slot, 1),
-                roll(above, 96 - 18 * slot, 1),
-            )
-            work[item, at, :] = jnp.where((lane8 >= 32) & (lane8 < 96), spread[item, at, :], moved)
+            value = roll(jnp.where(paired, near[b, tile], far[b, tile]), to, 1)
+            work[item, at, :] = jnp.where((lane8 >= 32) & (lane8 < 96), spread[item, at, :], value)
+    for copy in copies:
+        copy.wait()
     for j in range(5):
         step_x = velocities[rising[j]][0]
         state[sinking[j]] = roll(cross(work[j], lane, *params(0)), step_x, 0)
@@ -286,16 +303,17 @@
         if crossing is not None:
             value = cross(value, lane, *params(1))
         work[n] = roll(value, velocities[i][0], 0)
+    part = lane8 // 16
     for b in range(8):
         for tile in range(5):
             packed = jnp.zeros((8, 128), F32)
-            for slot in range(8):
-                n = tile * 8 + slot
-                if n >= 38:
+            for k in range(4):
+                n = tile * 4 + k
+                if n >= 19:
                     break
-                group, q = (n, 2) if n < 19 else (n - 19, 1)
-                moved = roll(work[group, 8 * b : 8 * b + 8, :], 16 * slot - 32 * q - 1, 1)
-                packed = jnp.where(lane8 < 16 * slot, packed, moved)
+                slot = 4 * (k // 2) + k % 2
+                moved = roll(work[n, 8 * b : 8 * b + 8, :], 16 * slot - 33, 1)
+                packed = jnp.where((part == slot) | (part == slot + 2), moved, packed)
             out[b, tile] = packed
 
 
@@ -349,7 +367,7 @@
             source = z - velocities[i][2]
             value = mended(p1[i, source], post_side[i], velocities[i][1], source)
             f.append(moved_x(value, i, z, rows_behind, rows_ahead, 6, row))
-        post = collide(f, codes[z] * (1.0 / LEVELS))
+        post = collide(f, codes[z].astype(F32) * (1.0 / LEVELS))
         for i in range(19):
             step = velocities[i][1]
             value = mended(roll(post[i], step, 1), beside[i], step, z)
@@ -376,8 +394,8 @@
     target = []
     for group in range(2):
         z, inner = (7, 6) if group == 0 else (0, 1)
-        inward, outward = (sinking, rising) if group == 0 else (rising, sinking)
-        target += [(i, z) for i in level] + [(i, inner) for i in inward] + [(i, z) for i in inward]
+        inward = sinking if group == 0 else rising
+        target.append([(i, z) for i in level] + [(i, inner) for i in inward] + [(i, z) for i in inward])
     part = lane // 16
     for tile in range(5):
         held = [planes[h, tile] for h in range(8)]
@@ -389,9 +407,9 @@
                     held[h] = jnp.where(fixed, lo, roll(hi, 16 * k, 1))
                     held[h | k] = jnp.where(fixed, roll(lo, -16 * k, 1), hi)
         for slot in range(8):
-            n = tile * 8 + slot
-            if n < 38:
-                i, z = target[n]
+            n = tile * 4 + 2 * (slot // 4) + slot % 2
+            if n < 19:
+                i, z = target[0 if slot % 4 >= 2 else 1][n]
                 held_out[i, z] = held[slot] * weight_inverse[i]
     copies = []
     for i in range(19):
@@ -400,28 +418,26 @@
             if 1 <= source <= 6:
                 value = moved_x(p2[i, source - 1], i, source, rows_behind, rows_ahead, 5, row)
                 held_out[i, z] = value * weight_inverse[i]
-        copies.append(pltpu.make_async_copy(held_out.at[i], out.at[i], sems.at[i]))
-        copies[i].start()
+        if i % 5 == 4 or i == 18:
+            start = i - i % 5
+            part = pl.ds(start, i + 1 - start)
+            copies.append(pltpu.make_async_copy(held_out.at[part], out.at[part], sems.at[i // 5]))
+            copies[-1].start()
     for copy in copies:
         copy.wait()
 
 
-def run(kernel, outs, args, scalars=0, scratch=(), far_in=False, far_out=False, sems=0):
+def run(kernel, outs, args, scratch=(), words=(), far_in=0, far_out=False, sems=0):
     near = pl.BlockSpec(memory_space=pltpu.VMEM)
     away = pl.BlockSpec(memory_space=pltpu.HBM)
-    specs = [pl.BlockSpec(memory_space=pltpu.SMEM)] * scalars
-    specs += [away if far_in else near] * (len(args) - scalars)
-    shapes = [jax.ShapeDtypeStruct(s, F32) for s in outs]
-
-    def held(s):
-        return pltpu.VMEM(s.shape, s.dtype) if isinstance(s, jax.ShapeDtypeStruct) else pltpu.VMEM(s, F32)
-
     return pl.pallas_call(
         kernel,
-        out_shape=shapes,
-        in_specs=specs,
+        out_shape=[s if isinstance(s, jax.ShapeDtypeStruct) else jax.ShapeDtypeStruct(s, F32) for s in outs],
+        in_specs=[away] * far_in + [near] * (len(args) - far_in),
         out_specs=[away if far_out else near] * len(outs),
-        scratch_shapes=[held(s) for s in scratch] + [pltpu.SemaphoreType.DMA((sems,))] * (sems > 0),
+        scratch_shapes=[pltpu.VMEM(s, F32) for s in scratch]
+        + [pltpu.SMEM(s, jnp.int32) for s in words]
+        + [pltpu.SemaphoreType.DMA((sems,))] * (sems > 0),
         compiler_params=pltpu.CompilerParams(vmem_limit_bytes=32 * 1024 * 1024),
     )(*args)
 
@@ -435,27 +451,25 @@
 
 def swaps(own):
     peers = lax.axis_size("gz")
-    even = lax.axis_index("gz") % 2 == 0
-    upper, lower = own[:, 0:3], own[:, 3:6]
     pair = [(i, i ^ 1) for i in range(peers)]
     other = [(i, (i + peers - 1) % peers if i % 2 == 0 else (i + 1) % peers) for i in range(peers)]
-    far = lax.ppermute(jnp.where(even, lower, upper), "gz", other)
-    near = lax.ppermute(jnp.where(even, upper, lower), "gz", pair)
+    far = lax.ppermute(own[:, 3:6], "gz", other)
+    near = lax.ppermute(own[:, 0:3], "gz", pair)
     return near, far
 
 
 def body(pops, codes, offsets, fractions):
     tile = (8, 128)
-    far = [pltpu.with_memory_space_constraint(value, pltpu.HBM) for value in (pops, codes)]
-    (edges,) = run(
+    pops, codes, offsets, fractions = (
+        pltpu.with_memory_space_constraint(value, pltpu.HBM) for value in (pops, codes, offsets, fractions)
+    )
+    edges, pops, codes = run(
         edge_kernel,
-        [(5,) + tile],
-        far,
-        scratch=[(19, 8) + tile, jax.ShapeDtypeStruct((8,) + tile, jnp.int32)],
-        far_in=True,
-        sems=20,
-    )
-    codes = codes.astype(F32)
+        [(5,) + tile, (19, 8) + tile, jax.ShapeDtypeStruct((8,) + tile, jnp.int32)],
+        (pops, codes),
+        far_in=2,
+        sems=6,
+    )
     left, right = neighbours(edges, edges, "gy")
     p1, wrapped, middle, ahead, behind = run(
         main_kernel,
@@ -474,17 +488,19 @@
         [(19, 6) + tile, (4,) + tile, (4,) + tile],
         (p1, post_side, side, codes, own),
     )
-    (spread,) = run(spread_kernel, [(20, 64, 128)], (offsets, fractions, own), scalars=2)
+    (spread,) = run(spread_kernel, [(20, 64, 128)], (own,))
     (planes,) = run(
         plane_kernel,
         [(8, 9) + tile],
         (offsets, fractions, spread, near, far, ahead, behind),
-        scalars=2,
+        far_in=2,
         scratch=[(20, 64, 128), (19, 64, 128)],
+        words=[offsets.shape] * 2,
+        sems=2,
     )
     planes = lax.all_to_all(planes, "gx", 0, 0)
     (out,) = run(
-        last_kernel, [(19, 8) + tile], (p2, planes), scratch=[(19, 8) + tile], far_out=True, sems=19
+        last_kernel, [(19, 8) + tile], (p2, planes), scratch=[(19, 8) + tile], far_out=True, sems=4
     )
     return out
 

time: 67.2 us -> 64.8 us (0.964)
  blocking collectives: 15.1 us -> 34.9 us
  starting transfers between devices: 28.5 us -> 18.5 us
  waiting for transfers between devices: 13.9 us -> 4.89 us
  Pallas kernels: 8.95 us -> 6.07 us
    all_to_all x0 -> x1, blocking collectives: none -> 19.8 us  [body(): own = lax.all_to_all(chunks, 'gx', 0, 0)]
    all_to_all x1 -> x0, starting transfers between devices: 10 us -> none  [body(): own = lax.all_to_all(chunks, 'gx', 0, 0)]
    all_to_all x1 -> x0, waiting for transfers between devices: 9.97 us -> none  [body(): own = lax.all_to_all(chunks, 'gx', 0, 0)]
    pallas_call x7, Pallas kernels: 8.95 us -> 6.07 us  [run(): pl.pallas_call(kernel, out_shape=[s if isinstance(s, jax.ShapeDtypeStruct...]
    ppermute x2, waiting for transfers between devices: 0.01 us -> 0.88 us  [the longest x1 0.88 us: swaps(): far = lax.ppermute(own[:, 3:6], 'gz', other)]
  transfers between devices with their start and end apart: 5 -> 4, of which waited for: 2 -> 2; matrix products, arithmetic and copies ran while one was open for 0% -> 0% of each run, Pallas kernels for 3% -> 2%
where the time goes in v4:
time: 64.8 us; the launch traced here: 64.5 us
  blocking collectives  34.9 us (54%)
  starting transfers between devices  18.5 us (29%)
  Pallas kernels  6.07 us (9%)
  waiting for transfers between devices  4.89 us (8%)
    all_to_all x1, blocking collectives, body(): own = lax.all_to_all(chunks, 'gx', 0, 0)  19.8 us
    all_to_all x1, blocking collectives, body(): planes = lax.all_to_all(planes, 'gx', 0, 0)  15.2 us
    ppermute x1, starting transfers between devices, swaps(): far = lax.ppermute(own[:, 3:6], 'gz', other)  8.42 us
    ppermute x1, starting transfers between devices, neighbours(): lax.ppermute(value_down, axis, down)  6.23 us
    pallas_call x7, Pallas kernels, run(): pl.pallas_call(kernel, out_shape=[s if isinstance(s, jax.ShapeDtypeStruct...  6.07 us
    ppermute x1, waiting for transfers between devices, neighbours(): lax.ppermute(value_up, axis, up)  4 us
    ppermute x1, starting transfers between devices, swaps(): near = lax.ppermute(own[:, 0:3], 'gz', pair)  1.92 us
    ppermute x1, starting transfers between devices, neighbours(): lax.ppermute(value_up, axis, up)  1.92 us
  transfers between devices with their start and end apart: 4, of which 2 were waited for; matrix products, arithmetic and copies ran while one was open for 0% of the time, Pallas kernels for 2%

profile of v4, /device:TPU:1, one launch (start us, length us, event | category | flops | bytes accessed | tf_op | source)
XLA Modules:
  0.0 64.5 jit_solution(9004911434986216305)
XLA Ops:
  0.0 1.5 %shard_map.46 = (f32[5,8,128]{2,1,0:T(8,128)S(1)}, f32[19,8,8,128]{3,2,1,0:T(8,128)S(1)}, s32[8,8,128]{2,1,0:T(8,128)S(1)}) custom-call(f32[19,8,8,128]{3,2,1,0:T(8,128)} %pops_far.1, s32[8,8,128]{2,1,0:T(8,128)} %codes_far.1), custom_call_target="tpu_custom_call" | custom-call | tf_op jit(solution)/shard_map/pallas_call | solution.py:433
  1.5 6.2 %collective-permute-start.1 = (f32[5,8,128]{2,1,0:T(8,128)S(1)}, f32[5,8,128]{2,1,0:T(8,128)S(1)}, u32[]{:S(2)}, u32[]{:S(2)}) collective-permute-start(f32[5,8,128]{2,1,0:T(8,128)S(1)} %get-tuple-element.22), channel_id=1, source_target_pairs={{8,0},{16,8},{24,16},{32,24},{40,32},{48,40},{56,48},{0,56},{9,1},... | collective-permute-start | bytes 61448 | tf_op jit(solution)/shard_map/ppermute | solution.py:449
  7.8 1.9 %collective-permute-start = (f32[5,8,128]{2,1,0:T(8,128)S(1)}, f32[5,8,128]{2,1,0:T(8,128)S(1)}, u32[]{:S(2)}, u32[]{:S(2)}) collective-permute-start(f32[5,8,128]{2,1,0:T(8,128)S(1)} %get-tuple-element.22), channel_id=1, source_target_pairs={{0,8},{8,16},{16,24},{24,32},{32,40},{40,48},{48,56},{56,0},{1,9},... | collective-permute-start | bytes 61448 | tf_op jit(solution)/shard_map/ppermute | solution.py:449
  9.7 0.7 %shard_map.47 = (f32[19,8,8,128]{3,2,1,0:T(8,128)S(1)}, f32[10,8,128]{2,1,0:T(8,128)S(1)}, f32[6,6,8,128]{3,2,1,0:T(8,128)S(1)}, f32[4,8,128]{2,1,0:T(8,128)S(1)}, f32[4,8,128]{2,1,0:T(8,128)S(1)}) custom-call(f32[19,8,8,128]{3,2,1,0:T(8,128)S(1)} %get-tuple-element.19.pops, s32[8,8,128]{2,1,0:T(8,128)S(1)} %get-tuple-element.20.codes), custom_call_target="tpu_custom_call" | custom-call | tf_op jit(solution)/shard_map/pallas_call | solution.py:433
  10.4 0.0 collective-permute-done.1.right
  10.4 4.0 %collective-permute-done.left = f32[5,8,128]{2,1,0:T(8,128)S(1)} collective-permute-done((f32[5,8,128]{2,1,0:T(8,128)S(1)}, f32[5,8,128]{2,1,0:T(8,128)S(1)}, u32[]{:S(2)}, u32[]{:S(2)}) %collective-permute-start) | collective-permute-done | bytes 20512 | tf_op jit(solution)/shard_map/ppermute | solution.py:449
  14.4 0.3 shard_map.48
  14.8 19.8 %all_to_all.10.own = f32[8,10,8,128]{3,2,1,0:T(8,128)S(1)} all-to-all(f32[8,10,8,128]{3,2,1,0:T(8,128)S(1)} %get-tuple-element.29), channel_id=1, replica_groups=mesh['gx'=8,'gy'=8,'gz'=8] {'gx'}, dimensions={0} | all-to-all | bytes 655360 | tf_op jit(solution)/shard_map/all_to_all | solution.py:484
  34.5 8.4 %collective-permute-start.3 = (f32[8,3,8,128]{3,2,1,0:T(8,128)S(1)}, f32[8,3,8,128]{3,2,1,0:T(8,128)S(1)}, u32[]{:S(2)}, u32[]{:S(2)}) collective-permute-start(f32[8,3,8,128]{3,2,1,0:T(8,128)S(1)} %get-tuple-element.33), channel_id=1, source_target_pairs={{0,7},{1,2},{2,1},{3,4},{4,3},{5,6},{6,5},{7,0},{8,15},{9,10},{10,... | collective-permute-start | bytes 294920 | tf_op jit(solution)/shard_map/ppermute | solution.py:456
  43.0 1.9 %collective-permute-start.2 = (f32[8,3,8,128]{3,2,1,0:T(8,128)S(1)}, f32[8,3,8,128]{3,2,1,0:T(8,128)S(1)}, u32[]{:S(2)}, u32[]{:S(2)}) collective-permute-start(f32[8,3,8,128]{3,2,1,0:T(8,128)S(1)} %get-tuple-element.34), channel_id=1, source_target_pairs={{0,1},{1,0},{2,3},{3,2},{4,5},{5,4},{6,7},{7,6},{8,9},{9,8},{10,11... | collective-permute-start | bytes 294920 | tf_op jit(solution)/shard_map/ppermute | solution.py:457
  44.9 0.2 shard_map.50.spread
  45.1 0.5 shard_map.49
  45.6 0.9 %collective-permute-done.3.far = f32[8,3,8,128]{3,2,1,0:T(8,128)S(1)} collective-permute-done((f32[8,3,8,128]{3,2,1,0:T(8,128)S(1)}, f32[8,3,8,128]{3,2,1,0:T(8,128)S(1)}, u32[]{:S(2)}, u32[]{:S(2)}) %collective-permute-start.3) | collective-permute-done | bytes 98336 | tf_op jit(solution)/shard_map/ppermute | solution.py:456
  46.5 0.0 collective-permute-done.2.near
  46.5 1.7 %shard_map.51 = f32[8,9,8,128]{3,2,1,0:T(8,128)S(1)} custom-call(s32[2,8]{1,0:T(2,128)} %offsets_far.1, s32[2,8]{1,0:T(2,128)} %fractions_far.1, f32[20,64,128]{2,1,0:T(8,128)S(1)} %shard_map.50.spread, f32[8,3,8,128]{3,2,1,0:T(8,128)S(1)} %collective-permute-done.2.near, f32[8,3,8,128]{3,2,1,0:T(8,128)S(1)} %collective-permute-done.3.far, ...), custom_call_target="tpu_custom_call" | custom-call | tf_op jit(solution)/shard_map/pallas_call | solution.py:433
  48.2 15.2 %all_to_all.11.planes = f32[8,9,8,128]{3,2,1,0:T(8,128)S(1)} all-to-all(f32[8,9,8,128]{3,2,1,0:T(8,128)S(1)} %shard_map.51), channel_id=1, replica_groups=mesh['gx'=8,'gy'=8,'gz'=8] {'gx'}, dimensions={0} | all-to-all | bytes 589824 | tf_op jit(solution)/shard_map/all_to_all | solution.py:501
  63.4 1.1 %shard_map.52 = f32[19,8,8,128]{3,2,1,0:T(8,128)} custom-call(f32[19,6,8,128]{3,2,1,0:T(8,128)S(1)} %get-tuple-element.30.p2, f32[8,9,8,128]{3,2,1,0:T(8,128)S(1)} %all_to_all.11.planes), custom_call_target="tpu_custom_call" | custom-call | tf_op jit(solution)/shard_map/pallas_call | solution.py:433
  (1 shorter events, 0.0 us)
Async XLA Ops:
  1.5 8.9 %collective-permute-start.1 = (f32[5,8,128]{2,1,0:T(8,128)S(1)}, f32[5,8,128]{2,1,0:T(8,128)S(1)}, u32[]{:S(2)}, u32[]{:S(2)}) collective-permute-start(f32[5,8,128]{2,1,0:T(8,128)S(1)} %get-tuple-element.22), channel_id=1, source_target_pairs={{8,0},{16,8},{24,16},{32,24},{40,32},{48,40},{56,48},{0,56},{9,1},... | collective-permute-start | bytes 61448 | tf_op jit(solution)/shard_map/ppermute | solution.py:449
  7.8 6.6 %collective-permute-start = (f32[5,8,128]{2,1,0:T(8,128)S(1)}, f32[5,8,128]{2,1,0:T(8,128)S(1)}, u32[]{:S(2)}, u32[]{:S(2)}) collective-permute-start(f32[5,8,128]{2,1,0:T(8,128)S(1)} %get-tuple-element.22), channel_id=1, source_target_pairs={{0,8},{8,16},{16,24},{24,32},{32,40},{40,48},{48,56},{56,0},{1,9},... | collective-permute-start | bytes 61448 | tf_op jit(solution)/shard_map/ppermute | solution.py:449
  34.5 11.9 %collective-permute-start.3 = (f32[8,3,8,128]{3,2,1,0:T(8,128)S(1)}, f32[8,3,8,128]{3,2,1,0:T(8,128)S(1)}, u32[]{:S(2)}, u32[]{:S(2)}) collective-permute-start(f32[8,3,8,128]{3,2,1,0:T(8,128)S(1)} %get-tuple-element.33), channel_id=1, source_target_pairs={{0,7},{1,2},{2,1},{3,4},{4,3},{5,6},{6,5},{7,0},{8,15},{9,10},{10,... | collective-permute-start | bytes 294920 | tf_op jit(solution)/shard_map/ppermute | solution.py:456
  43.0 3.5 %collective-permute-start.2 = (f32[8,3,8,128]{3,2,1,0:T(8,128)S(1)}, f32[8,3,8,128]{3,2,1,0:T(8,128)S(1)}, u32[]{:S(2)}, u32[]{:S(2)}) collective-permute-start(f32[8,3,8,128]{3,2,1,0:T(8,128)S(1)} %get-tuple-element.34), channel_id=1, source_target_pairs={{0,1},{1,0},{2,3},{3,2},{4,5},{5,4},{6,7},{7,6},{8,9},{9,8},{10,11... | collective-permute-start | bytes 294920 | tf_op jit(solution)/shard_map/ppermute | solution.py:457

commit v5 on v4

--- a/solution.py
+++ b/solution.py
@@ -157,7 +157,7 @@
                 chunks[d, group * 3 + tile] = held[d]
 
 
-def edge_kernel_2(left, right, p1, codes, wrapped, middle, ahead, behind, chunks, post_side, side):
+def edge_kernel_2(near, far, p1, codes, wrapped, middle, ahead, behind, chunks, post_side, side):
     lane = lanes()
     ends = (lane == 0) | (lane == 127)
     me, peers = lax.axis_index("gx"), lax.axis_size("gx")
@@ -171,8 +171,9 @@
             chunks[d, bases[0] + tile] = middle[d - 1, tile]
             chunks[d, bases[1] + tile] = middle[d - 1, 3 + tile]
     outer = []
+    paired = (lane // 2 + lax.axis_index("gy")) % 2 == 1
     for tile in range(5):
-        both = jnp.where(lane % 4 < 2, left[tile], right[tile])
+        both = jnp.where(paired, near[tile], far[tile])
         for slot in range(4):
             outer.append(roll(both, -32 * slot, 1))
     beside = collide([outer[i] * lattice_weights[i] for i in range(19)], outer[19] * (1.0 / LEVELS))
@@ -220,12 +221,15 @@
             chunks[7, bases[group] + tile] = held[1]
 
 
-def cross(outgoing, lane, shift_a, shift_b, frac_a, frac_b):
+def cross(outgoing, lane, shift_a, shift_b, frac_a, frac_b, outward=True):
     length = outgoing.shape[0]
     low = (lane // 32) % 2 == 1
-    up_a, down_a = roll(outgoing, shift_a, 0), roll(outgoing, (length - shift_a) % length, 0)
-    up_b, down_b = roll(outgoing, shift_b, 0), roll(outgoing, (length - shift_b) % length, 0)
-    near = jnp.where(lane < 64, jnp.where(low, down_a, up_a), jnp.where(low, down_b, up_b))
+    up_a, down_b = roll(outgoing, shift_a, 0), roll(outgoing, (length - shift_b) % length, 0)
+    if outward:
+        down_a, up_b = roll(outgoing, (length - shift_a) % length, 0), roll(outgoing, shift_b, 0)
+        near = jnp.where(lane < 64, jnp.where(low, down_a, up_a), jnp.where(low, down_b, up_b))
+    else:
+        near = jnp.where(lane < 64, up_a, down_b)
     far = jnp.where(low, roll(near, -1, 0), roll(near, 1, 0))
     share = jnp.where(lane < 64, frac_a, frac_b)
     mixed = (1.0 - share) * near + share * far
@@ -301,7 +305,7 @@
     for n, (i, crossing) in enumerate(final):
         value = state[i]
         if crossing is not None:
-            value = cross(value, lane, *params(1))
+            value = cross(value, lane, *params(1), outward=False)
         work[n] = roll(value, velocities[i][0], 0)
     part = lane8 // 16
     for b in range(8):
@@ -442,19 +446,12 @@
     )(*args)
 
 
-def neighbours(value_up, value_down, axis):
+def swaps(to_near, to_far, axis):
     peers = lax.axis_size(axis)
-    up = [(i, (i + 1) % peers) for i in range(peers)]
-    down = [(j, i) for i, j in up]
-    return lax.ppermute(value_up, axis, up), lax.ppermute(value_down, axis, down)
-
-
-def swaps(own):
-    peers = lax.axis_size("gz")
     pair = [(i, i ^ 1) for i in range(peers)]
     other = [(i, (i + peers - 1) % peers if i % 2 == 0 else (i + 1) % peers) for i in range(peers)]
-    far = lax.ppermute(own[:, 3:6], "gz", other)
-    near = lax.ppermute(own[:, 0:3], "gz", pair)
+    far = lax.ppermute(to_far, axis, other)
+    near = lax.ppermute(to_near, axis, pair)
     return near, far
 
 
@@ -470,7 +467,7 @@
         far_in=2,
         sems=6,
     )
-    left, right = neighbours(edges, edges, "gy")
+    near, far = swaps(edges, edges, "gy")
     p1, wrapped, middle, ahead, behind = run(
         main_kernel,
         [(19, 8) + tile, (10,) + tile, (6, 6) + tile, (4,) + tile, (4,) + tile],
@@ -479,10 +476,10 @@
     chunks, post_side, side = run(
         edge_kernel_2,
         [(8, 10) + tile, (20,) + tile, (20,) + tile],
-        (left, right, p1, codes, wrapped, middle, ahead, behind),
+        (near, far, p1, codes, wrapped, middle, ahead, behind),
     )
     own = lax.all_to_all(chunks, "gx", 0, 0)
-    near, far = swaps(own)
+    near, far = swaps(own[:, 0:3], own[:, 3:6], "gz")
     p2, ahead, behind = run(
         inner_kernel,
         [(19, 6) + tile, (4,) + tile, (4,) + tile],

time: 64.8 us -> 62.6 us (0.966)
  waiting for transfers between devices: 4.89 us -> 2.78 us
    ppermute x4, waiting for transfers between devices: 4.89 us -> 2.78 us  [the longest x2 1.9 us: swaps(): near = lax.ppermute(to_near, axis, pair)]
where the time goes in v5:
time: 62.6 us; the launch traced here: 62.3 us
  blocking collectives  34.9 us (56%)
  starting transfers between devices  18.5 us (30%)
  Pallas kernels  5.98 us (10%)
  waiting for transfers between devices  2.78 us (4%)
    all_to_all x1, blocking collectives, body(): own = lax.all_to_all(chunks, 'gx', 0, 0)  19.8 us
    all_to_all x1, blocking collectives, body(): planes = lax.all_to_all(planes, 'gx', 0, 0)  15.2 us
    ppermute x2, starting transfers between devices, swaps(): far = lax.ppermute(to_far, axis, other)  14.6 us
    pallas_call x7, Pallas kernels, run(): pl.pallas_call(kernel, out_shape=[s if isinstance(s, jax.ShapeDtypeStruct...  5.98 us
    ppermute x2, starting transfers between devices, swaps(): near = lax.ppermute(to_near, axis, pair)  3.84 us
    ppermute x2, waiting for transfers between devices, swaps(): near = lax.ppermute(to_near, axis, pair)  1.9 us
  transfers between devices with their start and end apart: 4, of which 2 were waited for; matrix products, arithmetic and copies ran while one was open for 0% of the time, Pallas kernels for 2%

profile of v5, /device:TPU:1, one launch (start us, length us, event | category | flops | bytes accessed | tf_op | source)
XLA Modules:
  0.0 62.3 jit_solution(3219790223374794799)
XLA Ops:
  0.0 1.5 %shard_map.46 = (f32[5,8,128]{2,1,0:T(8,128)S(1)}, f32[19,8,8,128]{3,2,1,0:T(8,128)S(1)}, s32[8,8,128]{2,1,0:T(8,128)S(1)}) custom-call(f32[19,8,8,128]{3,2,1,0:T(8,128)} %pops_far.1, s32[8,8,128]{2,1,0:T(8,128)} %codes_far.1), custom_call_target="tpu_custom_call" | custom-call | tf_op jit(solution)/shard_map/pallas_call | solution.py:437
  1.5 6.2 %collective-permute-start.1 = (f32[5,8,128]{2,1,0:T(8,128)S(1)}, f32[5,8,128]{2,1,0:T(8,128)S(1)}, u32[]{:S(2)}, u32[]{:S(2)}) collective-permute-start(f32[5,8,128]{2,1,0:T(8,128)S(1)} %get-tuple-element.22), channel_id=1, source_target_pairs={{0,56},{8,16},{16,8},{24,32},{32,24},{40,48},{48,40},{56,0},{1,57}... | collective-permute-start | bytes 61448 | tf_op jit(solution)/shard_map/ppermute | solution.py:453
  7.8 1.9 %collective-permute-start = (f32[5,8,128]{2,1,0:T(8,128)S(1)}, f32[5,8,128]{2,1,0:T(8,128)S(1)}, u32[]{:S(2)}, u32[]{:S(2)}) collective-permute-start(f32[5,8,128]{2,1,0:T(8,128)S(1)} %get-tuple-element.22), channel_id=1, source_target_pairs={{0,8},{8,0},{16,24},{24,16},{32,40},{40,32},{48,56},{56,48},{1,9},... | collective-permute-start | bytes 61448 | tf_op jit(solution)/shard_map/ppermute | solution.py:454
  9.7 0.7 %shard_map.47 = (f32[19,8,8,128]{3,2,1,0:T(8,128)S(1)}, f32[10,8,128]{2,1,0:T(8,128)S(1)}, f32[6,6,8,128]{3,2,1,0:T(8,128)S(1)}, f32[4,8,128]{2,1,0:T(8,128)S(1)}, f32[4,8,128]{2,1,0:T(8,128)S(1)}) custom-call(f32[19,8,8,128]{3,2,1,0:T(8,128)S(1)} %get-tuple-element.19.pops, s32[8,8,128]{2,1,0:T(8,128)S(1)} %get-tuple-element.20.codes), custom_call_target="tpu_custom_call" | custom-call | tf_op jit(solution)/shard_map/pallas_call | solution.py:437
  10.4 0.0 collective-permute-done.1.far
  10.4 1.9 %collective-permute-done.near = f32[5,8,128]{2,1,0:T(8,128)S(1)} collective-permute-done((f32[5,8,128]{2,1,0:T(8,128)S(1)}, f32[5,8,128]{2,1,0:T(8,128)S(1)}, u32[]{:S(2)}, u32[]{:S(2)}) %collective-permute-start) | collective-permute-done | bytes 20512 | tf_op jit(solution)/shard_map/ppermute | solution.py:454
  12.3 0.4 shard_map.48
  12.7 19.8 %all_to_all.10.own = f32[8,10,8,128]{3,2,1,0:T(8,128)S(1)} all-to-all(f32[8,10,8,128]{3,2,1,0:T(8,128)S(1)} %get-tuple-element.29), channel_id=1, replica_groups=mesh['gx'=8,'gy'=8,'gz'=8] {'gx'}, dimensions={0} | all-to-all | bytes 655360 | tf_op jit(solution)/shard_map/all_to_all | solution.py:481
  32.4 8.4 %collective-permute-start.3 = (f32[8,3,8,128]{3,2,1,0:T(8,128)S(1)}, f32[8,3,8,128]{3,2,1,0:T(8,128)S(1)}, u32[]{:S(2)}, u32[]{:S(2)}) collective-permute-start(f32[8,3,8,128]{3,2,1,0:T(8,128)S(1)} %get-tuple-element.33), channel_id=1, source_target_pairs={{0,7},{1,2},{2,1},{3,4},{4,3},{5,6},{6,5},{7,0},{8,15},{9,10},{10,... | collective-permute-start | bytes 294920 | tf_op jit(solution)/shard_map/ppermute | solution.py:453
  40.9 1.9 %collective-permute-start.2 = (f32[8,3,8,128]{3,2,1,0:T(8,128)S(1)}, f32[8,3,8,128]{3,2,1,0:T(8,128)S(1)}, u32[]{:S(2)}, u32[]{:S(2)}) collective-permute-start(f32[8,3,8,128]{3,2,1,0:T(8,128)S(1)} %get-tuple-element.34), channel_id=1, source_target_pairs={{0,1},{1,0},{2,3},{3,2},{4,5},{5,4},{6,7},{7,6},{8,9},{9,8},{10,11... | collective-permute-start | bytes 294920 | tf_op jit(solution)/shard_map/ppermute | solution.py:454
  42.8 0.2 shard_map.50.spread
  43.0 0.5 shard_map.49
  43.5 0.9 %collective-permute-done.3.far = f32[8,3,8,128]{3,2,1,0:T(8,128)S(1)} collective-permute-done((f32[8,3,8,128]{3,2,1,0:T(8,128)S(1)}, f32[8,3,8,128]{3,2,1,0:T(8,128)S(1)}, u32[]{:S(2)}, u32[]{:S(2)}) %collective-permute-start.3) | collective-permute-done | bytes 98336 | tf_op jit(solution)/shard_map/ppermute | solution.py:453
  44.4 0.0 collective-permute-done.2.near
  44.4 1.6 %shard_map.51 = f32[8,9,8,128]{3,2,1,0:T(8,128)S(1)} custom-call(s32[2,8]{1,0:T(2,128)} %offsets_far.1, s32[2,8]{1,0:T(2,128)} %fractions_far.1, f32[20,64,128]{2,1,0:T(8,128)S(1)} %shard_map.50.spread, f32[8,3,8,128]{3,2,1,0:T(8,128)S(1)} %collective-permute-done.2.near, f32[8,3,8,128]{3,2,1,0:T(8,128)S(1)} %collective-permute-done.3.far, ...), custom_call_target="tpu_custom_call" | custom-call | tf_op jit(solution)/shard_map/pallas_call | solution.py:437
  46.0 15.2 %all_to_all.11.planes = f32[8,9,8,128]{3,2,1,0:T(8,128)S(1)} all-to-all(f32[8,9,8,128]{3,2,1,0:T(8,128)S(1)} %shard_map.51), channel_id=1, replica_groups=mesh['gx'=8,'gy'=8,'gz'=8] {'gx'}, dimensions={0} | all-to-all | bytes 589824 | tf_op jit(solution)/shard_map/all_to_all | solution.py:498
  61.2 1.1 %shard_map.52 = f32[19,8,8,128]{3,2,1,0:T(8,128)} custom-call(f32[19,6,8,128]{3,2,1,0:T(8,128)S(1)} %get-tuple-element.30.p2, f32[8,9,8,128]{3,2,1,0:T(8,128)S(1)} %all_to_all.11.planes), custom_call_target="tpu_custom_call" | custom-call | tf_op jit(solution)/shard_map/pallas_call | solution.py:437
  (1 shorter events, 0.0 us)
Async XLA Ops:
  1.5 8.9 %collective-permute-start.1 = (f32[5,8,128]{2,1,0:T(8,128)S(1)}, f32[5,8,128]{2,1,0:T(8,128)S(1)}, u32[]{:S(2)}, u32[]{:S(2)}) collective-permute-start(f32[5,8,128]{2,1,0:T(8,128)S(1)} %get-tuple-element.22), channel_id=1, source_target_pairs={{0,56},{8,16},{16,8},{24,32},{32,24},{40,48},{48,40},{56,0},{1,57}... | collective-permute-start | bytes 61448 | tf_op jit(solution)/shard_map/ppermute | solution.py:453
  7.8 4.5 %collective-permute-start = (f32[5,8,128]{2,1,0:T(8,128)S(1)}, f32[5,8,128]{2,1,0:T(8,128)S(1)}, u32[]{:S(2)}, u32[]{:S(2)}) collective-permute-start(f32[5,8,128]{2,1,0:T(8,128)S(1)} %get-tuple-element.22), channel_id=1, source_target_pairs={{0,8},{8,0},{16,24},{24,16},{32,40},{40,32},{48,56},{56,48},{1,9},... | collective-permute-start | bytes 61448 | tf_op jit(solution)/shard_map/ppermute | solution.py:454
  32.4 11.9 %collective-permute-start.3 = (f32[8,3,8,128]{3,2,1,0:T(8,128)S(1)}, f32[8,3,8,128]{3,2,1,0:T(8,128)S(1)}, u32[]{:S(2)}, u32[]{:S(2)}) collective-permute-start(f32[8,3,8,128]{3,2,1,0:T(8,128)S(1)} %get-tuple-element.33), channel_id=1, source_target_pairs={{0,7},{1,2},{2,1},{3,4},{4,3},{5,6},{6,5},{7,0},{8,15},{9,10},{10,... | collective-permute-start | bytes 294920 | tf_op jit(solution)/shard_map/ppermute | solution.py:453
  40.9 3.5 %collective-permute-start.2 = (f32[8,3,8,128]{3,2,1,0:T(8,128)S(1)}, f32[8,3,8,128]{3,2,1,0:T(8,128)S(1)}, u32[]{:S(2)}, u32[]{:S(2)}) collective-permute-start(f32[8,3,8,128]{3,2,1,0:T(8,128)S(1)} %get-tuple-element.34), channel_id=1, source_target_pairs={{0,1},{1,0},{2,3},{3,2},{4,5},{5,4},{6,7},{7,6},{8,9},{9,8},{10,11... | collective-permute-start | bytes 294920 | tf_op jit(solution)/shard_map/ppermute | solution.py:454

commit v6 on v5

--- a/solution.py
+++ b/solution.py
@@ -81,34 +81,49 @@
     return post
 
 
-def edge_kernel(pops_far, codes_far, out, pops, codes, sems):
+def edge_kernel(pops_far, codes_far, offsets_far, fractions_far, out, pops, codes, params, offsets, fractions, sems):
     lane = lanes()
-    copies = []
-    for tile in range(5):
-        part = pl.ds(4 * tile, min(4, 19 - 4 * tile))
-        copies.append(pltpu.make_async_copy(pops_far.at[part], pops.at[part], sems.at[tile]))
-    copies.append(pltpu.make_async_copy(codes_far, codes, sems.at[5]))
+    copies = (
+        pltpu.make_async_copy(pops_far, pops, sems.at[0]),
+        pltpu.make_async_copy(codes_far, codes, sems.at[1]),
+        pltpu.make_async_copy(offsets_far, offsets, sems.at[2]),
+        pltpu.make_async_copy(fractions_far, fractions, sems.at[3]),
+    )
     for copy in copies:
         copy.start()
+    for copy in copies:
+        copy.wait()
     for tile in range(5):
-        copies[tile].wait()
         packed = jnp.zeros((8, 128), F32)
         for slot in range(4):
             item = tile * 4 + slot
-            if item == 19:
-                copies[5].wait()
             for z in range(8):
                 start = slot * 32 + z * 4
                 source = pops[item, z] if item < 19 else codes[z].astype(F32)
                 moved = roll(source, start + 2, 1)
                 packed = jnp.where(lane < start, packed, moved)
         out[tile] = packed
+    here = lax.axis_index("gz")
+    after = (here + 1) % lax.axis_size("gz")
+    length = 8 * lax.axis_size("gx")
+    row_lane = lanes((1, 128))
+    low = (row_lane // 32) % 2 == 1
+    for step in range(2):
+        shift = jnp.where(row_lane < 64, offsets[step, here], offsets[step, after])
+        shift = jnp.where(low, (length - shift) % length, shift)
+        params[step : step + 1, :] = shift.astype(F32)
+        share = jnp.where(row_lane < 64, fractions[step, here], fractions[step, after])
+        params[step + 2 : step + 3, :] = share.astype(F32) * (1.0 / FRAC_DEN)
 
 
 UPPER = [(i, 7) for i in rising] + [(i, 7) for i in level] + [(i, 6) for i in rising] + [(19, 7)]
 LOWER = [(i, 0) for i in sinking] + [(i, 0) for i in level] + [(i, 1) for i in sinking] + [(19, 0)]
 NEAR = [(group, tile, slot, i, z) for group, items in enumerate((UPPER, LOWER)) for tile in range(3) for slot, (i, z) in enumerate(items[7 * tile : 7 * tile + 7])]
-AHEAD_ROW, BEHIND_ROW = slice(7, 8), slice(0, 1)
+still = tuple(i for i in range(19) if velocities[i][0] == 0)
+ROWS = tuple(
+    [(i, edge) for i in members] + [(i, inner) for i in members] + [(i, edge) for i in still] + [(19, edge)]
+    for members, edge, inner in ((forward, 7, 6), (backward, 0, 1))
+)
 
 
 def set_bases():
@@ -116,12 +131,16 @@
     return 3 * odd, 3 - 3 * odd
 
 
-def row_place(j, z):
-    r = 6 * j + z - 1
-    return r // 8, slice(r % 8, r % 8 + 1)
-
-
-def main_kernel(pops, codes, p1, wrapped, chunks, ahead, behind):
+def put_rows(sides, i, z, value):
+    target = z + (velocities[i][2] if i < 19 else 0)
+    if 1 <= target <= 6:
+        for side in range(2):
+            for item, (member, x) in enumerate(ROWS[side]):
+                if member == i:
+                    sides[side, item, target : target + 1, :] = value[x : x + 1, :]
+
+
+def main_kernel(pops, codes, p1, wrapped, chunks, sides):
     lane = lanes()
     side = [jnp.zeros((8, 128), F32) for _ in range(19)]
     for z in range(8):
@@ -135,13 +154,8 @@
             elif step == -1:
                 side[i] = jnp.where(lane == 4 * z + 1, roll(value, 4 * z + 2, 1), side[i])
             p1[i, z] = value
-            target = z + velocities[i][2]
-            if 1 <= target <= 6 and i in forward:
-                tile, at = row_place(forward.index(i), target)
-                ahead[tile, at, :] = value[AHEAD_ROW, :]
-            if 1 <= target <= 6 and i in backward:
-                tile, at = row_place(backward.index(i), target)
-                behind[tile, at, :] = value[BEHIND_ROW, :]
+            put_rows(sides, i, z, value)
+        put_rows(sides, 19, z, codes[z].astype(F32))
     for k, i in enumerate(sideways):
         wrapped[k] = side[i]
     for group in range(2):
@@ -157,14 +171,9 @@
                 chunks[d, group * 3 + tile] = held[d]
 
 
-def edge_kernel_2(near, far, p1, codes, wrapped, middle, ahead, behind, chunks, post_side, side):
-    lane = lanes()
+def edge_kernel_2(near, far, p1, codes, wrapped, middle, sides, chunks, post_side, side, rows_near, rows_far):
+    lane, row = lanes(), rows()
     ends = (lane == 0) | (lane == 127)
-    me, peers = lax.axis_index("gx"), lax.axis_size("gx")
-    after, before = (me + 1) % peers, (me + peers - 1) % peers
-    for tile in range(4):
-        chunks[after, 6 + tile] = ahead[tile]
-        chunks[before, 6 + tile] = behind[tile]
     bases = set_bases()
     for d in range(1, 7):
         for tile in range(3):
@@ -185,21 +194,21 @@
     for i in range(20):
         side[i] = shifted[i]
         post_side[i] = beside[i]
-    row_lane = lanes((1, 128))
-    for members, to, source, at_x in ((forward, after, ahead, AHEAD_ROW), (backward, before, behind, BEHIND_ROW)):
-        extra = [jnp.zeros((1, 128), F32)] * 2
-        for j, i in enumerate(members):
-            extra[j // 4] = jnp.where(row_lane // 32 == j % 4, roll(shifted[i][at_x, :], 32 * (j % 4), 1), extra[j // 4])
-            step = velocities[i][1]
-            if step == 0:
-                continue
-            for z in range(1, 7):
-                tile, at = row_place(j, z)
-                lane_at, start = (0, 4 * z + 1) if step == 1 else (127, 4 * z + 2)
-                fixed = roll(beside[i][at_x, :], lane_at - start, 1)
-                chunks[to, 6 + tile, at, :] = jnp.where(row_lane == lane_at, fixed, source[tile, at, :])
-        chunks[to, 9, 6:7, :] = extra[0]
-        chunks[to, 9, 7:8, :] = extra[1]
+    even = lax.axis_index("gx") % 2 == 0
+    for item in range(20):
+        sent = []
+        for k in range(2):
+            i, x = ROWS[k][item]
+            step_y, step_z = velocities[i][1:] if i < 19 else (0, 0)
+            value = sides[k, item]
+            if step_y:
+                at, start = (0, 1) if step_y == 1 else (127, 2)
+                spot = jnp.broadcast_to(beside[i][x : x + 1, :], (8, 128))
+                spot = jnp.where(lane == 4 * (row - step_z) + start, spot, 0.0)
+                value = jnp.where(lane == at, jnp.sum(spot, axis=1, keepdims=True), value)
+            sent.append(jnp.where(row == 0, jnp.broadcast_to(shifted[i][x : x + 1, :], (8, 128)), value))
+        rows_near[item] = jnp.where(even, sent[0], sent[1])
+        rows_far[item] = jnp.where(even, sent[1], sent[0])
     for group in range(2):
         for tile in range(3):
             held = [jnp.zeros((8, 128), F32)] * 2
@@ -221,17 +230,15 @@
             chunks[7, bases[group] + tile] = held[1]
 
 
-def cross(outgoing, lane, shift_a, shift_b, frac_a, frac_b, outward=True):
+def cross(outgoing, lane, shift, share):
     length = outgoing.shape[0]
     low = (lane // 32) % 2 == 1
-    up_a, down_b = roll(outgoing, shift_a, 0), roll(outgoing, (length - shift_b) % length, 0)
-    if outward:
-        down_a, up_b = roll(outgoing, (length - shift_a) % length, 0), roll(outgoing, shift_b, 0)
-        near = jnp.where(lane < 64, jnp.where(low, down_a, up_a), jnp.where(low, down_b, up_b))
-    else:
-        near = jnp.where(lane < 64, up_a, down_b)
+    near = outgoing
+    bit = 1
+    while bit < length:
+        near = jnp.where((shift & bit) != 0, roll(near, bit, 0), near)
+        bit *= 2
     far = jnp.where(low, roll(near, -1, 0), roll(near, 1, 0))
-    share = jnp.where(lane < 64, frac_a, frac_b)
     mixed = (1.0 - share) * near + share * far
     return jnp.where(low, roll(mixed, 32, 1), roll(mixed, -32, 1))
 
@@ -248,31 +255,14 @@
             work[item, 8 * b : 8 * b + 8, :] = roll(value, to, 1)
 
 
-def plane_kernel(offsets_far, fractions_far, spread, near, far, ahead, behind, out, work, state, offsets, fractions, sems):
-    copies = [
-        pltpu.make_async_copy(offsets_far, offsets, sems.at[0]),
-        pltpu.make_async_copy(fractions_far, fractions, sems.at[1]),
-    ]
-    for copy in copies:
-        copy.start()
+def plane_kernel(params, spread, near, far, out, work, state):
     length = work.shape[1]
     lane8 = lanes()
     lane = lanes((length, 128))
-    here = lax.axis_index("gz")
-    odd = here % 2
-    after = (here + 1) % lax.axis_size("gz")
-    me, peers = lax.axis_index("gx"), lax.axis_size("gx")
-    for tile in range(4):
-        out[(me + 1) % peers, 5 + tile] = ahead[tile]
-        out[(me + peers - 1) % peers, 5 + tile] = behind[tile]
-
-    def params(step):
-        return (
-            offsets[step, here],
-            offsets[step, after],
-            fractions[step, here].astype(F32) * (1.0 / FRAC_DEN),
-            fractions[step, after].astype(F32) * (1.0 / FRAC_DEN),
-        )
+    odd = lax.axis_index("gz") % 2
+
+    def moves(step):
+        return params[step : step + 1, :].astype(jnp.int32), params[step + 2 : step + 3, :]
 
     for item in range(20):
         tile, slot = divmod(item, 7)
@@ -282,11 +272,9 @@
             at = slice(8 * b, 8 * b + 8)
             value = roll(jnp.where(paired, near[b, tile], far[b, tile]), to, 1)
             work[item, at, :] = jnp.where((lane8 >= 32) & (lane8 < 96), spread[item, at, :], value)
-    for copy in copies:
-        copy.wait()
     for j in range(5):
         step_x = velocities[rising[j]][0]
-        state[sinking[j]] = roll(cross(work[j], lane, *params(0)), step_x, 0)
+        state[sinking[j]] = roll(cross(work[j], lane, *moves(0)), step_x, 0)
         state[rising[j]] = roll(work[14 + j], step_x, 0)
     for k, i in enumerate(level):
         state[i] = roll(work[5 + k], velocities[i][0], 0)
@@ -305,7 +293,7 @@
     for n, (i, crossing) in enumerate(final):
         value = state[i]
         if crossing is not None:
-            value = cross(value, lane, *params(1), outward=False)
+            value = cross(value, lane, *moves(1))
         work[n] = roll(value, velocities[i][0], 0)
     part = lane8 // 16
     for b in range(8):
@@ -321,42 +309,59 @@
             out[b, tile] = packed
 
 
-def moved_x(value, i, z, rows_behind, rows_ahead, first_tile, row):
+def moved_x(value, i, z, behind, ahead, row):
     if i in forward:
-        tile, at = row_place(forward.index(i), z)
-        source, to = rows_behind(first_tile + tile, at), 0
+        source, to = behind(forward.index(i)), 0
     elif i in backward:
-        tile, at = row_place(backward.index(i), z)
-        source, to = rows_ahead(first_tile + tile, at), 7
+        source, to = ahead(backward.index(i)), 7
     else:
         return value
-    return jnp.where(row == to, jnp.broadcast_to(source, (8, 128)), roll(value, velocities[i][0], 0))
-
-
-def inner_kernel(p1, post_side, side, codes, own, p2, ahead, behind):
+    return jnp.where(row == to, jnp.broadcast_to(source[z : z + 1, :], (8, 128)), roll(value, velocities[i][0], 0))
+
+
+def inner_kernel(p1, post_side, side, codes, sent_near, sent_far, got_near, got_far, p2, ahead, behind):
     lane, row = lanes(), rows()
-    me, peers = lax.axis_index("gx"), lax.axis_size("gx")
-    after, before = (me + 1) % peers, (me + peers - 1) % peers
-
-    def rows_behind(tile, at):
-        return own[before, tile, at, :]
-
-    def rows_ahead(tile, at):
-        return own[after, tile, at, :]
-
-    f = []
+    even = lax.axis_index("gx") % 2 == 0
+    own = (
+        [jnp.where(even, sent_near[item], sent_far[item]) for item in range(5)],
+        [jnp.where(even, sent_far[item], sent_near[item]) for item in range(5)],
+    )
+    got = (
+        [jnp.where(even, got_far[item], got_near[item]) for item in range(20)],
+        [jnp.where(even, got_near[item], got_far[item]) for item in range(20)],
+    )
+
+    def entering(k):
+        f = [None] * 20
+        for j, i in enumerate((forward, backward)[k]):
+            f[i] = got[k][5 + j]
+        for j, i in enumerate((backward, forward)[k]):
+            f[i] = own[1 - k][j]
+        for j, i in enumerate(still + (19,)):
+            f[i] = got[k][10 + j]
+        return f
+
+    lines = [entering(k) for k in range(2)]
+    f, corner = [], []
     for i in range(19):
-        value = side[i]
-        for members, get, to in ((forward, rows_behind, 0), (backward, rows_ahead, 7)):
-            if i in members:
-                j = members.index(i)
-                source = roll(get(9, slice(6 + j // 4, 7 + j // 4)), -32 * (j % 4), 1)
-                value = jnp.where(row == to, jnp.broadcast_to(source, (8, 128)), roll(value, velocities[i][0], 0))
+        value = moved_x(side[i], i, 0, lambda j: got[0][j], lambda j: got[1][j], row)
         f.append(roll(value, 4 * velocities[i][2], 1))
+        ends = [jnp.broadcast_to(lines[k][i][0:1, :], (8, 128)) for k in range(2)]
+        corner.append(roll(jnp.where(row == 0, ends[0], ends[1]), 4 * velocities[i][2], 1))
     beside = collide(f, side[19] * (1.0 / LEVELS))
-    for j in range(2):
-        ahead[3, 6 + j : 7 + j, :] = jnp.zeros((1, 128), F32)
-        behind[3, 6 + j : 7 + j, :] = jnp.zeros((1, 128), F32)
+    ends = [jnp.broadcast_to(lines[k][19][0:1, :], (8, 128)) for k in range(2)]
+    corner = collide(corner, jnp.where(row == 0, ends[0], ends[1]) * (1.0 / LEVELS))
+    for k, (members, out) in enumerate(((forward, ahead), (backward, behind))):
+        post = collide(lines[k][:19], lines[k][19] * (1.0 / LEVELS))
+        for j, i in enumerate(members):
+            step = velocities[i][1]
+            value = roll(post[i], step, 1)
+            if step:
+                at, start = (0, 1) if step == 1 else (127, 2)
+                spot = jnp.broadcast_to(corner[i][7 * k : 7 * k + 1, :], (8, 128))
+                spot = jnp.where(lane == 4 * row + start, spot, 0.0)
+                value = jnp.where(lane == at, jnp.sum(spot, axis=1, keepdims=True), value)
+            out[j] = value
 
     def mended(value, edge, step, z):
         if step == 1:
@@ -370,31 +375,15 @@
         for i in range(19):
             source = z - velocities[i][2]
             value = mended(p1[i, source], post_side[i], velocities[i][1], source)
-            f.append(moved_x(value, i, z, rows_behind, rows_ahead, 6, row))
+            f.append(moved_x(value, i, z, lambda j: got[0][j], lambda j: got[1][j], row))
         post = collide(f, codes[z].astype(F32) * (1.0 / LEVELS))
         for i in range(19):
             step = velocities[i][1]
-            value = mended(roll(post[i], step, 1), beside[i], step, z)
-            p2[i, z - 1] = value
-            if i in forward:
-                tile, at = row_place(forward.index(i), z)
-                ahead[tile, at, :] = value[AHEAD_ROW, :]
-            if i in backward:
-                tile, at = row_place(backward.index(i), z)
-                behind[tile, at, :] = value[BEHIND_ROW, :]
-
-
-def last_kernel(p2, planes, out, held_out, sems):
+            p2[i, z - 1] = mended(roll(post[i], step, 1), beside[i], step, z)
+
+
+def last_kernel(p2, ahead, behind, planes, out, held_out, sems):
     lane, row = lanes(), rows()
-    me, peers = lax.axis_index("gx"), lax.axis_size("gx")
-    after, before = (me + 1) % peers, (me + peers - 1) % peers
-
-    def rows_behind(tile, at):
-        return planes[before, tile, at, :]
-
-    def rows_ahead(tile, at):
-        return planes[after, tile, at, :]
-
     target = []
     for group in range(2):
         z, inner = (7, 6) if group == 0 else (0, 1)
@@ -420,7 +409,7 @@
         for z in range(8):
             source = z - velocities[i][2]
             if 1 <= source <= 6:
-                value = moved_x(p2[i, source - 1], i, source, rows_behind, rows_ahead, 5, row)
+                value = moved_x(p2[i, source - 1], i, source, lambda j: ahead[j], lambda j: behind[j], row)
                 held_out[i, z] = value * weight_inverse[i]
         if i % 5 == 4 or i == 18:
             start = i - i % 5
@@ -460,44 +449,43 @@
     pops, codes, offsets, fractions = (
         pltpu.with_memory_space_constraint(value, pltpu.HBM) for value in (pops, codes, offsets, fractions)
     )
-    edges, pops, codes = run(
+    edges, pops, codes, params = run(
         edge_kernel,
-        [(5,) + tile, (19, 8) + tile, jax.ShapeDtypeStruct((8,) + tile, jnp.int32)],
+        [(5,) + tile, (19, 8) + tile, jax.ShapeDtypeStruct((8,) + tile, jnp.int32), tile],
+        (pops, codes, offsets, fractions),
+        far_in=4,
+        words=[offsets.shape] * 2,
+        sems=4,
+    )
+    near, far = swaps(edges, edges, "gy")
+    p1, wrapped, middle, sides = run(
+        main_kernel,
+        [(19, 8) + tile, (10,) + tile, (6, 6) + tile, (2, 20) + tile],
         (pops, codes),
-        far_in=2,
-        sems=6,
-    )
-    near, far = swaps(edges, edges, "gy")
-    p1, wrapped, middle, ahead, behind = run(
-        main_kernel,
-        [(19, 8) + tile, (10,) + tile, (6, 6) + tile, (4,) + tile, (4,) + tile],
-        (pops, codes),
-    )
-    chunks, post_side, side = run(
+    )
+    chunks, post_side, side, sent_near, sent_far = run(
         edge_kernel_2,
-        [(8, 10) + tile, (20,) + tile, (20,) + tile],
-        (near, far, p1, codes, wrapped, middle, ahead, behind),
-    )
+        [(8, 6) + tile, (20,) + tile, (20,) + tile, (20,) + tile, (20,) + tile],
+        (near, far, p1, codes, wrapped, middle, sides),
+    )
+    got_near, got_far = swaps(sent_near, sent_far, "gx")
     own = lax.all_to_all(chunks, "gx", 0, 0)
     near, far = swaps(own[:, 0:3], own[:, 3:6], "gz")
+    (spread,) = run(spread_kernel, [(20, 64, 128)], (own,))
     p2, ahead, behind = run(
         inner_kernel,
-        [(19, 6) + tile, (4,) + tile, (4,) + tile],
-        (p1, post_side, side, codes, own),
-    )
-    (spread,) = run(spread_kernel, [(20, 64, 128)], (own,))
+        [(19, 6) + tile, (5,) + tile, (5,) + tile],
+        (p1, post_side, side, codes, sent_near, sent_far, got_near, got_far),
+    )
     (planes,) = run(
         plane_kernel,
-        [(8, 9) + tile],
-        (offsets, fractions, spread, near, far, ahead, behind),
-        far_in=2,
+        [(8, 5) + tile],
+        (params, spread, near, far),
         scratch=[(20, 64, 128), (19, 64, 128)],
-        words=[offsets.shape] * 2,
-        sems=2,
     )
     planes = lax.all_to_all(planes, "gx", 0, 0)
     (out,) = run(
-        last_kernel, [(19, 8) + tile], (p2, planes), scratch=[(19, 8) + tile], far_out=True, sems=4
+        last_kernel, [(19, 8) + tile], (p2, ahead, behind, planes), scratch=[(19, 8) + tile], far_out=True, sems=4
     )
     return out
 

time: 62.6 us -> 60.4 us (0.965)
  the two profiles are of different devices: /device:TPU:1 before, /device:TPU:40 now
where the time goes in v6:
time: 60.4 us; the launch traced here: 60 us
  starting transfers between devices  23.9 us (40%)
  blocking collectives  19.9 us (33%)
  waiting for transfers between devices  10.1 us (17%)
  Pallas kernels  5.99 us (10%)
    all_to_all x1, blocking collectives, body(): own = lax.all_to_all(chunks, 'gx', 0, 0)  19.9 us
    ppermute x3, starting transfers between devices, swaps(): far = lax.ppermute(to_far, axis, other)  12 us
    ppermute x3, starting transfers between devices, swaps(): near = lax.ppermute(to_near, axis, pair)  8.54 us
    ppermute x3, waiting for transfers between devices, swaps(): far = lax.ppermute(to_far, axis, other)  7.02 us
    pallas_call x7, Pallas kernels, run(): pl.pallas_call(kernel, out_shape=[s if isinstance(s, jax.ShapeDtypeStruct...  5.99 us
    all_to_all x1, starting transfers between devices, body(): planes = lax.all_to_all(planes, 'gx', 0, 0)  3.38 us
    ppermute x3, waiting for transfers between devices, swaps(): near = lax.ppermute(to_near, axis, pair)  3.04 us
  transfers between devices with their start and end apart: 7, of which 3 were waited for; matrix products, arithmetic and copies ran while one was open for 0% of the time, Pallas kernels for 3%

profile of v6, /device:TPU:40, one launch (start us, length us, event | category | flops | bytes accessed | tf_op | source)
XLA Modules:
  0.0 60.0 jit_solution(8364923247334880575)
XLA Ops:
  0.0 1.4 %shard_map.46 = (f32[5,8,128]{2,1,0:T(8,128)S(1)}, f32[19,8,8,128]{3,2,1,0:T(8,128)S(1)}, s32[8,8,128]{2,1,0:T(8,128)S(1)}, f32[8,128]{1,0:T(8,128)S(1)}) custom-call(f32[19,8,8,128]{3,2,1,0:T(8,128)} %pops_far.1, s32[8,8,128]{2,1,0:T(8,128)} %codes_far.1, s32[2,8]{1,0:T(2,128)} %offsets_far.1, s32[2,8]{1,0:T(2,128)} %fractions_far.1), custom_call_target="tpu_custom_call" | custom-call | tf_op jit(solution)/shard_map/pallas_call | solution.py:426
  1.4 5.5 %collective-permute-start.1 = (f32[5,8,128]{2,1,0:T(8,128)S(1)}, f32[5,8,128]{2,1,0:T(8,128)S(1)}, u32[]{:S(2)}, u32[]{:S(2)}) collective-permute-start(f32[5,8,128]{2,1,0:T(8,128)S(1)} %get-tuple-element.24), channel_id=1, source_target_pairs={{0,56},{8,16},{16,8},{24,32},{32,24},{40,48},{48,40},{56,0},{1,57}... | collective-permute-start | bytes 61448 | tf_op jit(solution)/shard_map/ppermute | solution.py:442
  6.8 1.9 %collective-permute-start = (f32[5,8,128]{2,1,0:T(8,128)S(1)}, f32[5,8,128]{2,1,0:T(8,128)S(1)}, u32[]{:S(2)}, u32[]{:S(2)}) collective-permute-start(f32[5,8,128]{2,1,0:T(8,128)S(1)} %get-tuple-element.24), channel_id=1, source_target_pairs={{0,8},{8,0},{16,24},{24,16},{32,40},{40,32},{48,56},{56,48},{1,9},... | collective-permute-start | bytes 61448 | tf_op jit(solution)/shard_map/ppermute | solution.py:443
  8.8 0.7 %shard_map.47 = (f32[19,8,8,128]{3,2,1,0:T(8,128)S(1)}, f32[10,8,128]{2,1,0:T(8,128)S(1)}, f32[6,6,8,128]{3,2,1,0:T(8,128)S(1)}, f32[2,20,8,128]{3,2,1,0:T(8,128)S(1)}) custom-call(f32[19,8,8,128]{3,2,1,0:T(8,128)S(1)} %get-tuple-element.21.pops, s32[8,8,128]{2,1,0:T(8,128)S(1)} %get-tuple-element.22.codes), custom_call_target="tpu_custom_call" | custom-call | tf_op jit(solution)/shard_map/pallas_call | solution.py:426
  9.5 0.0 collective-permute-done.1.far
  9.5 3.0 %collective-permute-done.near = f32[5,8,128]{2,1,0:T(8,128)S(1)} collective-permute-done((f32[5,8,128]{2,1,0:T(8,128)S(1)}, f32[5,8,128]{2,1,0:T(8,128)S(1)}, u32[]{:S(2)}, u32[]{:S(2)}) %collective-permute-start) | collective-permute-done | bytes 20512 | tf_op jit(solution)/shard_map/ppermute | solution.py:443
  12.5 0.4 shard_map.48
  12.9 19.9 %all_to_all.10.own = f32[8,6,8,128]{3,2,1,0:T(8,128)S(1)} all-to-all(f32[8,6,8,128]{3,2,1,0:T(8,128)S(1)} %get-tuple-element.36), channel_id=1, replica_groups=mesh['gx'=8,'gy'=8,'gz'=8] {'gx'}, dimensions={0} | all-to-all | bytes 393216 | tf_op jit(solution)/shard_map/all_to_all | solution.py:472
  32.8 1.9 %collective-permute-start.5 = (f32[8,3,8,128]{3,2,1,0:T(8,128)S(1)}, f32[8,3,8,128]{3,2,1,0:T(8,128)S(1)}, u32[]{:S(2)}, u32[]{:S(2)}) collective-permute-start(f32[8,3,8,128]{3,2,1,0:T(8,128)S(1)} %get-tuple-element.37), channel_id=1, source_target_pairs={{0,7},{1,2},{2,1},{3,4},{4,3},{5,6},{6,5},{7,0},{8,15},{9,10},{10,... | collective-permute-start | bytes 294920 | tf_op jit(solution)/shard_map/ppermute | solution.py:442
  34.7 2.8 %collective-permute-start.4 = (f32[8,3,8,128]{3,2,1,0:T(8,128)S(1)}, f32[8,3,8,128]{3,2,1,0:T(8,128)S(1)}, u32[]{:S(2)}, u32[]{:S(2)}) collective-permute-start(f32[8,3,8,128]{3,2,1,0:T(8,128)S(1)} %get-tuple-element.38), channel_id=1, source_target_pairs={{0,1},{1,0},{2,3},{3,2},{4,5},{5,4},{6,7},{7,6},{8,9},{9,8},{10,11... | collective-permute-start | bytes 294920 | tf_op jit(solution)/shard_map/ppermute | solution.py:443
  37.5 0.2 shard_map.50.spread
  37.8 4.1 %collective-permute-done.5.far = f32[8,3,8,128]{3,2,1,0:T(8,128)S(1)} collective-permute-done((f32[8,3,8,128]{3,2,1,0:T(8,128)S(1)}, f32[8,3,8,128]{3,2,1,0:T(8,128)S(1)}, u32[]{:S(2)}, u32[]{:S(2)}) %collective-permute-start.5) | collective-permute-done | bytes 98336 | tf_op jit(solution)/shard_map/ppermute | solution.py:442
  41.9 0.0 collective-permute-done.4.near
  41.9 1.6 %shard_map.51 = f32[8,5,8,128]{3,2,1,0:T(8,128)} custom-call(f32[8,128]{1,0:T(8,128)S(1)} %get-tuple-element.35.params, f32[20,64,128]{2,1,0:T(8,128)S(1)} %shard_map.50.spread, f32[8,3,8,128]{3,2,1,0:T(8,128)S(1)} %collective-permute-done.4.near, f32[8,3,8,128]{3,2,1,0:T(8,128)S(1)} %collective-permute-done.5.far), custom_call_target="tpu_custom_call" | custom-call | tf_op jit(solution)/shard_map/pallas_call | solution.py:426
  43.5 3.4 %all-to-all-start.1 = ((f32[8,5,8,128]{3,2,1,0:T(8,128)}), f32[8,5,8,128]{3,2,1,0:T(8,128)S(1)}, u32[]{:S(2)}, u32[]{:S(2)}) async-start(f32[8,5,8,128]{3,2,1,0:T(8,128)} %shard_map.51), calls=%async_computation.1 | async-start | bytes 327680 | tf_op jit(solution)/shard_map/all_to_all | solution.py:486
  46.9 3.8 %collective-permute-start.2 = (f32[20,8,128]{2,1,0:T(8,128)S(1)}, f32[20,8,128]{2,1,0:T(8,128)S(1)}, u32[]{:S(2)}, u32[]{:S(2)}) collective-permute-start(f32[20,8,128]{2,1,0:T(8,128)S(1)} %get-tuple-element.30.sent_near), channel_id=1, source_target_pairs={{0,64},{64,0},{128,192},{192,128},{256,320},{320,256},{384,448},{4... | collective-permute-start | bytes 245768 | tf_op jit(solution)/shard_map/ppermute | solution.py:443
  50.7 4.6 %collective-permute-start.3 = (f32[20,8,128]{2,1,0:T(8,128)S(1)}, f32[20,8,128]{2,1,0:T(8,128)S(1)}, u32[]{:S(2)}, u32[]{:S(2)}) collective-permute-start(f32[20,8,128]{2,1,0:T(8,128)S(1)} %get-tuple-element.31.sent_far), channel_id=1, source_target_pairs={{0,448},{64,128},{128,64},{192,256},{256,192},{320,384},{384,320},... | collective-permute-start | bytes 245768 | tf_op jit(solution)/shard_map/ppermute | solution.py:442
  55.3 0.0 collective-permute-done.2.got_near
  55.3 2.9 %collective-permute-done.3.got_far = f32[20,8,128]{2,1,0:T(8,128)S(1)} collective-permute-done((f32[20,8,128]{2,1,0:T(8,128)S(1)}, f32[20,8,128]{2,1,0:T(8,128)S(1)}, u32[]{:S(2)}, u32[]{:S(2)}) %collective-permute-start.3) | collective-permute-done | bytes 81952 | tf_op jit(solution)/shard_map/ppermute | solution.py:442
  58.3 0.6 %shard_map.49 = (f32[19,6,8,128]{3,2,1,0:T(8,128)S(1)}, f32[5,8,128]{2,1,0:T(8,128)S(1)}, f32[5,8,128]{2,1,0:T(8,128)S(1)}) custom-call(f32[19,8,8,128]{3,2,1,0:T(8,128)S(1)} %get-tuple-element.23.p1, f32[20,8,128]{2,1,0:T(8,128)S(1)} %get-tuple-element.28.post_side, f32[20,8,128]{2,1,0:T(8,128)S(1)} %get-tuple-element.29.side, ...), custom_call_target="tpu_custom_call" | custom-call | tf_op jit(solution)/shard_map/pallas_call | solution.py:426
  58.9 0.0 all-to-all-done.1.planes
  58.9 1.1 %shard_map.52 = f32[19,8,8,128]{3,2,1,0:T(8,128)} custom-call(f32[19,6,8,128]{3,2,1,0:T(8,128)S(1)} %get-tuple-element.32.p2, f32[5,8,128]{2,1,0:T(8,128)S(1)} %get-tuple-element.33.ahead, f32[5,8,128]{2,1,0:T(8,128)S(1)} %get-tuple-element.34.behind, f32[8,5,8,128]{3,2,1,0:T(8,128)S(1)} %all-to-all-done.1.planes), custom_call_target="tpu_custom_call" | custom-call | tf_op jit(solution)/shard_map/pallas_call | solution.py:426
  (1 shorter events, 0.0 us)
Async XLA Ops:
  1.4 8.1 %collective-permute-start.1 = (f32[5,8,128]{2,1,0:T(8,128)S(1)}, f32[5,8,128]{2,1,0:T(8,128)S(1)}, u32[]{:S(2)}, u32[]{:S(2)}) collective-permute-start(f32[5,8,128]{2,1,0:T(8,128)S(1)} %get-tuple-element.24), channel_id=1, source_target_pairs={{0,56},{8,16},{16,8},{24,32},{32,24},{40,48},{48,40},{56,0},{1,57}... | collective-permute-start | bytes 61448 | tf_op jit(solution)/shard_map/ppermute | solution.py:442
  6.8 5.7 %collective-permute-start = (f32[5,8,128]{2,1,0:T(8,128)S(1)}, f32[5,8,128]{2,1,0:T(8,128)S(1)}, u32[]{:S(2)}, u32[]{:S(2)}) collective-permute-start(f32[5,8,128]{2,1,0:T(8,128)S(1)} %get-tuple-element.24), channel_id=1, source_target_pairs={{0,8},{8,0},{16,24},{24,16},{32,40},{40,32},{48,56},{56,48},{1,9},... | collective-permute-start | bytes 61448 | tf_op jit(solution)/shard_map/ppermute | solution.py:443
  32.8 9.1 %collective-permute-start.5 = (f32[8,3,8,128]{3,2,1,0:T(8,128)S(1)}, f32[8,3,8,128]{3,2,1,0:T(8,128)S(1)}, u32[]{:S(2)}, u32[]{:S(2)}) collective-permute-start(f32[8,3,8,128]{3,2,1,0:T(8,128)S(1)} %get-tuple-element.37), channel_id=1, source_target_pairs={{0,7},{1,2},{2,1},{3,4},{4,3},{5,6},{6,5},{7,0},{8,15},{9,10},{10,... | collective-permute-start | bytes 294920 | tf_op jit(solution)/shard_map/ppermute | solution.py:442
  34.7 7.2 %collective-permute-start.4 = (f32[8,3,8,128]{3,2,1,0:T(8,128)S(1)}, f32[8,3,8,128]{3,2,1,0:T(8,128)S(1)}, u32[]{:S(2)}, u32[]{:S(2)}) collective-permute-start(f32[8,3,8,128]{3,2,1,0:T(8,128)S(1)} %get-tuple-element.38), channel_id=1, source_target_pairs={{0,1},{1,0},{2,3},{3,2},{4,5},{5,4},{6,7},{7,6},{8,9},{9,8},{10,11... | collective-permute-start | bytes 294920 | tf_op jit(solution)/shard_map/ppermute | solution.py:443
  43.5 15.4 %all-to-all-start.1 = ((f32[8,5,8,128]{3,2,1,0:T(8,128)}), f32[8,5,8,128]{3,2,1,0:T(8,128)S(1)}, u32[]{:S(2)}, u32[]{:S(2)}) async-start(f32[8,5,8,128]{3,2,1,0:T(8,128)} %shard_map.51), calls=%async_computation.1 | async-start | bytes 327680 | tf_op jit(solution)/shard_map/all_to_all | solution.py:486
  46.9 8.4 %collective-permute-start.2 = (f32[20,8,128]{2,1,0:T(8,128)S(1)}, f32[20,8,128]{2,1,0:T(8,128)S(1)}, u32[]{:S(2)}, u32[]{:S(2)}) collective-permute-start(f32[20,8,128]{2,1,0:T(8,128)S(1)} %get-tuple-element.30.sent_near), channel_id=1, source_target_pairs={{0,64},{64,0},{128,192},{192,128},{256,320},{320,256},{384,448},{4... | collective-permute-start | bytes 245768 | tf_op jit(solution)/shard_map/ppermute | solution.py:443
  50.7 7.5 %collective-permute-start.3 = (f32[20,8,128]{2,1,0:T(8,128)S(1)}, f32[20,8,128]{2,1,0:T(8,128)S(1)}, u32[]{:S(2)}, u32[]{:S(2)}) collective-permute-start(f32[20,8,128]{2,1,0:T(8,128)S(1)} %get-tuple-element.31.sent_far), channel_id=1, source_target_pairs={{0,448},{64,128},{128,64},{192,256},{256,192},{320,384},{384,320},... | collective-permute-start | bytes 245768 | tf_op jit(solution)/shard_map/ppermute | solution.py:442

commit v7 on v6

--- a/solution.py
+++ b/solution.py
@@ -171,7 +171,7 @@
                 chunks[d, group * 3 + tile] = held[d]
 
 
-def edge_kernel_2(near, far, p1, codes, wrapped, middle, sides, chunks, post_side, side, rows_near, rows_far):
+def edge_kernel_2(near, far, p1, codes, wrapped, middle, sides, chunks, post_side, side, rows_ahead, rows_behind):
     lane, row = lanes(), rows()
     ends = (lane == 0) | (lane == 127)
     bases = set_bases()
@@ -194,7 +194,6 @@
     for i in range(20):
         side[i] = shifted[i]
         post_side[i] = beside[i]
-    even = lax.axis_index("gx") % 2 == 0
     for item in range(20):
         sent = []
         for k in range(2):
@@ -207,8 +206,7 @@
                 spot = jnp.where(lane == 4 * (row - step_z) + start, spot, 0.0)
                 value = jnp.where(lane == at, jnp.sum(spot, axis=1, keepdims=True), value)
             sent.append(jnp.where(row == 0, jnp.broadcast_to(shifted[i][x : x + 1, :], (8, 128)), value))
-        rows_near[item] = jnp.where(even, sent[0], sent[1])
-        rows_far[item] = jnp.where(even, sent[1], sent[0])
+        rows_ahead[item], rows_behind[item] = sent
     for group in range(2):
         for tile in range(3):
             held = [jnp.zeros((8, 128), F32)] * 2
@@ -319,17 +317,9 @@
     return jnp.where(row == to, jnp.broadcast_to(source[z : z + 1, :], (8, 128)), roll(value, velocities[i][0], 0))
 
 
-def inner_kernel(p1, post_side, side, codes, sent_near, sent_far, got_near, got_far, p2, ahead, behind):
+def inner_kernel(p1, post_side, side, codes, sent_ahead, sent_behind, from_behind, from_ahead, p2, ahead, behind):
     lane, row = lanes(), rows()
-    even = lax.axis_index("gx") % 2 == 0
-    own = (
-        [jnp.where(even, sent_near[item], sent_far[item]) for item in range(5)],
-        [jnp.where(even, sent_far[item], sent_near[item]) for item in range(5)],
-    )
-    got = (
-        [jnp.where(even, got_far[item], got_near[item]) for item in range(20)],
-        [jnp.where(even, got_near[item], got_far[item]) for item in range(20)],
-    )
+    own, got = (sent_ahead, sent_behind), (from_behind, from_ahead)
 
     def entering(k):
         f = [None] * 20
@@ -435,6 +425,13 @@
     )(*args)
 
 
+def neighbours(value_up, value_down, axis):
+    peers = lax.axis_size(axis)
+    up = [(i, (i + 1) % peers) for i in range(peers)]
+    down = [(j, i) for i, j in up]
+    return lax.ppermute(value_up, axis, up), lax.ppermute(value_down, axis, down)
+
+
 def swaps(to_near, to_far, axis):
     peers = lax.axis_size(axis)
     pair = [(i, i ^ 1) for i in range(peers)]
@@ -463,19 +460,19 @@
         [(19, 8) + tile, (10,) + tile, (6, 6) + tile, (2, 20) + tile],
         (pops, codes),
     )
-    chunks, post_side, side, sent_near, sent_far = run(
+    chunks, post_side, side, sent_ahead, sent_behind = run(
         edge_kernel_2,
         [(8, 6) + tile, (20,) + tile, (20,) + tile, (20,) + tile, (20,) + tile],
         (near, far, p1, codes, wrapped, middle, sides),
     )
-    got_near, got_far = swaps(sent_near, sent_far, "gx")
+    from_behind, from_ahead = neighbours(sent_ahead, sent_behind, "gx")
     own = lax.all_to_all(chunks, "gx", 0, 0)
     near, far = swaps(own[:, 0:3], own[:, 3:6], "gz")
     (spread,) = run(spread_kernel, [(20, 64, 128)], (own,))
     p2, ahead, behind = run(
         inner_kernel,
         [(19, 6) + tile, (5,) + tile, (5,) + tile],
-        (p1, post_side, side, codes, sent_near, sent_far, got_near, got_far),
+        (p1, post_side, side, codes, sent_ahead, sent_behind, from_behind, from_ahead),
     )
     (planes,) = run(
         plane_kernel,

time: 60.4 us -> 59.3 us (0.982)
  starting transfers between devices: 23.9 us -> 22.5 us
    ppermute x0 -> x2, starting transfers between devices: none -> 7.05 us  [the longest x1 3.82 us: neighbours(): lax.ppermute(value_up, axis, up)]
    ppermute x3 -> x2, starting transfers between devices: 12 us -> 7.37 us  [swaps(): far = lax.ppermute(to_far, axis, other)]
    ppermute x3 -> x2, starting transfers between devices: 8.54 us -> 4.72 us  [swaps(): near = lax.ppermute(to_near, axis, pair)]
    ppermute x0 -> x2, waiting for transfers between devices: none -> 3.09 us  [the longest x1 2.37 us: neighbours(): lax.ppermute(value_down, axis, down)]
    ppermute x3 -> x2, waiting for transfers between devices: 7.02 us -> 4.11 us  [swaps(): far = lax.ppermute(to_far, axis, other)]
    ppermute x3 -> x2, waiting for transfers between devices: 3.04 us -> 3.04 us  [swaps(): near = lax.ppermute(to_near, axis, pair)]
  transfers between devices with their start and end apart: 7 -> 7, of which waited for: 3 -> 4; matrix products, arithmetic and copies ran while one was open for 0% -> 0% of each run, Pallas kernels for 3% -> 3%
where the time goes in v7:
time: 59.3 us; the launch traced here: 58.9 us
  starting transfers between devices  22.5 us (38%)
  blocking collectives  19.9 us (34%)
  waiting for transfers between devices  10.2 us (17%)
  Pallas kernels  6.07 us (10%)
    all_to_all x1, blocking collectives, body(): own = lax.all_to_all(chunks, 'gx', 0, 0)  19.9 us
    ppermute x2, starting transfers between devices, swaps(): far = lax.ppermute(to_far, axis, other)  7.37 us
    pallas_call x7, Pallas kernels, run(): pl.pallas_call(kernel, out_shape=[s if isinstance(s, jax.ShapeDtypeStruct...  6.07 us
    ppermute x2, starting transfers between devices, swaps(): near = lax.ppermute(to_near, axis, pair)  4.72 us
    ppermute x2, waiting for transfers between devices, swaps(): far = lax.ppermute(to_far, axis, other)  4.11 us
    ppermute x1, starting transfers between devices, neighbours(): lax.ppermute(value_up, axis, up)  3.82 us
    all_to_all x1, starting transfers between devices, body(): planes = lax.all_to_all(planes, 'gx', 0, 0)  3.38 us
    ppermute x1, starting transfers between devices, neighbours(): lax.ppermute(value_down, axis, down)  3.24 us
  transfers between devices with their start and end apart: 7, of which 4 were waited for; matrix products, arithmetic and copies ran while one was open for 0% of the time, Pallas kernels for 3%

profile of v7, /device:TPU:40, one launch (start us, length us, event | category | flops | bytes accessed | tf_op | source)
XLA Modules:
  0.0 58.9 jit_solution(7072421813950538028)
XLA Ops:
  0.0 1.4 %shard_map.46 = (f32[5,8,128]{2,1,0:T(8,128)S(1)}, f32[19,8,8,128]{3,2,1,0:T(8,128)S(1)}, s32[8,8,128]{2,1,0:T(8,128)S(1)}, f32[8,128]{1,0:T(8,128)S(1)}) custom-call(f32[19,8,8,128]{3,2,1,0:T(8,128)} %pops_far.1, s32[8,8,128]{2,1,0:T(8,128)} %codes_far.1, s32[2,8]{1,0:T(2,128)} %offsets_far.1, s32[2,8]{1,0:T(2,128)} %fractions_far.1), custom_call_target="tpu_custom_call" | custom-call | tf_op jit(solution)/shard_map/pallas_call | solution.py:416
  1.4 5.5 %collective-permute-start.1 = (f32[5,8,128]{2,1,0:T(8,128)S(1)}, f32[5,8,128]{2,1,0:T(8,128)S(1)}, u32[]{:S(2)}, u32[]{:S(2)}) collective-permute-start(f32[5,8,128]{2,1,0:T(8,128)S(1)} %get-tuple-element.24), channel_id=1, source_target_pairs={{0,56},{8,16},{16,8},{24,32},{32,24},{40,48},{48,40},{56,0},{1,57}... | collective-permute-start | bytes 61448 | tf_op jit(solution)/shard_map/ppermute | solution.py:439
  6.8 1.9 %collective-permute-start = (f32[5,8,128]{2,1,0:T(8,128)S(1)}, f32[5,8,128]{2,1,0:T(8,128)S(1)}, u32[]{:S(2)}, u32[]{:S(2)}) collective-permute-start(f32[5,8,128]{2,1,0:T(8,128)S(1)} %get-tuple-element.24), channel_id=1, source_target_pairs={{0,8},{8,0},{16,24},{24,16},{32,40},{40,32},{48,56},{56,48},{1,9},... | collective-permute-start | bytes 61448 | tf_op jit(solution)/shard_map/ppermute | solution.py:440
  8.8 0.7 %shard_map.47 = (f32[19,8,8,128]{3,2,1,0:T(8,128)S(1)}, f32[10,8,128]{2,1,0:T(8,128)S(1)}, f32[6,6,8,128]{3,2,1,0:T(8,128)S(1)}, f32[2,20,8,128]{3,2,1,0:T(8,128)S(1)}) custom-call(f32[19,8,8,128]{3,2,1,0:T(8,128)S(1)} %get-tuple-element.21.pops, s32[8,8,128]{2,1,0:T(8,128)S(1)} %get-tuple-element.22.codes), custom_call_target="tpu_custom_call" | custom-call | tf_op jit(solution)/shard_map/pallas_call | solution.py:416
  9.5 0.0 collective-permute-done.1.far
  9.5 3.0 %collective-permute-done.near = f32[5,8,128]{2,1,0:T(8,128)S(1)} collective-permute-done((f32[5,8,128]{2,1,0:T(8,128)S(1)}, f32[5,8,128]{2,1,0:T(8,128)S(1)}, u32[]{:S(2)}, u32[]{:S(2)}) %collective-permute-start) | collective-permute-done | bytes 20512 | tf_op jit(solution)/shard_map/ppermute | solution.py:440
  12.5 0.4 shard_map.48
  12.9 19.9 %all_to_all.10.own = f32[8,6,8,128]{3,2,1,0:T(8,128)S(1)} all-to-all(f32[8,6,8,128]{3,2,1,0:T(8,128)S(1)} %get-tuple-element.36), channel_id=1, replica_groups=mesh['gx'=8,'gy'=8,'gz'=8] {'gx'}, dimensions={0} | all-to-all | bytes 393216 | tf_op jit(solution)/shard_map/all_to_all | solution.py:469
  32.8 1.9 %collective-permute-start.5 = (f32[8,3,8,128]{3,2,1,0:T(8,128)S(1)}, f32[8,3,8,128]{3,2,1,0:T(8,128)S(1)}, u32[]{:S(2)}, u32[]{:S(2)}) collective-permute-start(f32[8,3,8,128]{3,2,1,0:T(8,128)S(1)} %get-tuple-element.37), channel_id=1, source_target_pairs={{0,7},{1,2},{2,1},{3,4},{4,3},{5,6},{6,5},{7,0},{8,15},{9,10},{10,... | collective-permute-start | bytes 294920 | tf_op jit(solution)/shard_map/ppermute | solution.py:439
  34.7 2.8 %collective-permute-start.4 = (f32[8,3,8,128]{3,2,1,0:T(8,128)S(1)}, f32[8,3,8,128]{3,2,1,0:T(8,128)S(1)}, u32[]{:S(2)}, u32[]{:S(2)}) collective-permute-start(f32[8,3,8,128]{3,2,1,0:T(8,128)S(1)} %get-tuple-element.38), channel_id=1, source_target_pairs={{0,1},{1,0},{2,3},{3,2},{4,5},{5,4},{6,7},{7,6},{8,9},{9,8},{10,11... | collective-permute-start | bytes 294920 | tf_op jit(solution)/shard_map/ppermute | solution.py:440
  37.5 0.2 shard_map.50.spread
  37.8 4.1 %collective-permute-done.5.far = f32[8,3,8,128]{3,2,1,0:T(8,128)S(1)} collective-permute-done((f32[8,3,8,128]{3,2,1,0:T(8,128)S(1)}, f32[8,3,8,128]{3,2,1,0:T(8,128)S(1)}, u32[]{:S(2)}, u32[]{:S(2)}) %collective-permute-start.5) | collective-permute-done | bytes 98336 | tf_op jit(solution)/shard_map/ppermute | solution.py:439
  41.9 0.0 collective-permute-done.4.near
  41.9 1.6 %shard_map.51 = f32[8,5,8,128]{3,2,1,0:T(8,128)} custom-call(f32[8,128]{1,0:T(8,128)S(1)} %get-tuple-element.35.params, f32[20,64,128]{2,1,0:T(8,128)S(1)} %shard_map.50.spread, f32[8,3,8,128]{3,2,1,0:T(8,128)S(1)} %collective-permute-done.4.near, f32[8,3,8,128]{3,2,1,0:T(8,128)S(1)} %collective-permute-done.5.far), custom_call_target="tpu_custom_call" | custom-call | tf_op jit(solution)/shard_map/pallas_call | solution.py:416
  43.5 3.4 %all-to-all-start.1 = ((f32[8,5,8,128]{3,2,1,0:T(8,128)}), f32[8,5,8,128]{3,2,1,0:T(8,128)S(1)}, u32[]{:S(2)}, u32[]{:S(2)}) async-start(f32[8,5,8,128]{3,2,1,0:T(8,128)} %shard_map.51), calls=%async_computation.1 | async-start | bytes 327680 | tf_op jit(solution)/shard_map/all_to_all | solution.py:483
  46.9 3.8 %collective-permute-start.2 = (f32[20,8,128]{2,1,0:T(8,128)S(1)}, f32[20,8,128]{2,1,0:T(8,128)S(1)}, u32[]{:S(2)}, u32[]{:S(2)}) collective-permute-start(f32[20,8,128]{2,1,0:T(8,128)S(1)} %get-tuple-element.30.sent_ahead), channel_id=1, source_target_pairs={{0,64},{64,128},{128,192},{192,256},{256,320},{320,384},{384,448},... | collective-permute-start | bytes 245768 | tf_op jit(solution)/shard_map/ppermute | solution.py:432
  50.7 3.2 %collective-permute-start.3 = (f32[20,8,128]{2,1,0:T(8,128)S(1)}, f32[20,8,128]{2,1,0:T(8,128)S(1)}, u32[]{:S(2)}, u32[]{:S(2)}) collective-permute-start(f32[20,8,128]{2,1,0:T(8,128)S(1)} %get-tuple-element.31.sent_behind), channel_id=1, source_target_pairs={{64,0},{128,64},{192,128},{256,192},{320,256},{384,320},{448,384},... | collective-permute-start | bytes 245768 | tf_op jit(solution)/shard_map/ppermute | solution.py:432
  54.0 0.7 %collective-permute-done.2.from_behind = f32[20,8,128]{2,1,0:T(8,128)S(1)} collective-permute-done((f32[20,8,128]{2,1,0:T(8,128)S(1)}, f32[20,8,128]{2,1,0:T(8,128)S(1)}, u32[]{:S(2)}, u32[]{:S(2)}) %collective-permute-start.2) | collective-permute-done | bytes 81952 | tf_op jit(solution)/shard_map/ppermute | solution.py:432
  54.7 2.4 %collective-permute-done.3.from_ahead = f32[20,8,128]{2,1,0:T(8,128)S(1)} collective-permute-done((f32[20,8,128]{2,1,0:T(8,128)S(1)}, f32[20,8,128]{2,1,0:T(8,128)S(1)}, u32[]{:S(2)}, u32[]{:S(2)}) %collective-permute-start.3) | collective-permute-done | bytes 81952 | tf_op jit(solution)/shard_map/ppermute | solution.py:432
  57.0 0.7 %shard_map.49 = (f32[19,6,8,128]{3,2,1,0:T(8,128)S(1)}, f32[5,8,128]{2,1,0:T(8,128)S(1)}, f32[5,8,128]{2,1,0:T(8,128)S(1)}) custom-call(f32[19,8,8,128]{3,2,1,0:T(8,128)S(1)} %get-tuple-element.23.p1, f32[20,8,128]{2,1,0:T(8,128)S(1)} %get-tuple-element.28.post_side, f32[20,8,128]{2,1,0:T(8,128)S(1)} %get-tuple-element.29.side, ...), custom_call_target="tpu_custom_call" | custom-call | tf_op jit(solution)/shard_map/pallas_call | solution.py:416
  57.7 0.0 all-to-all-done.1.planes
  57.7 1.1 %shard_map.52 = f32[19,8,8,128]{3,2,1,0:T(8,128)} custom-call(f32[19,6,8,128]{3,2,1,0:T(8,128)S(1)} %get-tuple-element.32.p2, f32[5,8,128]{2,1,0:T(8,128)S(1)} %get-tuple-element.33.ahead, f32[5,8,128]{2,1,0:T(8,128)S(1)} %get-tuple-element.34.behind, f32[8,5,8,128]{3,2,1,0:T(8,128)S(1)} %all-to-all-done.1.planes), custom_call_target="tpu_custom_call" | custom-call | tf_op jit(solution)/shard_map/pallas_call | solution.py:416
  (1 shorter events, 0.0 us)
Async XLA Ops:
  1.4 8.1 %collective-permute-start.1 = (f32[5,8,128]{2,1,0:T(8,128)S(1)}, f32[5,8,128]{2,1,0:T(8,128)S(1)}, u32[]{:S(2)}, u32[]{:S(2)}) collective-permute-start(f32[5,8,128]{2,1,0:T(8,128)S(1)} %get-tuple-element.24), channel_id=1, source_target_pairs={{0,56},{8,16},{16,8},{24,32},{32,24},{40,48},{48,40},{56,0},{1,57}... | collective-permute-start | bytes 61448 | tf_op jit(solution)/shard_map/ppermute | solution.py:439
  6.8 5.7 %collective-permute-start = (f32[5,8,128]{2,1,0:T(8,128)S(1)}, f32[5,8,128]{2,1,0:T(8,128)S(1)}, u32[]{:S(2)}, u32[]{:S(2)}) collective-permute-start(f32[5,8,128]{2,1,0:T(8,128)S(1)} %get-tuple-element.24), channel_id=1, source_target_pairs={{0,8},{8,0},{16,24},{24,16},{32,40},{40,32},{48,56},{56,48},{1,9},... | collective-permute-start | bytes 61448 | tf_op jit(solution)/shard_map/ppermute | solution.py:440
  32.8 9.1 %collective-permute-start.5 = (f32[8,3,8,128]{3,2,1,0:T(8,128)S(1)}, f32[8,3,8,128]{3,2,1,0:T(8,128)S(1)}, u32[]{:S(2)}, u32[]{:S(2)}) collective-permute-start(f32[8,3,8,128]{3,2,1,0:T(8,128)S(1)} %get-tuple-element.37), channel_id=1, source_target_pairs={{0,7},{1,2},{2,1},{3,4},{4,3},{5,6},{6,5},{7,0},{8,15},{9,10},{10,... | collective-permute-start | bytes 294920 | tf_op jit(solution)/shard_map/ppermute | solution.py:439
  34.7 7.2 %collective-permute-start.4 = (f32[8,3,8,128]{3,2,1,0:T(8,128)S(1)}, f32[8,3,8,128]{3,2,1,0:T(8,128)S(1)}, u32[]{:S(2)}, u32[]{:S(2)}) collective-permute-start(f32[8,3,8,128]{3,2,1,0:T(8,128)S(1)} %get-tuple-element.38), channel_id=1, source_target_pairs={{0,1},{1,0},{2,3},{3,2},{4,5},{5,4},{6,7},{7,6},{8,9},{9,8},{10,11... | collective-permute-start | bytes 294920 | tf_op jit(solution)/shard_map/ppermute | solution.py:440
  43.5 14.2 %all-to-all-start.1 = ((f32[8,5,8,128]{3,2,1,0:T(8,128)}), f32[8,5,8,128]{3,2,1,0:T(8,128)S(1)}, u32[]{:S(2)}, u32[]{:S(2)}) async-start(f32[8,5,8,128]{3,2,1,0:T(8,128)} %shard_map.51), calls=%async_computation.1 | async-start | bytes 327680 | tf_op jit(solution)/shard_map/all_to_all | solution.py:483
  46.9 7.8 %collective-permute-start.2 = (f32[20,8,128]{2,1,0:T(8,128)S(1)}, f32[20,8,128]{2,1,0:T(8,128)S(1)}, u32[]{:S(2)}, u32[]{:S(2)}) collective-permute-start(f32[20,8,128]{2,1,0:T(8,128)S(1)} %get-tuple-element.30.sent_ahead), channel_id=1, source_target_pairs={{0,64},{64,128},{128,192},{192,256},{256,320},{320,384},{384,448},... | collective-permute-start | bytes 245768 | tf_op jit(solution)/shard_map/ppermute | solution.py:432
  50.7 6.3 %collective-permute-start.3 = (f32[20,8,128]{2,1,0:T(8,128)S(1)}, f32[20,8,128]{2,1,0:T(8,128)S(1)}, u32[]{:S(2)}, u32[]{:S(2)}) collective-permute-start(f32[20,8,128]{2,1,0:T(8,128)S(1)} %get-tuple-element.31.sent_behind), channel_id=1, source_target_pairs={{64,0},{128,64},{192,128},{256,192},{320,256},{384,320},{448,384},... | collective-permute-start | bytes 245768 | tf_op jit(solution)/shard_map/ppermute | solution.py:432

commit v8 on v7

--- a/solution.py
+++ b/solution.py
@@ -171,7 +171,7 @@
                 chunks[d, group * 3 + tile] = held[d]
 
 
-def edge_kernel_2(near, far, p1, codes, wrapped, middle, sides, chunks, post_side, side, rows_ahead, rows_behind):
+def edge_kernel_2(far, near, p1, codes, wrapped, middle, sides, chunks, post_side, side, rows_ahead, rows_behind):
     lane, row = lanes(), rows()
     ends = (lane == 0) | (lane == 127)
     bases = set_bases()
@@ -253,7 +253,7 @@
             work[item, 8 * b : 8 * b + 8, :] = roll(value, to, 1)
 
 
-def plane_kernel(params, spread, near, far, out, work, state):
+def plane_kernel(params, spread, far, near, out, work, state):
     length = work.shape[1]
     lane8 = lanes()
     lane = lanes((length, 128))
@@ -317,7 +317,24 @@
     return jnp.where(row == to, jnp.broadcast_to(source[z : z + 1, :], (8, 128)), roll(value, velocities[i][0], 0))
 
 
-def inner_kernel(p1, post_side, side, codes, sent_ahead, sent_behind, from_behind, from_ahead, p2, ahead, behind):
+def mended(value, edge, step, z):
+    lane = lanes()
+    if step == 1:
+        return jnp.where(lane == 0, roll(edge, -(4 * z + 1), 1), value)
+    if step == -1:
+        return jnp.where(lane == 127, roll(edge, 127 - (4 * z + 2), 1), value)
+    return value
+
+
+def arrive_kernel(p1, post_side, arrived):
+    for z in range(1, 7):
+        for i in range(19):
+            source = z - velocities[i][2]
+            value = mended(p1[i, source], post_side[i], velocities[i][1], source)
+            arrived[i, z - 1] = roll(value, velocities[i][0], 0)
+
+
+def inner_kernel(arrived, side, codes, sent_ahead, sent_behind, from_behind, from_ahead, p2, ahead, behind):
     lane, row = lanes(), rows()
     own, got = (sent_ahead, sent_behind), (from_behind, from_ahead)
 
@@ -353,19 +370,15 @@
                 value = jnp.where(lane == at, jnp.sum(spot, axis=1, keepdims=True), value)
             out[j] = value
 
-    def mended(value, edge, step, z):
-        if step == 1:
-            return jnp.where(lane == 0, roll(edge, -(4 * z + 1), 1), value)
-        if step == -1:
-            return jnp.where(lane == 127, roll(edge, 127 - (4 * z + 2), 1), value)
-        return value
-
     for z in range(1, 7):
         f = []
         for i in range(19):
-            source = z - velocities[i][2]
-            value = mended(p1[i, source], post_side[i], velocities[i][1], source)
-            f.append(moved_x(value, i, z, lambda j: got[0][j], lambda j: got[1][j], row))
+            value = arrived[i, z - 1]
+            for members, k, at in ((forward, 0, 0), (backward, 1, 7)):
+                if i in members:
+                    entered = got[k][members.index(i)][z : z + 1, :]
+                    value = jnp.where(row == at, jnp.broadcast_to(entered, (8, 128)), value)
+            f.append(value)
         post = collide(f, codes[z].astype(F32) * (1.0 / LEVELS))
         for i in range(19):
             step = velocities[i][1]
@@ -463,21 +476,22 @@
     chunks, post_side, side, sent_ahead, sent_behind = run(
         edge_kernel_2,
         [(8, 6) + tile, (20,) + tile, (20,) + tile, (20,) + tile, (20,) + tile],
-        (near, far, p1, codes, wrapped, middle, sides),
+        (far, near, p1, codes, wrapped, middle, sides),
     )
     from_behind, from_ahead = neighbours(sent_ahead, sent_behind, "gx")
     own = lax.all_to_all(chunks, "gx", 0, 0)
     near, far = swaps(own[:, 0:3], own[:, 3:6], "gz")
     (spread,) = run(spread_kernel, [(20, 64, 128)], (own,))
+    (arrived,) = run(arrive_kernel, [(19, 6) + tile], (p1, post_side))
     p2, ahead, behind = run(
         inner_kernel,
         [(19, 6) + tile, (5,) + tile, (5,) + tile],
-        (p1, post_side, side, codes, sent_ahead, sent_behind, from_behind, from_ahead),
+        (arrived, side, codes, sent_ahead, sent_behind, from_behind, from_ahead),
     )
     (planes,) = run(
         plane_kernel,
         [(8, 5) + tile],
-        (params, spread, near, far),
+        (params, spread, far, near),
         scratch=[(20, 64, 128), (19, 64, 128)],
     )
     planes = lax.all_to_all(planes, "gx", 0, 0)

time: 59.3 us -> 58.9 us (level)
    pallas_call x7 -> x8, Pallas kernels: 6.07 us -> 5.88 us  [run(): pl.pallas_call(kernel, out_shape=[s if isinstance(s, jax.ShapeDtypeStruct...]
  transfers between devices with their start and end apart: 7 -> 7, of which waited for: 4 -> 4; matrix products, arithmetic and copies ran while one was open for 0% -> 0% of each run, Pallas kernels for 3% -> 2%
where the time goes in v8:
time: 58.9 us; the launch traced here: 58.5 us
  starting transfers between devices  22.5 us (38%)
  blocking collectives  19.9 us (34%)
  waiting for transfers between devices  10.1 us (17%)
  Pallas kernels  5.88 us (10%)
    all_to_all x1, blocking collectives, body(): own = lax.all_to_all(chunks, 'gx', 0, 0)  19.9 us
    ppermute x2, starting transfers between devices, swaps(): far = lax.ppermute(to_far, axis, other)  7.37 us
    pallas_call x8, Pallas kernels, run(): pl.pallas_call(kernel, out_shape=[s if isinstance(s, jax.ShapeDtypeStruct...  5.88 us
    ppermute x2, starting transfers between devices, swaps(): near = lax.ppermute(to_near, axis, pair)  4.72 us
    ppermute x2, waiting for transfers between devices, swaps(): far = lax.ppermute(to_far, axis, other)  4.11 us
    ppermute x1, starting transfers between devices, neighbours(): lax.ppermute(value_up, axis, up)  3.82 us
    all_to_all x1, starting transfers between devices, body(): planes = lax.all_to_all(planes, 'gx', 0, 0)  3.38 us
    ppermute x1, starting transfers between devices, neighbours(): lax.ppermute(value_down, axis, down)  3.24 us
  transfers between devices with their start and end apart: 7, of which 4 were waited for; matrix products, arithmetic and copies ran while one was open for 0% of the time, Pallas kernels for 2%

profile of v8, /device:TPU:40, one launch (start us, length us, event | category | flops | bytes accessed | tf_op | source)
XLA Modules:
  0.0 58.5 jit_solution(6880344044386027597)
XLA Ops:
  0.0 1.4 %shard_map.46 = (f32[5,8,128]{2,1,0:T(8,128)S(1)}, f32[19,8,8,128]{3,2,1,0:T(8,128)S(1)}, s32[8,8,128]{2,1,0:T(8,128)S(1)}, f32[8,128]{1,0:T(8,128)S(1)}) custom-call(f32[19,8,8,128]{3,2,1,0:T(8,128)} %pops_far.1, s32[8,8,128]{2,1,0:T(8,128)} %codes_far.1, s32[2,8]{1,0:T(2,128)} %offsets_far.1, s32[2,8]{1,0:T(2,128)} %fractions_far.1), custom_call_target="tpu_custom_call" | custom-call | tf_op jit(solution)/shard_map/pallas_call | solution.py:429
  1.4 5.5 %collective-permute-start = (f32[5,8,128]{2,1,0:T(8,128)S(1)}, f32[5,8,128]{2,1,0:T(8,128)S(1)}, u32[]{:S(2)}, u32[]{:S(2)}) collective-permute-start(f32[5,8,128]{2,1,0:T(8,128)S(1)} %get-tuple-element.24), channel_id=1, source_target_pairs={{0,56},{8,16},{16,8},{24,32},{32,24},{40,48},{48,40},{56,0},{1,57}... | collective-permute-start | bytes 61448 | tf_op jit(solution)/shard_map/ppermute | solution.py:452
  6.8 1.9 %collective-permute-start.1 = (f32[5,8,128]{2,1,0:T(8,128)S(1)}, f32[5,8,128]{2,1,0:T(8,128)S(1)}, u32[]{:S(2)}, u32[]{:S(2)}) collective-permute-start(f32[5,8,128]{2,1,0:T(8,128)S(1)} %get-tuple-element.24), channel_id=1, source_target_pairs={{0,8},{8,0},{16,24},{24,16},{32,40},{40,32},{48,56},{56,48},{1,9},... | collective-permute-start | bytes 61448 | tf_op jit(solution)/shard_map/ppermute | solution.py:453
  8.8 0.7 %shard_map.47 = (f32[19,8,8,128]{3,2,1,0:T(8,128)S(1)}, f32[10,8,128]{2,1,0:T(8,128)S(1)}, f32[6,6,8,128]{3,2,1,0:T(8,128)S(1)}, f32[2,20,8,128]{3,2,1,0:T(8,128)S(1)}) custom-call(f32[19,8,8,128]{3,2,1,0:T(8,128)S(1)} %get-tuple-element.21.pops, s32[8,8,128]{2,1,0:T(8,128)S(1)} %get-tuple-element.22.codes), custom_call_target="tpu_custom_call" | custom-call | tf_op jit(solution)/shard_map/pallas_call | solution.py:429
  9.5 0.0 collective-permute-done.far
  9.5 3.0 %collective-permute-done.1.near = f32[5,8,128]{2,1,0:T(8,128)S(1)} collective-permute-done((f32[5,8,128]{2,1,0:T(8,128)S(1)}, f32[5,8,128]{2,1,0:T(8,128)S(1)}, u32[]{:S(2)}, u32[]{:S(2)}) %collective-permute-start.1) | collective-permute-done | bytes 20512 | tf_op jit(solution)/shard_map/ppermute | solution.py:453
  12.5 0.4 shard_map.48
  12.9 19.9 %all_to_all.10.own = f32[8,6,8,128]{3,2,1,0:T(8,128)S(1)} all-to-all(f32[8,6,8,128]{3,2,1,0:T(8,128)S(1)} %get-tuple-element.36), channel_id=1, replica_groups=mesh['gx'=8,'gy'=8,'gz'=8] {'gx'}, dimensions={0} | all-to-all | bytes 393216 | tf_op jit(solution)/shard_map/all_to_all | solution.py:482
  32.8 1.9 %collective-permute-start.4 = (f32[8,3,8,128]{3,2,1,0:T(8,128)S(1)}, f32[8,3,8,128]{3,2,1,0:T(8,128)S(1)}, u32[]{:S(2)}, u32[]{:S(2)}) collective-permute-start(f32[8,3,8,128]{3,2,1,0:T(8,128)S(1)} %get-tuple-element.38), channel_id=1, source_target_pairs={{0,7},{1,2},{2,1},{3,4},{4,3},{5,6},{6,5},{7,0},{8,15},{9,10},{10,... | collective-permute-start | bytes 294920 | tf_op jit(solution)/shard_map/ppermute | solution.py:452
  34.7 2.8 %collective-permute-start.5 = (f32[8,3,8,128]{3,2,1,0:T(8,128)S(1)}, f32[8,3,8,128]{3,2,1,0:T(8,128)S(1)}, u32[]{:S(2)}, u32[]{:S(2)}) collective-permute-start(f32[8,3,8,128]{3,2,1,0:T(8,128)S(1)} %get-tuple-element.37), channel_id=1, source_target_pairs={{0,1},{1,0},{2,3},{3,2},{4,5},{5,4},{6,7},{7,6},{8,9},{9,8},{10,11... | collective-permute-start | bytes 294920 | tf_op jit(solution)/shard_map/ppermute | solution.py:453
  37.5 0.2 shard_map.51.spread
  37.8 4.1 %collective-permute-done.4.far = f32[8,3,8,128]{3,2,1,0:T(8,128)S(1)} collective-permute-done((f32[8,3,8,128]{3,2,1,0:T(8,128)S(1)}, f32[8,3,8,128]{3,2,1,0:T(8,128)S(1)}, u32[]{:S(2)}, u32[]{:S(2)}) %collective-permute-start.4) | collective-permute-done | bytes 98336 | tf_op jit(solution)/shard_map/ppermute | solution.py:452
  41.9 0.0 collective-permute-done.5.near
  41.9 1.6 %shard_map.52 = f32[8,5,8,128]{3,2,1,0:T(8,128)} custom-call(f32[8,128]{1,0:T(8,128)S(1)} %get-tuple-element.35.params, f32[20,64,128]{2,1,0:T(8,128)S(1)} %shard_map.51.spread, f32[8,3,8,128]{3,2,1,0:T(8,128)S(1)} %collective-permute-done.4.far, f32[8,3,8,128]{3,2,1,0:T(8,128)S(1)} %collective-permute-done.5.near), custom_call_target="tpu_custom_call" | custom-call | tf_op jit(solution)/shard_map/pallas_call | solution.py:429
  43.5 3.4 %all-to-all-start.1 = ((f32[8,5,8,128]{3,2,1,0:T(8,128)}), f32[8,5,8,128]{3,2,1,0:T(8,128)S(1)}, u32[]{:S(2)}, u32[]{:S(2)}) async-start(f32[8,5,8,128]{3,2,1,0:T(8,128)} %shard_map.52), calls=%async_computation.1 | async-start | bytes 327680 | tf_op jit(solution)/shard_map/all_to_all | solution.py:497
  46.9 3.8 %collective-permute-start.2 = (f32[20,8,128]{2,1,0:T(8,128)S(1)}, f32[20,8,128]{2,1,0:T(8,128)S(1)}, u32[]{:S(2)}, u32[]{:S(2)}) collective-permute-start(f32[20,8,128]{2,1,0:T(8,128)S(1)} %get-tuple-element.30.sent_ahead), channel_id=1, source_target_pairs={{0,64},{64,128},{128,192},{192,256},{256,320},{320,384},{384,448},... | collective-permute-start | bytes 245768 | tf_op jit(solution)/shard_map/ppermute | solution.py:445
  50.7 3.2 %collective-permute-start.3 = (f32[20,8,128]{2,1,0:T(8,128)S(1)}, f32[20,8,128]{2,1,0:T(8,128)S(1)}, u32[]{:S(2)}, u32[]{:S(2)}) collective-permute-start(f32[20,8,128]{2,1,0:T(8,128)S(1)} %get-tuple-element.31.sent_behind), channel_id=1, source_target_pairs={{64,0},{128,64},{192,128},{256,192},{320,256},{384,320},{448,384},... | collective-permute-start | bytes 245768 | tf_op jit(solution)/shard_map/ppermute | solution.py:445
  54.0 0.1 shard_map.49.arrived
  54.1 0.6 collective-permute-done.2.from_behind
  54.7 2.4 %collective-permute-done.3.from_ahead = f32[20,8,128]{2,1,0:T(8,128)S(1)} collective-permute-done((f32[20,8,128]{2,1,0:T(8,128)S(1)}, f32[20,8,128]{2,1,0:T(8,128)S(1)}, u32[]{:S(2)}, u32[]{:S(2)}) %collective-permute-start.3) | collective-permute-done | bytes 81952 | tf_op jit(solution)/shard_map/ppermute | solution.py:445
  57.1 0.4 shard_map.50
  57.4 0.0 all-to-all-done.1.planes
  57.4 1.1 %shard_map.53 = f32[19,8,8,128]{3,2,1,0:T(8,128)} custom-call(f32[19,6,8,128]{3,2,1,0:T(8,128)S(1)} %get-tuple-element.32.p2, f32[5,8,128]{2,1,0:T(8,128)S(1)} %get-tuple-element.33.ahead, f32[5,8,128]{2,1,0:T(8,128)S(1)} %get-tuple-element.34.behind, f32[8,5,8,128]{3,2,1,0:T(8,128)S(1)} %all-to-all-done.1.planes), custom_call_target="tpu_custom_call" | custom-call | tf_op jit(solution)/shard_map/pallas_call | solution.py:429
  (1 shorter events, 0.0 us)
Async XLA Ops:
  1.4 8.1 %collective-permute-start = (f32[5,8,128]{2,1,0:T(8,128)S(1)}, f32[5,8,128]{2,1,0:T(8,128)S(1)}, u32[]{:S(2)}, u32[]{:S(2)}) collective-permute-start(f32[5,8,128]{2,1,0:T(8,128)S(1)} %get-tuple-element.24), channel_id=1, source_target_pairs={{0,56},{8,16},{16,8},{24,32},{32,24},{40,48},{48,40},{56,0},{1,57}... | collective-permute-start | bytes 61448 | tf_op jit(solution)/shard_map/ppermute | solution.py:452
  6.8 5.7 %collective-permute-start.1 = (f32[5,8,128]{2,1,0:T(8,128)S(1)}, f32[5,8,128]{2,1,0:T(8,128)S(1)}, u32[]{:S(2)}, u32[]{:S(2)}) collective-permute-start(f32[5,8,128]{2,1,0:T(8,128)S(1)} %get-tuple-element.24), channel_id=1, source_target_pairs={{0,8},{8,0},{16,24},{24,16},{32,40},{40,32},{48,56},{56,48},{1,9},... | collective-permute-start | bytes 61448 | tf_op jit(solution)/shard_map/ppermute | solution.py:453
  32.8 9.1 %collective-permute-start.4 = (f32[8,3,8,128]{3,2,1,0:T(8,128)S(1)}, f32[8,3,8,128]{3,2,1,0:T(8,128)S(1)}, u32[]{:S(2)}, u32[]{:S(2)}) collective-permute-start(f32[8,3,8,128]{3,2,1,0:T(8,128)S(1)} %get-tuple-element.38), channel_id=1, source_target_pairs={{0,7},{1,2},{2,1},{3,4},{4,3},{5,6},{6,5},{7,0},{8,15},{9,10},{10,... | collective-permute-start | bytes 294920 | tf_op jit(solution)/shard_map/ppermute | solution.py:452
  34.7 7.2 %collective-permute-start.5 = (f32[8,3,8,128]{3,2,1,0:T(8,128)S(1)}, f32[8,3,8,128]{3,2,1,0:T(8,128)S(1)}, u32[]{:S(2)}, u32[]{:S(2)}) collective-permute-start(f32[8,3,8,128]{3,2,1,0:T(8,128)S(1)} %get-tuple-element.37), channel_id=1, source_target_pairs={{0,1},{1,0},{2,3},{3,2},{4,5},{5,4},{6,7},{7,6},{8,9},{9,8},{10,11... | collective-permute-start | bytes 294920 | tf_op jit(solution)/shard_map/ppermute | solution.py:453
  43.5 13.9 %all-to-all-start.1 = ((f32[8,5,8,128]{3,2,1,0:T(8,128)}), f32[8,5,8,128]{3,2,1,0:T(8,128)S(1)}, u32[]{:S(2)}, u32[]{:S(2)}) async-start(f32[8,5,8,128]{3,2,1,0:T(8,128)} %shard_map.52), calls=%async_computation.1 | async-start | bytes 327680 | tf_op jit(solution)/shard_map/all_to_all | solution.py:497
  46.9 7.8 %collective-permute-start.2 = (f32[20,8,128]{2,1,0:T(8,128)S(1)}, f32[20,8,128]{2,1,0:T(8,128)S(1)}, u32[]{:S(2)}, u32[]{:S(2)}) collective-permute-start(f32[20,8,128]{2,1,0:T(8,128)S(1)} %get-tuple-element.30.sent_ahead), channel_id=1, source_target_pairs={{0,64},{64,128},{128,192},{192,256},{256,320},{320,384},{384,448},... | collective-permute-start | bytes 245768 | tf_op jit(solution)/shard_map/ppermute | solution.py:445
  50.7 6.3 %collective-permute-start.3 = (f32[20,8,128]{2,1,0:T(8,128)S(1)}, f32[20,8,128]{2,1,0:T(8,128)S(1)}, u32[]{:S(2)}, u32[]{:S(2)}) collective-permute-start(f32[20,8,128]{2,1,0:T(8,128)S(1)} %get-tuple-element.31.sent_behind), channel_id=1, source_target_pairs={{64,0},{128,64},{192,128},{256,192},{320,256},{384,320},{448,384},... | collective-permute-start | bytes 245768 | tf_op jit(solution)/shard_map/ppermute | solution.py:445

commit v9 on v8

--- a/solution.py
+++ b/solution.py
@@ -81,13 +81,11 @@
     return post
 
 
-def edge_kernel(pops_far, codes_far, offsets_far, fractions_far, out, pops, codes, params, offsets, fractions, sems):
+def edge_kernel(pops_far, codes_far, out, pops, codes, sems):
     lane = lanes()
     copies = (
         pltpu.make_async_copy(pops_far, pops, sems.at[0]),
         pltpu.make_async_copy(codes_far, codes, sems.at[1]),
-        pltpu.make_async_copy(offsets_far, offsets, sems.at[2]),
-        pltpu.make_async_copy(fractions_far, fractions, sems.at[3]),
     )
     for copy in copies:
         copy.start()
@@ -103,17 +101,6 @@
                 moved = roll(source, start + 2, 1)
                 packed = jnp.where(lane < start, packed, moved)
         out[tile] = packed
-    here = lax.axis_index("gz")
-    after = (here + 1) % lax.axis_size("gz")
-    length = 8 * lax.axis_size("gx")
-    row_lane = lanes((1, 128))
-    low = (row_lane // 32) % 2 == 1
-    for step in range(2):
-        shift = jnp.where(row_lane < 64, offsets[step, here], offsets[step, after])
-        shift = jnp.where(low, (length - shift) % length, shift)
-        params[step : step + 1, :] = shift.astype(F32)
-        share = jnp.where(row_lane < 64, fractions[step, here], fractions[step, after])
-        params[step + 2 : step + 3, :] = share.astype(F32) * (1.0 / FRAC_DEN)
 
 
 UPPER = [(i, 7) for i in rising] + [(i, 7) for i in level] + [(i, 6) for i in rising] + [(19, 7)]
@@ -140,8 +127,14 @@
                     sides[side, item, target : target + 1, :] = value[x : x + 1, :]
 
 
-def main_kernel(pops, codes, p1, wrapped, chunks, sides):
+def main_kernel(offsets_far, fractions_far, pops, codes, p1, wrapped, chunks, sides, params, offsets, fractions, sems):
     lane = lanes()
+    copies = (
+        pltpu.make_async_copy(offsets_far, offsets, sems.at[0]),
+        pltpu.make_async_copy(fractions_far, fractions, sems.at[1]),
+    )
+    for copy in copies:
+        copy.start()
     side = [jnp.zeros((8, 128), F32) for _ in range(19)]
     for z in range(8):
         f = [pops[i, z] * lattice_weights[i] for i in range(19)]
@@ -169,6 +162,19 @@
                     held[d - 1] = jnp.where(place < 18 * slot, held[d - 1], moved)
             for d in range(6):
                 chunks[d, group * 3 + tile] = held[d]
+    for copy in copies:
+        copy.wait()
+    here = lax.axis_index("gz")
+    after = (here + 1) % lax.axis_size("gz")
+    length = 8 * lax.axis_size("gx")
+    row_lane = lanes((1, 128))
+    low = (row_lane // 32) % 2 == 1
+    for step in range(2):
+        shift = jnp.where(row_lane < 64, offsets[step, here], offsets[step, after])
+        shift = jnp.where(low, (length - shift) % length, shift)
+        params[step : step + 1, :] = shift.astype(F32)
+        share = jnp.where(row_lane < 64, fractions[step, here], fractions[step, after])
+        params[step + 2 : step + 3, :] = share.astype(F32) * (1.0 / FRAC_DEN)
 
 
 def edge_kernel_2(far, near, p1, codes, wrapped, middle, sides, chunks, post_side, side, rows_ahead, rows_behind):
@@ -459,19 +465,21 @@
     pops, codes, offsets, fractions = (
         pltpu.with_memory_space_constraint(value, pltpu.HBM) for value in (pops, codes, offsets, fractions)
     )
-    edges, pops, codes, params = run(
+    edges, pops, codes = run(
         edge_kernel,
-        [(5,) + tile, (19, 8) + tile, jax.ShapeDtypeStruct((8,) + tile, jnp.int32), tile],
-        (pops, codes, offsets, fractions),
-        far_in=4,
+        [(5,) + tile, (19, 8) + tile, jax.ShapeDtypeStruct((8,) + tile, jnp.int32)],
+        (pops, codes),
+        far_in=2,
+        sems=2,
+    )
+    near, far = swaps(edges, edges, "gy")
+    p1, wrapped, middle, sides, params = run(
+        main_kernel,
+        [(19, 8) + tile, (10,) + tile, (6, 6) + tile, (2, 20) + tile, tile],
+        (offsets, fractions, pops, codes),
+        far_in=2,
         words=[offsets.shape] * 2,
-        sems=4,
-    )
-    near, far = swaps(edges, edges, "gy")
-    p1, wrapped, middle, sides = run(
-        main_kernel,
-        [(19, 8) + tile, (10,) + tile, (6, 6) + tile, (2, 20) + tile],
-        (pops, codes),
+        sems=2,
     )
     chunks, post_side, side, sent_ahead, sent_behind = run(
         edge_kernel_2,

time: 58.9 us -> 58.9 us (level)
  waiting for transfers between devices: 10.1 us -> 9.42 us
  Pallas kernels: 5.88 us -> 6.53 us
    ppermute x2, waiting for transfers between devices: 3.04 us -> 2.36 us  [swaps(): near = lax.ppermute(to_near, axis, pair)]
    pallas_call x8, Pallas kernels: 5.88 us -> 6.53 us  [run(): pl.pallas_call(kernel, out_shape=[s if isinstance(s, jax.ShapeDtypeStruct...]
  transfers between devices with their start and end apart: 7 -> 7, of which waited for: 4 -> 4; matrix products, arithmetic and copies ran while one was open for 0% -> 0% of each run, Pallas kernels for 2% -> 4%
where the time goes in v9:
time: 58.9 us; the launch traced here: 58.5 us
  starting transfers between devices  22.5 us (38%)
  blocking collectives  19.9 us (34%)
  waiting for transfers between devices  9.42 us (16%)
  Pallas kernels  6.53 us (11%)
    all_to_all x1, blocking collectives, body(): own = lax.all_to_all(chunks, 'gx', 0, 0)  19.9 us
    ppermute x2, starting transfers between devices, swaps(): far = lax.ppermute(to_far, axis, other)  7.37 us
    pallas_call x8, Pallas kernels, run(): pl.pallas_call(kernel, out_shape=[s if isinstance(s, jax.ShapeDtypeStruct...  6.53 us
    ppermute x2, starting transfers between devices, swaps(): near = lax.ppermute(to_near, axis, pair)  4.72 us
    ppermute x2, waiting for transfers between devices, swaps(): far = lax.ppermute(to_far, axis, other)  4.11 us
    ppermute x1, starting transfers between devices, neighbours(): lax.ppermute(value_up, axis, up)  3.82 us
    all_to_all x1, starting transfers between devices, body(): planes = lax.all_to_all(planes, 'gx', 0, 0)  3.38 us
    ppermute x1, starting transfers between devices, neighbours(): lax.ppermute(value_down, axis, down)  3.24 us
  transfers between devices with their start and end apart: 7, of which 4 were waited for; matrix products, arithmetic and copies ran while one was open for 0% of the time, Pallas kernels for 4%

profile of v9, /device:TPU:40, one launch (start us, length us, event | category | flops | bytes accessed | tf_op | source)
XLA Modules:
  0.0 58.5 jit_solution(2342540451144621339)
XLA Ops:
  0.0 1.3 %shard_map.46 = (f32[5,8,128]{2,1,0:T(8,128)S(1)}, f32[19,8,8,128]{3,2,1,0:T(8,128)S(1)}, s32[8,8,128]{2,1,0:T(8,128)S(1)}) custom-call(f32[19,8,8,128]{3,2,1,0:T(8,128)} %pops_far.1, s32[8,8,128]{2,1,0:T(8,128)} %codes_far.1), custom_call_target="tpu_custom_call" | custom-call | tf_op jit(solution)/shard_map/pallas_call | solution.py:435
  1.3 5.5 %collective-permute-start = (f32[5,8,128]{2,1,0:T(8,128)S(1)}, f32[5,8,128]{2,1,0:T(8,128)S(1)}, u32[]{:S(2)}, u32[]{:S(2)}) collective-permute-start(f32[5,8,128]{2,1,0:T(8,128)S(1)} %get-tuple-element.24), channel_id=1, source_target_pairs={{0,56},{8,16},{16,8},{24,32},{32,24},{40,48},{48,40},{56,0},{1,57}... | collective-permute-start | bytes 61448 | tf_op jit(solution)/shard_map/ppermute | solution.py:458
  6.8 1.9 %collective-permute-start.1 = (f32[5,8,128]{2,1,0:T(8,128)S(1)}, f32[5,8,128]{2,1,0:T(8,128)S(1)}, u32[]{:S(2)}, u32[]{:S(2)}) collective-permute-start(f32[5,8,128]{2,1,0:T(8,128)S(1)} %get-tuple-element.24), channel_id=1, source_target_pairs={{0,8},{8,0},{16,24},{24,16},{32,40},{40,32},{48,56},{56,48},{1,9},... | collective-permute-start | bytes 61448 | tf_op jit(solution)/shard_map/ppermute | solution.py:459
  8.7 1.4 %shard_map.47 = (f32[19,8,8,128]{3,2,1,0:T(8,128)S(1)}, f32[10,8,128]{2,1,0:T(8,128)S(1)}, f32[6,6,8,128]{3,2,1,0:T(8,128)S(1)}, f32[2,20,8,128]{3,2,1,0:T(8,128)S(1)}, f32[8,128]{1,0:T(8,128)S(1)}) custom-call(s32[2,8]{1,0:T(2,128)} %offsets_far.1, s32[2,8]{1,0:T(2,128)} %fractions_far.1, f32[19,8,8,128]{3,2,1,0:T(8,128)S(1)} %get-tuple-element.21.pops, ...), custom_call_target="tpu_custom_call" | custom-call | tf_op jit(solution)/shard_map/pallas_call | solution.py:435
  10.1 0.0 collective-permute-done.far
  10.1 2.4 %collective-permute-done.1.near = f32[5,8,128]{2,1,0:T(8,128)S(1)} collective-permute-done((f32[5,8,128]{2,1,0:T(8,128)S(1)}, f32[5,8,128]{2,1,0:T(8,128)S(1)}, u32[]{:S(2)}, u32[]{:S(2)}) %collective-permute-start.1) | collective-permute-done | bytes 20512 | tf_op jit(solution)/shard_map/ppermute | solution.py:459
  12.5 0.4 shard_map.48
  12.9 19.9 %all_to_all.10.own = f32[8,6,8,128]{3,2,1,0:T(8,128)S(1)} all-to-all(f32[8,6,8,128]{3,2,1,0:T(8,128)S(1)} %get-tuple-element.36), channel_id=1, replica_groups=mesh['gx'=8,'gy'=8,'gz'=8] {'gx'}, dimensions={0} | all-to-all | bytes 393216 | tf_op jit(solution)/shard_map/all_to_all | solution.py:490
  32.8 1.9 %collective-permute-start.4 = (f32[8,3,8,128]{3,2,1,0:T(8,128)S(1)}, f32[8,3,8,128]{3,2,1,0:T(8,128)S(1)}, u32[]{:S(2)}, u32[]{:S(2)}) collective-permute-start(f32[8,3,8,128]{3,2,1,0:T(8,128)S(1)} %get-tuple-element.38), channel_id=1, source_target_pairs={{0,7},{1,2},{2,1},{3,4},{4,3},{5,6},{6,5},{7,0},{8,15},{9,10},{10,... | collective-permute-start | bytes 294920 | tf_op jit(solution)/shard_map/ppermute | solution.py:458
  34.7 2.8 %collective-permute-start.5 = (f32[8,3,8,128]{3,2,1,0:T(8,128)S(1)}, f32[8,3,8,128]{3,2,1,0:T(8,128)S(1)}, u32[]{:S(2)}, u32[]{:S(2)}) collective-permute-start(f32[8,3,8,128]{3,2,1,0:T(8,128)S(1)} %get-tuple-element.37), channel_id=1, source_target_pairs={{0,1},{1,0},{2,3},{3,2},{4,5},{5,4},{6,7},{7,6},{8,9},{9,8},{10,11... | collective-permute-start | bytes 294920 | tf_op jit(solution)/shard_map/ppermute | solution.py:459
  37.5 0.2 shard_map.51.spread
  37.8 4.1 %collective-permute-done.4.far = f32[8,3,8,128]{3,2,1,0:T(8,128)S(1)} collective-permute-done((f32[8,3,8,128]{3,2,1,0:T(8,128)S(1)}, f32[8,3,8,128]{3,2,1,0:T(8,128)S(1)}, u32[]{:S(2)}, u32[]{:S(2)}) %collective-permute-start.4) | collective-permute-done | bytes 98336 | tf_op jit(solution)/shard_map/ppermute | solution.py:458
  41.9 0.0 collective-permute-done.5.near
  41.9 1.6 %shard_map.52 = f32[8,5,8,128]{3,2,1,0:T(8,128)} custom-call(f32[8,128]{1,0:T(8,128)S(1)} %get-tuple-element.35.params, f32[20,64,128]{2,1,0:T(8,128)S(1)} %shard_map.51.spread, f32[8,3,8,128]{3,2,1,0:T(8,128)S(1)} %collective-permute-done.4.far, f32[8,3,8,128]{3,2,1,0:T(8,128)S(1)} %collective-permute-done.5.near), custom_call_target="tpu_custom_call" | custom-call | tf_op jit(solution)/shard_map/pallas_call | solution.py:435
  43.5 3.4 %all-to-all-start.1 = ((f32[8,5,8,128]{3,2,1,0:T(8,128)}), f32[8,5,8,128]{3,2,1,0:T(8,128)S(1)}, u32[]{:S(2)}, u32[]{:S(2)}) async-start(f32[8,5,8,128]{3,2,1,0:T(8,128)} %shard_map.52), calls=%async_computation.1 | async-start | bytes 327680 | tf_op jit(solution)/shard_map/all_to_all | solution.py:505
  46.9 3.8 %collective-permute-start.2 = (f32[20,8,128]{2,1,0:T(8,128)S(1)}, f32[20,8,128]{2,1,0:T(8,128)S(1)}, u32[]{:S(2)}, u32[]{:S(2)}) collective-permute-start(f32[20,8,128]{2,1,0:T(8,128)S(1)} %get-tuple-element.30.sent_ahead), channel_id=1, source_target_pairs={{0,64},{64,128},{128,192},{192,256},{256,320},{320,384},{384,448},... | collective-permute-start | bytes 245768 | tf_op jit(solution)/shard_map/ppermute | solution.py:451
  50.7 3.2 %collective-permute-start.3 = (f32[20,8,128]{2,1,0:T(8,128)S(1)}, f32[20,8,128]{2,1,0:T(8,128)S(1)}, u32[]{:S(2)}, u32[]{:S(2)}) collective-permute-start(f32[20,8,128]{2,1,0:T(8,128)S(1)} %get-tuple-element.31.sent_behind), channel_id=1, source_target_pairs={{64,0},{128,64},{192,128},{256,192},{320,256},{384,320},{448,384},... | collective-permute-start | bytes 245768 | tf_op jit(solution)/shard_map/ppermute | solution.py:451
  53.9 0.1 shard_map.49.arrived
  54.1 0.6 collective-permute-done.2.from_behind
  54.6 2.4 %collective-permute-done.3.from_ahead = f32[20,8,128]{2,1,0:T(8,128)S(1)} collective-permute-done((f32[20,8,128]{2,1,0:T(8,128)S(1)}, f32[20,8,128]{2,1,0:T(8,128)S(1)}, u32[]{:S(2)}, u32[]{:S(2)}) %collective-permute-start.3) | collective-permute-done | bytes 81952 | tf_op jit(solution)/shard_map/ppermute | solution.py:451
  57.0 0.4 shard_map.50
  57.4 0.0 all-to-all-done.1.planes
  57.4 1.1 %shard_map.53 = f32[19,8,8,128]{3,2,1,0:T(8,128)} custom-call(f32[19,6,8,128]{3,2,1,0:T(8,128)S(1)} %get-tuple-element.32.p2, f32[5,8,128]{2,1,0:T(8,128)S(1)} %get-tuple-element.33.ahead, f32[5,8,128]{2,1,0:T(8,128)S(1)} %get-tuple-element.34.behind, f32[8,5,8,128]{3,2,1,0:T(8,128)S(1)} %all-to-all-done.1.planes), custom_call_target="tpu_custom_call" | custom-call | tf_op jit(solution)/shard_map/pallas_call | solution.py:435
  (1 shorter events, 0.0 us)
Async XLA Ops:
  1.3 8.8 %collective-permute-start = (f32[5,8,128]{2,1,0:T(8,128)S(1)}, f32[5,8,128]{2,1,0:T(8,128)S(1)}, u32[]{:S(2)}, u32[]{:S(2)}) collective-permute-start(f32[5,8,128]{2,1,0:T(8,128)S(1)} %get-tuple-element.24), channel_id=1, source_target_pairs={{0,56},{8,16},{16,8},{24,32},{32,24},{40,48},{48,40},{56,0},{1,57}... | collective-permute-start | bytes 61448 | tf_op jit(solution)/shard_map/ppermute | solution.py:458
  6.8 5.7 %collective-permute-start.1 = (f32[5,8,128]{2,1,0:T(8,128)S(1)}, f32[5,8,128]{2,1,0:T(8,128)S(1)}, u32[]{:S(2)}, u32[]{:S(2)}) collective-permute-start(f32[5,8,128]{2,1,0:T(8,128)S(1)} %get-tuple-element.24), channel_id=1, source_target_pairs={{0,8},{8,0},{16,24},{24,16},{32,40},{40,32},{48,56},{56,48},{1,9},... | collective-permute-start | bytes 61448 | tf_op jit(solution)/shard_map/ppermute | solution.py:459
  32.8 9.1 %collective-permute-start.4 = (f32[8,3,8,128]{3,2,1,0:T(8,128)S(1)}, f32[8,3,8,128]{3,2,1,0:T(8,128)S(1)}, u32[]{:S(2)}, u32[]{:S(2)}) collective-permute-start(f32[8,3,8,128]{3,2,1,0:T(8,128)S(1)} %get-tuple-element.38), channel_id=1, source_target_pairs={{0,7},{1,2},{2,1},{3,4},{4,3},{5,6},{6,5},{7,0},{8,15},{9,10},{10,... | collective-permute-start | bytes 294920 | tf_op jit(solution)/shard_map/ppermute | solution.py:458
  34.7 7.2 %collective-permute-start.5 = (f32[8,3,8,128]{3,2,1,0:T(8,128)S(1)}, f32[8,3,8,128]{3,2,1,0:T(8,128)S(1)}, u32[]{:S(2)}, u32[]{:S(2)}) collective-permute-start(f32[8,3,8,128]{3,2,1,0:T(8,128)S(1)} %get-tuple-element.37), channel_id=1, source_target_pairs={{0,1},{1,0},{2,3},{3,2},{4,5},{5,4},{6,7},{7,6},{8,9},{9,8},{10,11... | collective-permute-start | bytes 294920 | tf_op jit(solution)/shard_map/ppermute | solution.py:459
  43.5 13.9 %all-to-all-start.1 = ((f32[8,5,8,128]{3,2,1,0:T(8,128)}), f32[8,5,8,128]{3,2,1,0:T(8,128)S(1)}, u32[]{:S(2)}, u32[]{:S(2)}) async-start(f32[8,5,8,128]{3,2,1,0:T(8,128)} %shard_map.52), calls=%async_computation.1 | async-start | bytes 327680 | tf_op jit(solution)/shard_map/all_to_all | solution.py:505
  46.9 7.8 %collective-permute-start.2 = (f32[20,8,128]{2,1,0:T(8,128)S(1)}, f32[20,8,128]{2,1,0:T(8,128)S(1)}, u32[]{:S(2)}, u32[]{:S(2)}) collective-permute-start(f32[20,8,128]{2,1,0:T(8,128)S(1)} %get-tuple-element.30.sent_ahead), channel_id=1, source_target_pairs={{0,64},{64,128},{128,192},{192,256},{256,320},{320,384},{384,448},... | collective-permute-start | bytes 245768 | tf_op jit(solution)/shard_map/ppermute | solution.py:451
  50.7 6.3 %collective-permute-start.3 = (f32[20,8,128]{2,1,0:T(8,128)S(1)}, f32[20,8,128]{2,1,0:T(8,128)S(1)}, u32[]{:S(2)}, u32[]{:S(2)}) collective-permute-start(f32[20,8,128]{2,1,0:T(8,128)S(1)} %get-tuple-element.31.sent_behind), channel_id=1, source_target_pairs={{64,0},{128,64},{192,128},{256,192},{320,256},{384,320},{448,384},... | collective-permute-start | bytes 245768 | tf_op jit(solution)/shard_map/ppermute | solution.py:451
